TPU v7x, 32 devices: a whole 2x2x4 slice. The times are simulated.
32 devices in a mesh: space: 8 (over y, x, core), chan: 4 (over z).
Axes of the slice: x: 2, y: 2, z: 4, core: 2. Of those that a mesh axis runs over, the one named last changes fastest.
Arguments:
- features: bfloat16 [8, 128, 8, 8, 256], P('space'), may hold values from -6 to 6
- column_heights: int32 [8], replicated, may hold values from 1 to 32, as said below
- weight_one: bfloat16 [27, 128, 128], P(None, 'chan'), may hold values from -0.109375 to 0.109375
- bias_one: float32 [128], P('chan'), may hold values from 0 to 1
- weight_two: bfloat16 [27, 128, 128], P(None, 'chan'), may hold values from -0.109375 to 0.109375
- bias_two: float32 [128], P('chan'), may hold values from 0 to 1
Outputs:
- output: bfloat16 [8, 128, 8, 8, 256], P('space', 'chan')
Inputs may be any that keep to these rules, and one draw needn't show every extreme that they name: Column c holds its active bricks at its lowest column_heights[c] of 32 levels; some column holds exactly 32.
All inputs are finite; a program needn't handle non-finite values.
Results may differ from a plain program's by a relative error of at most 0.004.
Values may be sent and summed in bfloat16 or wider, within the bound.
No kernel may reach another device: no remote copies, remote signals or barrier semaphores. Data moves between devices by JAX's collectives and lax.ppermute only.
A program may use at most 128 MiB of HBM per device.

v0:
```python
import functools

import jax
import jax.numpy as jnp
from jax import lax
from jax.experimental import pallas as pl
from jax.experimental.pallas import tpu as pltpu
from jax.sharding import PartitionSpec as P

COL_Y = 8
TAPS = 3
BF16 = jnp.bfloat16
F32 = jnp.float32
ANY = pl.BlockSpec(memory_space=pl.ANY)
WHOLE = pl.BlockSpec(memory_space=pltpu.VMEM)
SCALARS = pl.BlockSpec(memory_space=pltpu.SMEM)


class Place:
    def __init__(self, heights):
        self.heights = heights
        self.column = lax.axis_index("space")
        self.peers = lax.axis_size("space")
        self.odd = lax.rem(self.column, 2)
        chan = lax.axis_index("chan")
        self.half = lax.div(chan, 2)
        near = lax.rem(chan, 2)
        far = jnp.where(self.odd == 1, 1 - near, near)
        self.slots = (near, 1 - near, far, 1 - far)

    def top(self, by_x=0, across=False):
        column, inside = self.column, True
        if across:
            y = lax.rem(column, COL_Y)
            step = jnp.where(self.odd == 1, 1, -1)
            inside = (y + step >= 0) & (y + step < COL_Y)
            column = column + step
        if by_x:
            column = column + by_x * COL_Y
            inside = inside & (column >= 0) & (column < self.peers)
        column = jnp.clip(column, 0, self.peers - 1)
        return jnp.where(inside, self.heights[column] * 8, 0)


def as_column(row):
    size = row.shape[1]
    wide = jnp.broadcast_to(row, (size, size))
    same = lax.broadcasted_iota(jnp.int32, (size, size), 0) == lax.broadcasted_iota(jnp.int32, (size, size), 1)
    return jnp.sum(jnp.where(same, wide, 0.0), axis=1, keepdims=True)


def pack_kernel(weights, bias, packed):
    taps, rows, lanes = weights.shape
    packed[:taps] = weights[...]
    column = as_column(bias[...])
    lane = lax.broadcasted_iota(jnp.int32, (rows, lanes), 1)
    extra = jnp.zeros((rows, lanes), F32)
    for at in range(3):
        piece = column.astype(BF16).astype(F32)
        extra = jnp.where(lane == at, piece, extra)
        column = column - piece
    packed[taps] = extra.astype(BF16)


def arrange_kernel(heights, features, after, fields, cross, mate):
    _, channels, width, _, depth = features.shape
    place = Place(heights)
    group = 256 // COL_Y
    row = lax.broadcasted_iota(jnp.int32, (256, 256), 0)
    column = lax.broadcasted_iota(jnp.int32, (256, 256), 1)
    u = lax.div(row, group)
    y = jnp.where(place.odd == 1, COL_Y - 1 - u, u)
    swap = (column == lax.rem(row, group) * COL_Y + y).astype(F32).astype(BF16)
    live = lax.broadcasted_iota(jnp.int32, (1, depth), 1) < place.top()
    for x in range(width):
        for first in range(0, channels, group):
            tile = features[0, first : first + group, x].reshape(256, depth)
            moved = jnp.dot(swap, tile, preferred_element_type=F32)
            moved = jnp.where(live, moved, 0.0).astype(BF16).reshape(COL_Y, group, depth)
            fields[:, x, first : first + group] = moved
            cross[:, x, first : first + group] = moved[:2]
            mate[x, first : first + group] = moved[COL_Y - 1]


def finish(partial, bias, live_top):
    rows, depth = partial.shape[0] // TAPS, partial.shape[1]
    z = lax.broadcasted_iota(jnp.int32, (rows, depth), 1)
    below = jnp.where(z == 0, 0.0, pltpu.roll(partial[:rows], 1, 1))
    above = jnp.where(z == depth - 1, 0.0, pltpu.roll(partial[2 * rows :], depth - 1, 1))
    total = jnp.maximum(below + partial[rows : 2 * rows] + above + bias, 0.0)
    return jnp.where(z < live_top, total, 0.0).astype(BF16)


def fill_first(parts, slots, odd, matrix, low_matrix, high_matrix, bias):
    quarter, channels = parts[0].shape[1], parts[0].shape[2]
    block = quarter * len(parts)
    for part, slot in zip(parts, slots, strict=True):
        at = slot * quarter
        for k in range(TAPS):
            span = pl.ds(pl.multiple_of(k * block + at, quarter), quarter)
            for j in range(TAPS):
                tap_j = jnp.where(odd == 1, 2 - j, j)
                for i in range(TAPS):
                    tile = part[9 * i + 3 * tap_j + k]
                    matrix[span, pl.ds((j * TAPS + i) * channels, channels)] = tile
                    if i > 0:
                        low_matrix[span, pl.ds((j * 2 + i - 1) * channels, channels)] = tile
                    if i < 2:
                        high_matrix[span, pl.ds((j * 2 + i) * channels, channels)] = tile
        extra = part[27].astype(F32)
        value = extra[:, 0:1] + extra[:, 1:2] + extra[:, 2:3]
        bias[pl.ds(pl.multiple_of(at, quarter), quarter), :] = jnp.broadcast_to(value, (quarter, bias.shape[1]))


def reach(x, width, stored, pad):
    return max(x - 1 + pad, 0), min(x + width + 1 + pad, stored)


def first_row(get, stored, halo, matrices, bias, top):
    for x in range(-halo, COL_Y + halo):
        low, high = reach(x, 1, stored, 2 * halo)
        lhs = matrices[0]
        if high - low == 2:
            lhs = matrices[1] if x == 0 else matrices[2]
        taken = jnp.concatenate([get(j, low, high) for j in range(TAPS)], axis=0)
        partial = jnp.dot(lhs[...], taken, preferred_element_type=F32)
        side = -1 if x < 0 else 1 if x >= COL_Y else 0
        yield x + halo, finish(partial, bias[:, 0:1], top(side))


def span_of(ref, *at):
    *lead, low, high = at
    value = ref[(*lead, slice(low, high))]
    return value.reshape(-1, value.shape[-1])


def first_inner_kernel(halo, heights, own, mate, part_a, part_b, after, out, out_last, matrix, low_matrix, high_matrix, bias, *, far):
    place = Place(heights)
    slots = place.slots[2:] if far else place.slots[:2]
    fill_first([part_a, part_b], slots, place.odd, matrix, low_matrix, high_matrix, bias)
    matrices, width = (matrix, low_matrix, high_matrix), own.shape[1]

    def pair(step, _):
        for more in range(2):
            u = step * 2 + more
            for x, done in first_row(lambda j, a, b: span_of(own, u + j, a, b), width, halo, matrices, bias, place.top):
                out[u, x] = done
        return 0

    lax.fori_loop(0, (COL_Y - 2) // 2, pair, 0)

    def get(j, a, b):
        return span_of(mate, a, b) if j == 2 else span_of(own, COL_Y - 2 + j, a, b)

    for x, done in first_row(get, width, halo, matrices, bias, place.top):
        out_last[x] = done


def fill_second(weights, place, matrix, low_matrix, high_matrix):
    quarter, channels = weights.shape[1], weights.shape[2]
    empty = jnp.zeros((quarter, channels), BF16)
    for k in range(TAPS):
        for to in range(2):
            span = pl.ds((k * 2 + to) * quarter, quarter)
            for j in range(TAPS):
                tap_j = jnp.where(place.odd == 1, 2 - j, j)
                for at in range(4):
                    tile = empty
                    if 0 <= at - to < TAPS:
                        tile = weights[9 * (at - to) + 3 * tap_j + k].astype(F32)
                        tile = jnp.where(place.half == 1, pltpu.roll(tile, channels // 2, 1), tile).astype(BF16)
                    matrix[span, pl.ds((j * 4 + at) * channels, channels)] = tile
                    if at > 0:
                        low_matrix[span, pl.ds((j * 3 + at - 1) * channels, channels)] = tile
                    if at < 3:
                        high_matrix[span, pl.ds((j * 3 + at) * channels, channels)] = tile


def second_row(get, stored, halo, matrices, both, top):
    quarter = both.shape[0] // 2
    for x in range(0, COL_Y, 2):
        low, high = reach(x, 2, stored, halo)
        lhs = matrices[0]
        if high - low == 3:
            lhs = matrices[1] if x == 0 else matrices[2]
        taken = jnp.concatenate([piece for j in range(TAPS) for piece in get(j, low, high)], axis=0)
        partial = jnp.dot(lhs[...], taken, preferred_element_type=F32)
        done = finish(partial, both, top)
        yield x, done[:quarter], done[quarter:]


def halves(ref_a, ref_b, *at):
    *lead, low, high = at
    return [ref[(*lead, x)] for x in range(low, high) for ref in (ref_a, ref_b)]


def fill_bias(bias, both):
    quarter = bias.shape[1]
    column = jnp.broadcast_to(as_column(bias[...]), (quarter, both.shape[1]))
    both[:quarter] = column
    both[quarter:] = column


def second_inner_kernel(halo, heights, inner_a, inner_b, last_a, last_b, mate_a, mate_b, weights, bias, out, matrix, low_matrix, high_matrix, both):
    place = Place(heights)
    fill_second(weights, place, matrix, low_matrix, high_matrix)
    fill_bias(bias, both)
    matrices, width, top = (matrix, low_matrix, high_matrix), inner_a.shape[1], place.top()

    def pair(step, _):
        for more in range(2):
            u = step * 2 + more
            for x, here, beside in second_row(lambda j, a, b: halves(inner_a, inner_b, u + j, a, b), width, halo, matrices, both[:, 0:1], top):
                out[u, x] = here
                out[u, x + 1] = beside
        return 0

    lax.fori_loop(0, 2, pair, 0)

    def row(u, a, b):
        if u < 7:
            return halves(inner_a, inner_b, u - 1, a, b)
        return halves(last_a, last_b, a, b) if u == 7 else halves(mate_a, mate_b, a, b)

    for u in (6, 7):
        for x, here, beside in second_row(lambda j, a, b: row(u - 1 + j, a, b), width, halo, matrices, both[:, 0:1], top):
            out[u - 2, x] = here
            out[u - 2, x + 1] = beside


def last_kernel(halo, heights, own, cross, part_0, part_1, part_2, part_3, inner_a, inner_b, done_inner, weights, bias, out, matrix, low_matrix, high_matrix, bias_one, matrix_two, low_two, high_two, both, edge, done_edge):
    place = Place(heights)
    fill_first([part_0, part_1, part_2, part_3], [place.slots[0], place.slots[1], 2 + place.slots[2], 2 + place.slots[3]], place.odd, matrix, low_matrix, high_matrix, bias_one)
    fill_second(weights, place, matrix_two, low_two, high_two)
    fill_bias(bias, both)
    width = own.shape[1]

    def fields(u, a, b):
        return span_of(own, u, a, b) if u >= 0 else span_of(cross, -1 - u, a, b)

    for u in (-1, 0):
        for x, done in first_row(
            lambda j, a, b: fields(u - 1 + j, a, b),
            width,
            halo,
            (matrix, low_matrix, high_matrix),
            bias_one,
            lambda side: place.top(side, across=u < 0),
        ):
            edge[u + 1, x] = done

    def row(u, a, b):
        return [edge[u + 1, x] for x in range(a, b)] if u < 1 else halves(inner_a, inner_b, u - 1, a, b)

    for u in (0, 1):
        for x, here, beside in second_row(
            lambda j, a, b: row(u - 1 + j, a, b),
            inner_a.shape[1],
            halo,
            (matrix_two, low_two, high_two),
            both[:, 0:1],
            place.top(),
        ):
            done_edge[u, x] = here
            done_edge[u, x + 1] = beside
    quarter, depth = out.shape[1], out.shape[4]
    size = quarter * COL_Y
    at_row = lax.broadcasted_iota(jnp.int32, (size, size), 0)
    at_column = lax.broadcasted_iota(jnp.int32, (size, size), 1)
    y = lax.rem(at_row, COL_Y)
    u = jnp.where(place.odd == 1, COL_Y - 1 - y, y)
    swap = (at_column == u * quarter + lax.div(at_row, COL_Y)).astype(F32).astype(BF16)
    for x in range(COL_Y):
        tile = jnp.concatenate([done_edge[0, x], done_edge[1, x]] + [done_inner[v, x] for v in range(COL_Y - 2)], axis=0)
        moved = jnp.dot(swap, tile, preferred_element_type=F32).astype(BF16)
        out[0, :, x] = moved.reshape(quarter, COL_Y, depth)


def call(kernel, name, inputs, outputs, scratch, flops, *args):
    nbytes = sum(2 * a.size for a in args)
    return pl.pallas_call(
        kernel,
        out_shape=[jax.ShapeDtypeStruct(dims, BF16) for dims in outputs],
        in_specs=inputs,
        out_specs=[WHOLE] * len(outputs),
        scratch_shapes=scratch,
        compiler_params=pltpu.CompilerParams(vmem_limit_bytes=16 * 2**20),
        cost_estimate=pl.CostEstimate(flops=int(flops), bytes_accessed=int(nbytes), transcendentals=0),
        name=name,
    )(*args)


def pack(weights, bias):
    taps, rows, lanes = weights.shape
    return call(pack_kernel, "pack", [WHOLE, WHOLE], [(taps + 1, rows, lanes)], [], 0, weights, bias[None])[0]


def arrange(heights, features, after):
    _, channels, width, _, depth = features.shape
    row = (width, channels, depth)
    outputs = [(COL_Y, *row), (2, *row), row]
    inputs = [SCALARS, WHOLE, ANY]
    return call(arrange_kernel, "arrange", inputs, outputs, [], 512 * features.size, heights, features, after)


def first_scratch(channels, rows):
    wide = TAPS * channels
    return [
        pltpu.VMEM((TAPS * rows, 3 * wide), BF16),
        pltpu.VMEM((TAPS * rows, 2 * wide), BF16),
        pltpu.VMEM((TAPS * rows, 2 * wide), BF16),
        pltpu.VMEM((rows, 128), F32),
    ]


def second_scratch(channels, quarter):
    tall = TAPS * 2 * quarter
    return [
        pltpu.VMEM((tall, 12 * channels), BF16),
        pltpu.VMEM((tall, 9 * channels), BF16),
        pltpu.VMEM((tall, 9 * channels), BF16),
        pltpu.VMEM((2 * quarter, 128), F32),
    ]


def first_inner(halo, far, heights, own, mate, part_a, part_b, after):
    _, _, channels, depth = own.shape
    half, width = 2 * part_a.shape[1], COL_Y + 2 * halo
    kernel = functools.partial(first_inner_kernel, halo, far=far)
    inputs = [SCALARS] + [WHOLE] * 4 + [ANY]
    outputs = [(COL_Y - 2, width, half, depth), (width, half, depth)]
    flops = 2 * (COL_Y - 1) * COL_Y * depth * 27 * channels * half
    name = "first_far" if far else "first_near"
    return call(kernel, name, inputs, outputs, first_scratch(channels, half), flops, heights, own, mate, part_a, part_b, after)


def second_inner(halo, heights, inner_a, inner_b, last_a, last_b, mate_a, mate_b, weights, bias):
    rows, _, half, depth = inner_a.shape
    channels, quarter = 2 * half, weights.shape[1]
    kernel = functools.partial(second_inner_kernel, halo)
    flops = 2 * rows * COL_Y * depth * 27 * channels * quarter
    return call(
        kernel, "second_inner", [SCALARS] + [WHOLE] * 8, [(rows, COL_Y, quarter, depth)], second_scratch(channels, quarter), flops,
        heights, inner_a, inner_b, last_a, last_b, mate_a, mate_b, weights, bias[None],
    )[0]


def last(halo, heights, own, cross, parts, inner_a, inner_b, done_inner, weights, bias):
    _, _, channels, depth = own.shape
    quarter, width = weights.shape[1], COL_Y + 2 * halo
    kernel = functools.partial(last_kernel, halo)
    scratch = first_scratch(channels, channels) + second_scratch(channels, quarter)
    scratch += [pltpu.VMEM((2, width, channels, depth), BF16), pltpu.VMEM((2, COL_Y, quarter, depth), BF16)]
    flops = 4 * COL_Y * depth * 27 * channels * (channels + quarter)
    return call(
        kernel, "last", [SCALARS] + [WHOLE] * 11, [(1, quarter, COL_Y, COL_Y, depth)], scratch, flops,
        heights, own, cross, *parts, inner_a, inner_b, done_inner, weights, bias[None],
    )[0]


def across_pairs(peers):
    pairs = []
    for i in range(peers):
        to = i + 1 if i % 2 else i - 1
        if 0 <= to < peers and to // COL_Y == i // COL_Y:
            pairs.append((i, to))
    return pairs


def to_mate(value):
    return lax.ppermute(value, "space", [(i, i ^ 1) for i in range(lax.axis_size("space"))])


def far_pairs(peers, chans):
    pairs = []
    for i in range(peers):
        for c in range(chans):
            pairs.append((i * chans + c, i * chans + (c ^ (3 if i % 2 else 2))))
    return pairs


def with_x_borders(rows, peers):
    forth = [(i, i + COL_Y) for i in range(peers - COL_Y)]
    back = [(i + COL_Y, i) for i in range(peers - COL_Y)]
    before = lax.ppermute(rows[:, COL_Y - 2 :], "space", forth)
    behind = lax.ppermute(rows[:, :2], "space", back)
    return jnp.concatenate([before, rows, behind], axis=1)


def on_device(features, column_heights, weight_one, bias_one, weight_two, bias_two):
    peers, chans = lax.axis_size("space"), lax.axis_size("chan")
    halo = 1 if peers > COL_Y else 0

    own_part = pack(weight_one, bias_one)
    far_part = lax.ppermute(own_part, ("space", "chan"), far_pairs(peers, chans))
    near_part = lax.ppermute(own_part, "chan", [(c, c ^ 1) for c in range(chans)])
    fields, cross, mate = arrange(column_heights, features, own_part)
    cross = lax.ppermute(cross, "space", across_pairs(peers))
    mate = to_mate(mate)
    if halo:
        fields = with_x_borders(jnp.concatenate([cross, fields, mate[None]], axis=0), peers)
        cross, fields, mate = fields[:2], fields[2:-1], fields[-1]

    inner_a, last_a = first_inner(halo, False, column_heights, fields, mate, own_part, near_part, mate)
    mate_a = to_mate(last_a)
    other_part = to_mate(far_part)
    inner_b, last_b = first_inner(halo, True, column_heights, fields, mate, far_part, other_part, last_a)
    mate_b = to_mate(last_b)
    done_inner = second_inner(
        halo, column_heights, inner_a, inner_b, last_a, last_b, mate_a, mate_b, weight_two, bias_two
    )
    parts = (own_part, near_part, far_part, other_part)
    return last(halo, column_heights, fields, cross, parts, inner_a, inner_b, done_inner, weight_two, bias_two)


def solution(mesh):
    placed = (
        P("space", None, None, None, None),
        P(),
        P(None, "chan", None),
        P("chan"),
        P(None, "chan", None),
        P("chan"),
    )
    return jax.shard_map(
        on_device,
        mesh=mesh,
        in_specs=placed,
        out_specs=P("space", "chan", None, None, None),
        check_vma=False,
    )
```

profile of v0, /device:TPU:1, one launch (start us, length us, event | category | flops | bytes accessed | tf_op | source)
XLA Modules:
  0.0 53.4 jit_solution(691987484679885653)
XLA Ops:
  0.0 0.9 %copy-done.1 = bf16[27,32,128]{2,1,0:T(8,128)(2,1)S(1)} copy-done((bf16[27,32,128]{2,1,0:T(8,128)(2,1)S(1)}, bf16[27,32,128]{2,1,0:T(8,128)(2,1)}, u32[]{:S(2)}) %copy-start.1) | copy-done | bytes 221208
  0.9 0.7 %copy-done.4 = f32[32]{0:T(128)S(1)} copy-done((f32[32]{0:T(128)S(1)}, f32[32]{0:T(128)}, u32[]{:S(2)}) %copy-start.4) | copy-done | bytes 152
  1.6 0.1 pack.1.after.part_a.part_0
  1.7 0.0 copy-start
  1.7 2.2 %copy-done = bf16[1,128,8,8,256]{4,3,2,1,0:T(8,128)(2,1)S(1)} copy-done((bf16[1,128,8,8,256]{4,3,2,1,0:T(8,128)(2,1)S(1)}, bf16[1,128,8,8,256]{4,3,2,1,0:T(8,128)(2,1)}, u32[]{:S(2)}) %copy-start) | copy-done | bytes 4194328
  3.9 0.7 %copy-done.2 = s32[8]{0:T(128)S(1)} copy-done((s32[8]{0:T(128)S(1)}, s32[8]{0:T(128)}, u32[]{:S(2)}) %copy-start.2) | copy-done | bytes 56
  4.5 1.8 %arrange.1 = (bf16[8,8,128,256]{3,2,1,0:T(8,128)(2,1)S(1)}, bf16[2,8,128,256]{3,2,1,0:T(8,128)(2,1)S(1)}, bf16[8,128,256]{2,1,0:T(8,128)(2,1)S(1)}) custom-call(s32[8]{0:T(128)S(1)} %copy-done.2, bf16[1,128,8,8,256]{4,3,2,1,0:T(8,128)(2,1)S(1)} %copy-done, bf16[28,32,128]{2,1,0:T(8,128)(2,1)S(1)} %pack.1.after.part_a.part_0), custom_call_target="tpu_custom_call" | custom-call | flops 1073741824 | bytes 4423696 | tf_op jit(solution)/shard_map/arrange/pallas_call | solution.py:281
  6.3 0.1 collective-permute-start.4
  6.5 4.8 %collective-permute-start.2 = (bf16[28,32,128]{2,1,0:T(8,128)(2,1)S(1)}, bf16[28,32,128]{2,1,0:T(8,128)(2,1)S(1)}, u32[]{:S(2)}, u32[]{:S(2)}) collective-permute-start(bf16[28,32,128]{2,1,0:T(8,128)(2,1)S(1)} %pack.1.after.part_a.part_0), channel_id=1, source_target_pairs={{0,2},{1,3},{2,0},{3,1},{4,7},{5,6},{6,5},{7,4},{8,10},{9,11},{10,... | collective-permute-start | bytes 688136 | tf_op jit(solution)/shard_map/ppermute | solution.py:395
  11.2 3.9 %collective-permute-start = (bf16[2,8,128,256]{3,2,1,0:T(8,128)(2,1)S(1)}, bf16[2,8,128,256]{3,2,1,0:T(8,128)(2,1)S(1)}, u32[]{:S(2)}, u32[]{:S(2)}) collective-permute-start(bf16[2,8,128,256]{3,2,1,0:T(8,128)(2,1)S(1)} %get-tuple-element.13), channel_id=1, source_target_pairs={{4,8},{8,4},{12,16},{16,12},{20,24},{24,20},{5,9},{9,5},{13,17},{1... | collective-permute-start | bytes 3145736 | tf_op jit(solution)/shard_map/ppermute | solution.py:398
  15.2 1.5 %collective-permute-done.2.part_a.part_2 = bf16[28,32,128]{2,1,0:T(8,128)(2,1)S(1)} collective-permute-done((bf16[28,32,128]{2,1,0:T(8,128)(2,1)S(1)}, bf16[28,32,128]{2,1,0:T(8,128)(2,1)S(1)}, u32[]{:S(2)}, u32[]{:S(2)}) %collective-permute-start.2) | collective-permute-done | bytes 229408 | tf_op jit(solution)/shard_map/ppermute | solution.py:395
  16.7 5.3 %collective-permute-start.3 = (bf16[28,32,128]{2,1,0:T(8,128)(2,1)S(1)}, bf16[28,32,128]{2,1,0:T(8,128)(2,1)S(1)}, u32[]{:S(2)}, u32[]{:S(2)}) collective-permute-start(bf16[28,32,128]{2,1,0:T(8,128)(2,1)S(1)} %collective-permute-done.2.part_a.part_2), channel_id=1, source_target_pairs={{0,4},{4,0},{8,12},{12,8},{16,20},{20,16},{24,28},{28,24},{1,5},{5... | collective-permute-start | bytes 688136 | tf_op jit(solution)/shard_map/ppermute | solution.py:371
  22.0 0.2 collective-permute-done.1.part_b.part_1
  22.2 0.0 collective-permute-done.4.mate.after
  22.2 8.3 %first_near.1 = (bf16[6,8,64,256]{3,2,1,0:T(8,128)(2,1)S(1)}, bf16[8,64,256]{2,1,0:T(8,128)(2,1)S(1)}) custom-call(s32[8]{0:T(128)S(1)} %copy-done.2, bf16[8,8,128,256]{3,2,1,0:T(8,128)(2,1)S(1)} %get-tuple-element.12.own, bf16[8,128,256]{2,1,0:T(8,128)(2,1)S(1)} %collective-permute-done.4.mate.after, bf16[28,32,128]{2,1,0:T(8,128)(2,1)S(1)} %pack.1.after.part_a.part_0, ...), custom_call_target="tpu_custom_call" | custom-call | flops 6341787648 | bytes 5701648 | tf_op jit(solution)/shard_map/first_near/pallas_call | solution.py:281
  30.5 0.0 copy-start.5
  30.5 0.0 copy-start.6
  30.5 0.5 collective-permute-start.5
  31.0 8.3 %first_far.1 = (bf16[6,8,64,256]{3,2,1,0:T(8,128)(2,1)S(1)}, bf16[8,64,256]{2,1,0:T(8,128)(2,1)S(1)}) custom-call(s32[8]{0:T(128)S(1)} %copy-done.2, bf16[8,8,128,256]{3,2,1,0:T(8,128)(2,1)S(1)} %get-tuple-element.12.own, bf16[8,128,256]{2,1,0:T(8,128)(2,1)S(1)} %collective-permute-done.4.mate.after, ...), custom_call_target="tpu_custom_call" | custom-call | flops 6341787648 | bytes 5439504 | tf_op jit(solution)/shard_map/first_far/pallas_call | solution.py:281
  39.3 0.2 collective-permute-start.6
  39.5 0.0 collective-permute-done.5.mate_a
  39.5 1.4 %collective-permute-done.6.mate_b = bf16[8,64,256]{2,1,0:T(8,128)(2,1)S(1)} collective-permute-done((bf16[8,64,256]{2,1,0:T(8,128)(2,1)S(1)}, bf16[8,64,256]{2,1,0:T(8,128)(2,1)S(1)}, u32[]{:S(2)}, u32[]{:S(2)}) %collective-permute-start.6) | collective-permute-done | bytes 262176 | tf_op jit(solution)/shard_map/ppermute | solution.py:371
  40.9 5.2 %second_inner.1.done_inner = bf16[6,8,32,256]{3,2,1,0:T(8,128)(2,1)S(1)} custom-call(s32[8]{0:T(128)S(1)} %copy-done.2, bf16[6,8,64,256]{3,2,1,0:T(8,128)(2,1)S(1)} %get-tuple-element.15.inner_a, bf16[6,8,64,256]{3,2,1,0:T(8,128)(2,1)S(1)} %get-tuple-element.17.inner_b, bf16[8,64,256]{2,1,0:T(8,128)(2,1)S(1)} %get-tuple-element.16.after.last_a, ...), custom_call_target="tpu_custom_call" | custom-call | flops 2717908992 | bytes 4415568 | tf_op jit(solution)/shard_map/second_inner/pallas_call | solution.py:281
  46.1 7.3 %last.1 = bf16[1,32,8,8,256]{4,3,2,1,0:T(8,128)(2,1)} custom-call(s32[8]{0:T(128)S(1)} %copy-done.3, bf16[8,8,128,256]{3,2,1,0:T(8,128)(2,1)S(1)} %get-tuple-element.12.own, bf16[2,8,128,256]{3,2,1,0:T(8,128)(2,1)S(1)} %collective-permute-done.cross, bf16[28,32,128]{2,1,0:T(8,128)(2,1)S(1)} %pack.1.after.part_a.part_0, ...), custom_call_target="tpu_custom_call" | custom-call | flops 4529848320 | bytes 10313808 | tf_op jit(solution)/shard_map/last/pallas_call | solution.py:281
  (10 shorter events, 0.0 us)
Async XLA Ops:
  0.0 0.9 %copy-start.1 = (bf16[27,32,128]{2,1,0:T(8,128)(2,1)S(1)}, bf16[27,32,128]{2,1,0:T(8,128)(2,1)}, u32[]{:S(2)}) copy-start(bf16[27,32,128]{2,1,0:T(8,128)(2,1)} %weights.3) | copy-start | bytes 663556
  0.9 0.7 %copy-start.4 = (f32[32]{0:T(128)S(1)}, f32[32]{0:T(128)}, u32[]{:S(2)}) copy-start(f32[32]{0:T(128)} %param.9) | copy-start | bytes 388
  1.7 2.2 %copy-start = (bf16[1,128,8,8,256]{4,3,2,1,0:T(8,128)(2,1)S(1)}, bf16[1,128,8,8,256]{4,3,2,1,0:T(8,128)(2,1)}, u32[]{:S(2)}) copy-start(bf16[1,128,8,8,256]{4,3,2,1,0:T(8,128)(2,1)} %features.1) | copy-start | bytes 12582916
  3.9 0.7 %copy-start.2 = (s32[8]{0:T(128)S(1)}, s32[8]{0:T(128)}, u32[]{:S(2)}) copy-start(s32[8]{0:T(128)} %heights.9) | copy-start | bytes 100
  6.3 15.9 %collective-permute-start.4 = (bf16[8,128,256]{2,1,0:T(8,128)(2,1)S(1)}, bf16[8,128,256]{2,1,0:T(8,128)(2,1)S(1)}, u32[]{:S(2)}, u32[]{:S(2)}) collective-permute-start(bf16[8,128,256]{2,1,0:T(8,128)(2,1)S(1)} %get-tuple-element.14), channel_id=1, source_target_pairs={{0,4},{4,0},{8,12},{12,8},{16,20},{20,16},{24,28},{28,24},{1,5},{5... | collective-permute-start | bytes 1572872 | tf_op jit(solution)/shard_map/ppermute | solution.py:371
  6.5 10.2 %collective-permute-start.2 = (bf16[28,32,128]{2,1,0:T(8,128)(2,1)S(1)}, bf16[28,32,128]{2,1,0:T(8,128)(2,1)S(1)}, u32[]{:S(2)}, u32[]{:S(2)}) collective-permute-start(bf16[28,32,128]{2,1,0:T(8,128)(2,1)S(1)} %pack.1.after.part_a.part_0), channel_id=1, source_target_pairs={{0,2},{1,3},{2,0},{3,1},{4,7},{5,6},{6,5},{7,4},{8,10},{9,11},{10,... | collective-permute-start | bytes 688136 | tf_op jit(solution)/shard_map/ppermute | solution.py:395
  11.2 11.0 %collective-permute-start.1 = (bf16[28,32,128]{2,1,0:T(8,128)(2,1)S(1)}, bf16[28,32,128]{2,1,0:T(8,128)(2,1)S(1)}, u32[]{:S(2)}, u32[]{:S(2)}) collective-permute-start(bf16[28,32,128]{2,1,0:T(8,128)(2,1)S(1)} %pack.1.after.part_a.part_0), channel_id=1, source_target_pairs={{0,1},{1,0},{2,3},{3,2},{4,5},{5,4},{6,7},{7,6},{8,9},{9,8},{10,11... | collective-permute-start | bytes 688136 | tf_op jit(solution)/shard_map/ppermute | solution.py:396
  11.2 34.8 %collective-permute-start = (bf16[2,8,128,256]{3,2,1,0:T(8,128)(2,1)S(1)}, bf16[2,8,128,256]{3,2,1,0:T(8,128)(2,1)S(1)}, u32[]{:S(2)}, u32[]{:S(2)}) collective-permute-start(bf16[2,8,128,256]{3,2,1,0:T(8,128)(2,1)S(1)} %get-tuple-element.13), channel_id=1, source_target_pairs={{4,8},{8,4},{12,16},{16,12},{20,24},{24,20},{5,9},{9,5},{13,17},{1... | collective-permute-start | bytes 3145736 | tf_op jit(solution)/shard_map/ppermute | solution.py:398
  16.7 14.3 %collective-permute-start.3 = (bf16[28,32,128]{2,1,0:T(8,128)(2,1)S(1)}, bf16[28,32,128]{2,1,0:T(8,128)(2,1)S(1)}, u32[]{:S(2)}, u32[]{:S(2)}) collective-permute-start(bf16[28,32,128]{2,1,0:T(8,128)(2,1)S(1)} %collective-permute-done.2.part_a.part_2), channel_id=1, source_target_pairs={{0,4},{4,0},{8,12},{12,8},{16,20},{20,16},{24,28},{28,24},{1,5},{5... | collective-permute-start | bytes 688136 | tf_op jit(solution)/shard_map/ppermute | solution.py:371
  30.5 10.4 %copy-start.5 = (bf16[27,32,128]{2,1,0:T(8,128)(2,1)S(1)}, bf16[27,32,128]{2,1,0:T(8,128)(2,1)}, u32[]{:S(2)}) copy-start(bf16[27,32,128]{2,1,0:T(8,128)(2,1)} %weights.5) | copy-start | bytes 663556
  30.5 10.4 %copy-start.6 = (f32[32]{0:T(128)S(1)}, f32[32]{0:T(128)}, u32[]{:S(2)}) copy-start(f32[32]{0:T(128)} %param.11) | copy-start | bytes 388
  30.5 8.9 %collective-permute-start.5 = (bf16[8,64,256]{2,1,0:T(8,128)(2,1)S(1)}, bf16[8,64,256]{2,1,0:T(8,128)(2,1)S(1)}, u32[]{:S(2)}, u32[]{:S(2)}) collective-permute-start(bf16[8,64,256]{2,1,0:T(8,128)(2,1)S(1)} %get-tuple-element.16.after.last_a), channel_id=1, source_target_pairs={{0,4},{4,0},{8,12},{12,8},{16,20},{20,16},{24,28},{28,24},{1,5},{5... | collective-permute-start | bytes 786440 | tf_op jit(solution)/shard_map/ppermute | solution.py:371
  39.3 1.6 %collective-permute-start.6 = (bf16[8,64,256]{2,1,0:T(8,128)(2,1)S(1)}, bf16[8,64,256]{2,1,0:T(8,128)(2,1)S(1)}, u32[]{:S(2)}, u32[]{:S(2)}) collective-permute-start(bf16[8,64,256]{2,1,0:T(8,128)(2,1)S(1)} %get-tuple-element.18.last_b), channel_id=1, source_target_pairs={{0,4},{4,0},{8,12},{12,8},{16,20},{20,16},{24,28},{28,24},{1,5},{5... | collective-permute-start | bytes 786440 | tf_op jit(solution)/shard_map/ppermute | solution.py:371
  40.9 5.2 %copy-start.3 = (s32[8]{0:T(128)S(1)}, s32[8]{0:T(128)}, u32[]{:S(2)}) copy-start(s32[8]{0:T(128)} %heights.9) | copy-start | bytes 100
where the time goes:
time: 53.7 us; the launch traced here: 53.4 us
  Pallas kernels  30.9 us (58%)
  starting transfers between devices  14.7 us (27%)
  local copies, waits for them, and re-layouts  4.44 us (8%)
  waiting for transfers between devices  3.17 us (6%)
    pallas_call x6, Pallas kernels, call(): pl.pallas_call(kernel, out_shape=[jax.ShapeDtypeStruct(dims, BF16) for di...  30.9 us
    ppermute x4, starting transfers between devices, to_mate(): lax.ppermute(value, 'space', [(i, i ^ 1) for i in range(lax.axis_size('sp...  6.07 us
    ppermute x1, starting transfers between devices, on_device(): lax.ppermute(own_part, ('space', 'chan'), far_pairs(peers, chans))  4.77 us
    unnamed x14, local copies, waits for them, and re-layouts  4.44 us
    ppermute x1, starting transfers between devices, on_device(): cross = lax.ppermute(cross, 'space', across_pairs(peers))  3.91 us
    ppermute x1, waiting for transfers between devices, on_device(): lax.ppermute(own_part, ('space', 'chan'), far_pairs(peers, chans))  1.5 us
    ppermute x4, waiting for transfers between devices, to_mate(): lax.ppermute(value, 'space', [(i, i ^ 1) for i in range(lax.axis_size('sp...  1.42 us
  transfers between devices with their start and end apart: 7, of which 3 were waited for; matrix products, arithmetic and copies ran while one was open for 0% of the time, Pallas kernels for 41%

commit v1 on v0

--- a/solution.py
+++ b/solution.py
@@ -49,21 +49,16 @@
     return jnp.sum(jnp.where(same, wide, 0.0), axis=1, keepdims=True)
 
 
-def pack_kernel(weights, bias, packed):
+def prepare_kernel(heights, weights, bias, features, packed, fields, cross, mate, bias_here, stored, sems):
+    _, channels, width, _, depth = features.shape
     taps, rows, lanes = weights.shape
-    packed[:taps] = weights[...]
-    column = as_column(bias[...])
-    lane = lax.broadcasted_iota(jnp.int32, (rows, lanes), 1)
-    extra = jnp.zeros((rows, lanes), F32)
-    for at in range(3):
-        piece = column.astype(BF16).astype(F32)
-        extra = jnp.where(lane == at, piece, extra)
-        column = column - piece
-    packed[taps] = extra.astype(BF16)
-
-
-def arrange_kernel(heights, features, after, fields, cross, mate):
-    _, channels, width, _, depth = features.shape
+    copies = [
+        pltpu.make_async_copy(bias, bias_here, sems.at[width]),
+        pltpu.make_async_copy(weights, packed.at[pl.ds(0, taps)], sems.at[width + 1]),
+    ]
+    copies += [pltpu.make_async_copy(features.at[0, :, x], stored.at[x], sems.at[x]) for x in range(width)]
+    for copy in copies:
+        copy.start()
     place = Place(heights)
     group = 256 // COL_Y
     row = lax.broadcasted_iota(jnp.int32, (256, 256), 0)
@@ -72,9 +67,22 @@
     y = jnp.where(place.odd == 1, COL_Y - 1 - u, u)
     swap = (column == lax.rem(row, group) * COL_Y + y).astype(F32).astype(BF16)
     live = lax.broadcasted_iota(jnp.int32, (1, depth), 1) < place.top()
+
+    copies[0].wait()
+    column = as_column(bias_here[...])
+    lane = lax.broadcasted_iota(jnp.int32, (rows, lanes), 1)
+    extra = jnp.zeros((rows, lanes), F32)
+    for at in range(3):
+        piece = column.astype(BF16).astype(F32)
+        extra = jnp.where(lane == at, piece, extra)
+        column = column - piece
+    packed[taps] = extra.astype(BF16)
+    copies[1].wait()
+
     for x in range(width):
+        copies[2 + x].wait()
         for first in range(0, channels, group):
-            tile = features[0, first : first + group, x].reshape(256, depth)
+            tile = stored[x, first : first + group].reshape(256, depth)
             moved = jnp.dot(swap, tile, preferred_element_type=F32)
             moved = jnp.where(live, moved, 0.0).astype(BF16).reshape(COL_Y, group, depth)
             fields[:, x, first : first + group] = moved
@@ -201,10 +209,13 @@
     both[quarter:] = column
 
 
-def second_inner_kernel(halo, heights, inner_a, inner_b, last_a, last_b, mate_a, mate_b, weights, bias, out, matrix, low_matrix, high_matrix, both):
+def fill_kernel(heights, weights, bias, after, matrix, low_matrix, high_matrix, both):
+    fill_second(weights, Place(heights), matrix, low_matrix, high_matrix)
+    fill_bias(bias, both)
+
+
+def second_inner_kernel(halo, heights, inner_a, inner_b, last_a, last_b, matrix, low_matrix, high_matrix, both, out):
     place = Place(heights)
-    fill_second(weights, place, matrix, low_matrix, high_matrix)
-    fill_bias(bias, both)
     matrices, width, top = (matrix, low_matrix, high_matrix), inner_a.shape[1], place.top()
 
     def pair(step, _):
@@ -218,41 +229,61 @@
     lax.fori_loop(0, 2, pair, 0)
 
     def row(u, a, b):
+        return halves(inner_a, inner_b, u - 1, a, b) if u < 7 else halves(last_a, last_b, a, b)
+
+    for x, here, beside in second_row(lambda j, a, b: row(5 + j, a, b), width, halo, matrices, both[:, 0:1], top):
+        out[4, x] = here
+        out[4, x + 1] = beside
+
+
+def last_kernel(
+    halo, heights, own, cross, part_0, part_1, part_2, part_3, inner_a, inner_b, last_a, last_b, mate_a, mate_b,
+    done_inner, matrix_two, low_two, high_two, both, out, matrix, low_matrix, high_matrix, bias_one, edge, done_edge,
+):
+    place = Place(heights)
+    fill_first([part_0, part_1, part_2, part_3], [place.slots[0], place.slots[1], 2 + place.slots[2], 2 + place.slots[3]], place.odd, matrix, low_matrix, high_matrix, bias_one)
+    width, depth = own.shape[1], own.shape[3]
+    matrices = (matrix, low_matrix, high_matrix)
+
+    def fields(u, a, b):
+        return span_of(own, u, a, b) if u >= 0 else span_of(cross, -1 - u, a, b)
+
+    def edge_row(u, levels):
+        def top(side):
+            return place.top(side, across=u < 0)
+
+        def get(j, a, b):
+            return fields(u - 1 + j, a, b)[:, :levels]
+
+        for x, done in first_row(get, width, halo, matrices, bias_one, top):
+            edge[u + 1, x, :, :levels] = done
+            if levels < depth:
+                edge[u + 1, x, :, levels:] = jnp.zeros((done.shape[0], depth - levels), BF16)
+
+    part = depth // 2 if depth % 256 == 0 else depth
+    highest = place.top(0, across=True)
+    if halo:
+        highest = jnp.maximum(highest, jnp.maximum(place.top(-1, across=True), place.top(1, across=True)))
+    low = highest < part
+
+    @pl.when(low)
+    def _():
+        edge_row(-1, part)
+
+    @pl.when(jnp.logical_not(low))
+    def _():
+        edge_row(-1, depth)
+
+    edge_row(0, depth)
+
+    def row(u, a, b):
+        if u < 1:
+            return [edge[u + 1, x] for x in range(a, b)]
         if u < 7:
             return halves(inner_a, inner_b, u - 1, a, b)
         return halves(last_a, last_b, a, b) if u == 7 else halves(mate_a, mate_b, a, b)
 
-    for u in (6, 7):
-        for x, here, beside in second_row(lambda j, a, b: row(u - 1 + j, a, b), width, halo, matrices, both[:, 0:1], top):
-            out[u - 2, x] = here
-            out[u - 2, x + 1] = beside
-
-
-def last_kernel(halo, heights, own, cross, part_0, part_1, part_2, part_3, inner_a, inner_b, done_inner, weights, bias, out, matrix, low_matrix, high_matrix, bias_one, matrix_two, low_two, high_two, both, edge, done_edge):
-    place = Place(heights)
-    fill_first([part_0, part_1, part_2, part_3], [place.slots[0], place.slots[1], 2 + place.slots[2], 2 + place.slots[3]], place.odd, matrix, low_matrix, high_matrix, bias_one)
-    fill_second(weights, place, matrix_two, low_two, high_two)
-    fill_bias(bias, both)
-    width = own.shape[1]
-
-    def fields(u, a, b):
-        return span_of(own, u, a, b) if u >= 0 else span_of(cross, -1 - u, a, b)
-
-    for u in (-1, 0):
-        for x, done in first_row(
-            lambda j, a, b: fields(u - 1 + j, a, b),
-            width,
-            halo,
-            (matrix, low_matrix, high_matrix),
-            bias_one,
-            lambda side: place.top(side, across=u < 0),
-        ):
-            edge[u + 1, x] = done
-
-    def row(u, a, b):
-        return [edge[u + 1, x] for x in range(a, b)] if u < 1 else halves(inner_a, inner_b, u - 1, a, b)
-
-    for u in (0, 1):
+    for at, u in enumerate((0, 1, 7)):
         for x, here, beside in second_row(
             lambda j, a, b: row(u - 1 + j, a, b),
             inner_a.shape[1],
@@ -261,9 +292,9 @@
             both[:, 0:1],
             place.top(),
         ):
-            done_edge[u, x] = here
-            done_edge[u, x + 1] = beside
-    quarter, depth = out.shape[1], out.shape[4]
+            done_edge[at, x] = here
+            done_edge[at, x + 1] = beside
+    quarter = out.shape[1]
     size = quarter * COL_Y
     at_row = lax.broadcasted_iota(jnp.int32, (size, size), 0)
     at_column = lax.broadcasted_iota(jnp.int32, (size, size), 1)
@@ -271,36 +302,38 @@
     u = jnp.where(place.odd == 1, COL_Y - 1 - y, y)
     swap = (at_column == u * quarter + lax.div(at_row, COL_Y)).astype(F32).astype(BF16)
     for x in range(COL_Y):
-        tile = jnp.concatenate([done_edge[0, x], done_edge[1, x]] + [done_inner[v, x] for v in range(COL_Y - 2)], axis=0)
+        tiles = [done_edge[0, x], done_edge[1, x]] + [done_inner[v, x] for v in range(COL_Y - 3)] + [done_edge[2, x]]
+        tile = jnp.concatenate(tiles, axis=0)
         moved = jnp.dot(swap, tile, preferred_element_type=F32).astype(BF16)
         out[0, :, x] = moved.reshape(quarter, COL_Y, depth)
 
 
-def call(kernel, name, inputs, outputs, scratch, flops, *args):
+def call(kernel, name, inputs, outputs, scratch, flops, *args, kinds=None, vmem=16):
     nbytes = sum(2 * a.size for a in args)
     return pl.pallas_call(
         kernel,
-        out_shape=[jax.ShapeDtypeStruct(dims, BF16) for dims in outputs],
+        out_shape=[jax.ShapeDtypeStruct(*each) for each in zip(outputs, kinds or [BF16] * len(outputs))],
         in_specs=inputs,
         out_specs=[WHOLE] * len(outputs),
         scratch_shapes=scratch,
-        compiler_params=pltpu.CompilerParams(vmem_limit_bytes=16 * 2**20),
-        cost_estimate=pl.CostEstimate(flops=int(flops), bytes_accessed=int(nbytes), transcendentals=0),
+        compiler_params=pltpu.CompilerParams(vmem_limit_bytes=vmem * 2**20),
+        cost_estimate=pl.CostEstimate(flops=0, bytes_accessed=0, transcendentals=0),
         name=name,
     )(*args)
 
 
-def pack(weights, bias):
+def prepare(heights, weights, bias, features):
+    _, channels, width, _, depth = features.shape
     taps, rows, lanes = weights.shape
-    return call(pack_kernel, "pack", [WHOLE, WHOLE], [(taps + 1, rows, lanes)], [], 0, weights, bias[None])[0]
-
-
-def arrange(heights, features, after):
-    _, channels, width, _, depth = features.shape
     row = (width, channels, depth)
-    outputs = [(COL_Y, *row), (2, *row), row]
-    inputs = [SCALARS, WHOLE, ANY]
-    return call(arrange_kernel, "arrange", inputs, outputs, [], 512 * features.size, heights, features, after)
+    outputs = [(taps + 1, rows, lanes), (COL_Y, *row), (2, *row), row]
+    scratch = [
+        pltpu.VMEM((1, rows), F32),
+        pltpu.VMEM((width, channels, COL_Y, depth), BF16),
+        pltpu.SemaphoreType.DMA((width + 2,)),
+    ]
+    inputs = [SCALARS, ANY, ANY, ANY]
+    return call(prepare_kernel, "prepare", inputs, outputs, scratch, 0, heights, weights, bias[None], features, vmem=47)
 
 
 def first_scratch(channels, rows):
@@ -313,14 +346,12 @@
     ]
 
 
-def second_scratch(channels, quarter):
+def fill(heights, weights, bias, after):
+    quarter, channels = weights.shape[1], weights.shape[2]
     tall = TAPS * 2 * quarter
-    return [
-        pltpu.VMEM((tall, 12 * channels), BF16),
-        pltpu.VMEM((tall, 9 * channels), BF16),
-        pltpu.VMEM((tall, 9 * channels), BF16),
-        pltpu.VMEM((2 * quarter, 128), F32),
-    ]
+    outputs = [(tall, 12 * channels), (tall, 9 * channels), (tall, 9 * channels), (2 * quarter, 128)]
+    kinds = [BF16, BF16, BF16, F32]
+    return call(fill_kernel, "fill", [SCALARS, WHOLE, WHOLE, ANY], outputs, [], 0, heights, weights, bias[None], after, kinds=kinds)
 
 
 def first_inner(halo, far, heights, own, mate, part_a, part_b, after):
@@ -334,28 +365,26 @@
     return call(kernel, name, inputs, outputs, first_scratch(channels, half), flops, heights, own, mate, part_a, part_b, after)
 
 
-def second_inner(halo, heights, inner_a, inner_b, last_a, last_b, mate_a, mate_b, weights, bias):
+def second_inner(halo, heights, inner_a, inner_b, last_a, last_b, matrices):
     rows, _, half, depth = inner_a.shape
-    channels, quarter = 2 * half, weights.shape[1]
+    quarter = matrices[-1].shape[0] // 2
     kernel = functools.partial(second_inner_kernel, halo)
-    flops = 2 * rows * COL_Y * depth * 27 * channels * quarter
-    return call(
-        kernel, "second_inner", [SCALARS] + [WHOLE] * 8, [(rows, COL_Y, quarter, depth)], second_scratch(channels, quarter), flops,
-        heights, inner_a, inner_b, last_a, last_b, mate_a, mate_b, weights, bias[None],
-    )[0]
-
-
-def last(halo, heights, own, cross, parts, inner_a, inner_b, done_inner, weights, bias):
+    flops = 2 * (rows - 1) * COL_Y * depth * 27 * 2 * half * quarter
+    outputs = [(rows - 1, COL_Y, quarter, depth)]
+    args = (heights, inner_a, inner_b, last_a, last_b, *matrices)
+    return call(kernel, "second_inner", [SCALARS] + [WHOLE] * 8, outputs, [], flops, *args)[0]
+
+
+def last(halo, heights, own, cross, parts, hidden, done_inner, matrices):
     _, _, channels, depth = own.shape
-    quarter, width = weights.shape[1], COL_Y + 2 * halo
+    quarter, width = matrices[-1].shape[0] // 2, COL_Y + 2 * halo
     kernel = functools.partial(last_kernel, halo)
-    scratch = first_scratch(channels, channels) + second_scratch(channels, quarter)
-    scratch += [pltpu.VMEM((2, width, channels, depth), BF16), pltpu.VMEM((2, COL_Y, quarter, depth), BF16)]
+    scratch = first_scratch(channels, channels)
+    scratch += [pltpu.VMEM((2, width, channels, depth), BF16), pltpu.VMEM((3, COL_Y, quarter, depth), BF16)]
     flops = 4 * COL_Y * depth * 27 * channels * (channels + quarter)
-    return call(
-        kernel, "last", [SCALARS] + [WHOLE] * 11, [(1, quarter, COL_Y, COL_Y, depth)], scratch, flops,
-        heights, own, cross, *parts, inner_a, inner_b, done_inner, weights, bias[None],
-    )[0]
+    outputs = [(1, quarter, COL_Y, COL_Y, depth)]
+    args = (heights, own, cross, *parts, *hidden, done_inner, *matrices)
+    return call(kernel, "last", [SCALARS] + [WHOLE] * (len(args) - 1), outputs, scratch, flops, *args)[0]
 
 
 def across_pairs(peers):
@@ -391,26 +420,26 @@
     peers, chans = lax.axis_size("space"), lax.axis_size("chan")
     halo = 1 if peers > COL_Y else 0
 
-    own_part = pack(weight_one, bias_one)
+    own_part, fields, cross, mate = prepare(column_heights, weight_one, bias_one, features)
     far_part = lax.ppermute(own_part, ("space", "chan"), far_pairs(peers, chans))
     near_part = lax.ppermute(own_part, "chan", [(c, c ^ 1) for c in range(chans)])
-    fields, cross, mate = arrange(column_heights, features, own_part)
     cross = lax.ppermute(cross, "space", across_pairs(peers))
     mate = to_mate(mate)
     if halo:
         fields = with_x_borders(jnp.concatenate([cross, fields, mate[None]], axis=0), peers)
         cross, fields, mate = fields[:2], fields[2:-1], fields[-1]
 
-    inner_a, last_a = first_inner(halo, False, column_heights, fields, mate, own_part, near_part, mate)
+    matrices = fill(column_heights, weight_two, bias_two, mate)
+    inner_a, last_a = first_inner(halo, False, column_heights, fields, mate, own_part, near_part, matrices[-1])
     mate_a = to_mate(last_a)
+    far_part, last_a = lax.optimization_barrier((far_part, last_a))
     other_part = to_mate(far_part)
     inner_b, last_b = first_inner(halo, True, column_heights, fields, mate, far_part, other_part, last_a)
     mate_b = to_mate(last_b)
-    done_inner = second_inner(
-        halo, column_heights, inner_a, inner_b, last_a, last_b, mate_a, mate_b, weight_two, bias_two
-    )
+    done_inner = second_inner(halo, column_heights, inner_a, inner_b, last_a, last_b, matrices)
     parts = (own_part, near_part, far_part, other_part)
-    return last(halo, column_heights, fields, cross, parts, inner_a, inner_b, done_inner, weight_two, bias_two)
+    hidden = (inner_a, inner_b, last_a, last_b, mate_a, mate_b)
+    return last(halo, column_heights, fields, cross, parts, hidden, done_inner, matrices)
 
 
 def solution(mesh):

time: 53.7 us -> 53.6 us (level)
  Pallas kernels: 30.9 us -> 34.2 us
  local copies, waits for them, and re-layouts: 4.44 us -> 2.29 us
  starting transfers between devices: 14.7 us -> 12.8 us
  waiting for transfers between devices: 3.17 us -> 4.11 us
    pallas_call x6, Pallas kernels: 30.9 us -> 34.2 us  [call(): pl.pallas_call(kernel, out_shape=[jax.ShapeDtypeStruct(*each) for each in...]
    ppermute x1, waiting for transfers between devices: 0.24 us -> 3.06 us  [on_device(): lax.ppermute(own_part, 'chan', [(c, c ^ 1) for c in range(chans)])]
    ppermute x1, starting transfers between devices: 4.77 us -> 2.2 us  [on_device(): lax.ppermute(own_part, ('space', 'chan'), far_pairs(peers, chans))]
    unnamed x14 -> x10, local copies, waits for them, and re-layouts: 4.44 us -> 2.29 us
    ppermute x1, waiting for transfers between devices: 1.5 us -> 0.01 us  [on_device(): lax.ppermute(own_part, ('space', 'chan'), far_pairs(peers, chans))]
    ppermute x1, starting transfers between devices: 0.01 us -> 1.36 us  [on_device(): lax.ppermute(own_part, 'chan', [(c, c ^ 1) for c in range(chans)])]
    ppermute x4, starting transfers between devices: 6.07 us -> 4.74 us  [to_mate(): lax.ppermute(value, 'space', [(i, i ^ 1) for i in range(lax.axis_size('sp...]
    ppermute x1, starting transfers between devices: 3.91 us -> 4.51 us  [on_device(): cross = lax.ppermute(cross, 'space', across_pairs(peers))]
  transfers between devices with their start and end apart: 7 -> 7, of which waited for: 3 -> 2; matrix products, arithmetic and copies ran while one was open for 0% -> 0% of each run, Pallas kernels for 41% -> 40%
where the time goes in v1:
time: 53.6 us; the launch traced here: 53.5 us
  Pallas kernels  34.2 us (64%)
  starting transfers between devices  12.8 us (24%)
  waiting for transfers between devices  4.11 us (8%)
  local copies, waits for them, and re-layouts  2.29 us (4%)
    pallas_call x6, Pallas kernels, call(): pl.pallas_call(kernel, out_shape=[jax.ShapeDtypeStruct(*each) for each in...  34.2 us
    ppermute x4, starting transfers between devices, to_mate(): lax.ppermute(value, 'space', [(i, i ^ 1) for i in range(lax.axis_size('sp...  4.74 us
    ppermute x1, starting transfers between devices, on_device(): cross = lax.ppermute(cross, 'space', across_pairs(peers))  4.51 us
    ppermute x1, waiting for transfers between devices, on_device(): lax.ppermute(own_part, 'chan', [(c, c ^ 1) for c in range(chans)])  3.06 us
    unnamed x10, local copies, waits for them, and re-layouts  2.29 us
    ppermute x1, starting transfers between devices, on_device(): lax.ppermute(own_part, ('space', 'chan'), far_pairs(peers, chans))  2.2 us
    ppermute x1, starting transfers between devices, on_device(): lax.ppermute(own_part, 'chan', [(c, c ^ 1) for c in range(chans)])  1.36 us
  transfers between devices with their start and end apart: 7, of which 2 were waited for; matrix products, arithmetic and copies ran while one was open for 0% of the time, Pallas kernels for 40%

profile of v1, /device:TPU:1, one launch (start us, length us, event | category | flops | bytes accessed | tf_op | source)
XLA Modules:
  0.0 53.5 jit_solution(10535533649201149956)
XLA Ops:
  0.0 1.0 %copy-done.1 = bf16[27,32,128]{2,1,0:T(8,128)(2,1)S(1)} copy-done((bf16[27,32,128]{2,1,0:T(8,128)(2,1)S(1)}, bf16[27,32,128]{2,1,0:T(8,128)(2,1)}, u32[]{:S(2)}) %copy-start.1) | copy-done | bytes 221208
  1.0 0.7 %copy-done.2 = s32[8]{0:T(128)S(1)} copy-done((s32[8]{0:T(128)S(1)}, s32[8]{0:T(128)}, u32[]{:S(2)}) %copy-start.2) | copy-done | bytes 56
  1.6 0.7 %copy-done.3 = f32[32]{0:T(128)S(1)} copy-done((f32[32]{0:T(128)S(1)}, f32[32]{0:T(128)}, u32[]{:S(2)}) %copy-start.3) | copy-done | bytes 152
  2.3 4.4 %prepare.1 = (bf16[28,32,128]{2,1,0:T(8,128)(2,1)S(1)}, bf16[8,8,128,256]{3,2,1,0:T(8,128)(2,1)S(1)}, bf16[2,8,128,256]{3,2,1,0:T(8,128)(2,1)S(1)}, bf16[8,128,256]{2,1,0:T(8,128)(2,1)S(1)}) custom-call(s32[8]{0:T(128)S(1)} %copy-done.2, bf16[27,32,128]{2,1,0:T(8,128)(2,1)S(1)} %copy-done.1, f32[1,32]{1,0:T(1,128)S(1)} %bitcast.2, ...), custom_call_target="tpu_custom_call" | custom-call | tf_op jit(solution)/shard_map/prepare/pallas_call | solution.py:313
  6.7 4.5 %collective-permute-start = (bf16[2,8,128,256]{3,2,1,0:T(8,128)(2,1)S(1)}, bf16[2,8,128,256]{3,2,1,0:T(8,128)(2,1)S(1)}, u32[]{:S(2)}, u32[]{:S(2)}) collective-permute-start(bf16[2,8,128,256]{3,2,1,0:T(8,128)(2,1)S(1)} %get-tuple-element.20), channel_id=1, source_target_pairs={{4,8},{8,4},{12,16},{16,12},{20,24},{24,20},{5,9},{9,5},{13,17},{1... | collective-permute-start | bytes 3145736 | tf_op jit(solution)/shard_map/ppermute | solution.py:426
  11.2 0.1 collective-permute-start.3
  11.3 1.4 %collective-permute-start.1 = (bf16[28,32,128]{2,1,0:T(8,128)(2,1)S(1)}, bf16[28,32,128]{2,1,0:T(8,128)(2,1)S(1)}, u32[]{:S(2)}, u32[]{:S(2)}) collective-permute-start(bf16[28,32,128]{2,1,0:T(8,128)(2,1)S(1)} %get-tuple-element.21.part_a.part_0), channel_id=1, source_target_pairs={{0,1},{1,0},{2,3},{3,2},{4,5},{5,4},{6,7},{7,6},{8,9},{9,8},{10,11... | collective-permute-start | bytes 688136 | tf_op jit(solution)/shard_map/ppermute | solution.py:425
  12.7 2.2 %collective-permute-start.2 = (bf16[28,32,128]{2,1,0:T(8,128)(2,1)S(1)}, bf16[28,32,128]{2,1,0:T(8,128)(2,1)S(1)}, u32[]{:S(2)}, u32[]{:S(2)}) collective-permute-start(bf16[28,32,128]{2,1,0:T(8,128)(2,1)S(1)} %get-tuple-element.21.part_a.part_0), channel_id=1, source_target_pairs={{0,2},{1,3},{2,0},{3,1},{4,7},{5,6},{6,5},{7,4},{8,10},{9,11},{10,... | collective-permute-start | bytes 688136 | tf_op jit(solution)/shard_map/ppermute | solution.py:424
  14.8 0.0 collective-permute-done.3.after.mate
  14.9 0.0 copy-done
  14.9 0.8 %fill.1 = (bf16[192,1536]{1,0:T(8,128)(2,1)S(1)}, bf16[192,1152]{1,0:T(8,128)(2,1)S(1)}, bf16[192,1152]{1,0:T(8,128)(2,1)S(1)}, f32[64,128]{1,0:T(8,128)S(1)}) custom-call(s32[8]{0:T(128)S(1)} %copy-done.2, bf16[27,32,128]{2,1,0:T(8,128)(2,1)S(1)} %copy-done, f32[1,32]{1,0:T(1,128)S(1)} %bitcast.3, bf16[8,128,256]{2,1,0:T(8,128)(2,1)S(1)} %collective-permute-done.3.after.mate), custom_call_target="tpu_custom_call" | custom-call | tf_op jit(solution)/shard_map/fill/pallas_call | solution.py:313
  15.7 3.1 %collective-permute-done.1.part_b.part_1 = bf16[28,32,128]{2,1,0:T(8,128)(2,1)S(1)} collective-permute-done((bf16[28,32,128]{2,1,0:T(8,128)(2,1)S(1)}, bf16[28,32,128]{2,1,0:T(8,128)(2,1)S(1)}, u32[]{:S(2)}, u32[]{:S(2)}) %collective-permute-start.1) | collective-permute-done | bytes 229408 | tf_op jit(solution)/shard_map/ppermute | solution.py:425
  18.7 8.3 %first_near.1 = (bf16[6,8,64,256]{3,2,1,0:T(8,128)(2,1)S(1)}, bf16[8,64,256]{2,1,0:T(8,128)(2,1)S(1)}) custom-call(s32[8]{0:T(128)S(1)} %copy-done.2, bf16[8,8,128,256]{3,2,1,0:T(8,128)(2,1)S(1)} %get-tuple-element.19.own, bf16[8,128,256]{2,1,0:T(8,128)(2,1)S(1)} %collective-permute-done.3.after.mate, ...), custom_call_target="tpu_custom_call" | custom-call | tf_op jit(solution)/shard_map/first_near/pallas_call | solution.py:313
  27.0 0.0 collective-permute-done.2.part_a.part_2
  27.0 4.1 %collective-permute-start.4 = (bf16[28,32,128]{2,1,0:T(8,128)(2,1)S(1)}, bf16[28,32,128]{2,1,0:T(8,128)(2,1)S(1)}, u32[]{:S(2)}, u32[]{:S(2)}) collective-permute-start(bf16[28,32,128]{2,1,0:T(8,128)(2,1)S(1)} %collective-permute-done.2.part_a.part_2), channel_id=1, source_target_pairs={{0,4},{4,0},{8,12},{12,8},{16,20},{20,16},{24,28},{28,24},{1,5},{5... | collective-permute-start | bytes 688136 | tf_op jit(solution)/shard_map/ppermute | solution.py:400
  31.2 0.1 collective-permute-start.5
  31.2 1.0 %collective-permute-done.4.part_b.part_3 = bf16[28,32,128]{2,1,0:T(8,128)(2,1)S(1)} collective-permute-done((bf16[28,32,128]{2,1,0:T(8,128)(2,1)S(1)}, bf16[28,32,128]{2,1,0:T(8,128)(2,1)S(1)}, u32[]{:S(2)}, u32[]{:S(2)}) %collective-permute-start.4) | collective-permute-done | bytes 229408 | tf_op jit(solution)/shard_map/ppermute | solution.py:400
  32.3 8.3 %first_far.1 = (bf16[6,8,64,256]{3,2,1,0:T(8,128)(2,1)S(1)}, bf16[8,64,256]{2,1,0:T(8,128)(2,1)S(1)}) custom-call(s32[8]{0:T(128)S(1)} %copy-done.2, bf16[8,8,128,256]{3,2,1,0:T(8,128)(2,1)S(1)} %get-tuple-element.19.own, bf16[8,128,256]{2,1,0:T(8,128)(2,1)S(1)} %collective-permute-done.3.after.mate, ...), custom_call_target="tpu_custom_call" | custom-call | tf_op jit(solution)/shard_map/first_far/pallas_call | solution.py:313
  40.6 0.5 collective-permute-start.6
  41.0 4.2 %second_inner.1.done_inner = bf16[5,8,32,256]{3,2,1,0:T(8,128)(2,1)S(1)} custom-call(s32[8]{0:T(128)S(1)} %copy-done.2, bf16[6,8,64,256]{3,2,1,0:T(8,128)(2,1)S(1)} %get-tuple-element.26.inner_a, bf16[6,8,64,256]{3,2,1,0:T(8,128)(2,1)S(1)} %get-tuple-element.28.inner_b, bf16[8,64,256]{2,1,0:T(8,128)(2,1)S(1)} %get-tuple-element.27.after.last_a, ...), custom_call_target="tpu_custom_call" | custom-call | tf_op jit(solution)/shard_map/second_inner/pallas_call | solution.py:313
  45.2 0.0 collective-permute-done.5.mate_a
  45.2 0.0 collective-permute-done.6.mate_b
  45.2 0.0 collective-permute-done.cross
  45.2 8.3 %last.1 = bf16[1,32,8,8,256]{4,3,2,1,0:T(8,128)(2,1)} custom-call(s32[8]{0:T(128)S(1)} %copy-done.2, bf16[8,8,128,256]{3,2,1,0:T(8,128)(2,1)S(1)} %get-tuple-element.19.own, bf16[2,8,128,256]{3,2,1,0:T(8,128)(2,1)S(1)} %collective-permute-done.cross, bf16[28,32,128]{2,1,0:T(8,128)(2,1)S(1)} %get-tuple-element.21.part_a.part_0, ...), custom_call_target="tpu_custom_call" | custom-call | tf_op jit(solution)/shard_map/last/pallas_call | solution.py:313
  (6 shorter events, 0.0 us)
Async XLA Ops:
  0.0 14.9 %copy-start = (bf16[27,32,128]{2,1,0:T(8,128)(2,1)S(1)}, bf16[27,32,128]{2,1,0:T(8,128)(2,1)}, u32[]{:S(2)}) copy-start(bf16[27,32,128]{2,1,0:T(8,128)(2,1)} %weights.3) | copy-start | bytes 663556
  0.0 1.0 %copy-start.1 = (bf16[27,32,128]{2,1,0:T(8,128)(2,1)S(1)}, bf16[27,32,128]{2,1,0:T(8,128)(2,1)}, u32[]{:S(2)}) copy-start(bf16[27,32,128]{2,1,0:T(8,128)(2,1)} %weights.2) | copy-start | bytes 663556
  1.0 0.7 %copy-start.2 = (s32[8]{0:T(128)S(1)}, s32[8]{0:T(128)}, u32[]{:S(2)}) copy-start(s32[8]{0:T(128)} %heights.11) | copy-start | bytes 100
  1.6 0.7 %copy-start.3 = (f32[32]{0:T(128)S(1)}, f32[32]{0:T(128)}, u32[]{:S(2)}) copy-start(f32[32]{0:T(128)} %param.9) | copy-start | bytes 388
  2.3 12.6 %copy-start.4 = (f32[32]{0:T(128)S(1)}, f32[32]{0:T(128)}, u32[]{:S(2)}) copy-start(f32[32]{0:T(128)} %param.11) | copy-start | bytes 388
  6.7 38.5 %collective-permute-start = (bf16[2,8,128,256]{3,2,1,0:T(8,128)(2,1)S(1)}, bf16[2,8,128,256]{3,2,1,0:T(8,128)(2,1)S(1)}, u32[]{:S(2)}, u32[]{:S(2)}) collective-permute-start(bf16[2,8,128,256]{3,2,1,0:T(8,128)(2,1)S(1)} %get-tuple-element.20), channel_id=1, source_target_pairs={{4,8},{8,4},{12,16},{16,12},{20,24},{24,20},{5,9},{9,5},{13,17},{1... | collective-permute-start | bytes 3145736 | tf_op jit(solution)/shard_map/ppermute | solution.py:426
  11.2 3.6 %collective-permute-start.3 = (bf16[8,128,256]{2,1,0:T(8,128)(2,1)S(1)}, bf16[8,128,256]{2,1,0:T(8,128)(2,1)S(1)}, u32[]{:S(2)}, u32[]{:S(2)}) collective-permute-start(bf16[8,128,256]{2,1,0:T(8,128)(2,1)S(1)} %get-tuple-element.22), channel_id=1, source_target_pairs={{0,4},{4,0},{8,12},{12,8},{16,20},{20,16},{24,28},{28,24},{1,5},{5... | collective-permute-start | bytes 1572872 | tf_op jit(solution)/shard_map/ppermute | solution.py:400
  11.3 7.5 %collective-permute-start.1 = (bf16[28,32,128]{2,1,0:T(8,128)(2,1)S(1)}, bf16[28,32,128]{2,1,0:T(8,128)(2,1)S(1)}, u32[]{:S(2)}, u32[]{:S(2)}) collective-permute-start(bf16[28,32,128]{2,1,0:T(8,128)(2,1)S(1)} %get-tuple-element.21.part_a.part_0), channel_id=1, source_target_pairs={{0,1},{1,0},{2,3},{3,2},{4,5},{5,4},{6,7},{7,6},{8,9},{9,8},{10,11... | collective-permute-start | bytes 688136 | tf_op jit(solution)/shard_map/ppermute | solution.py:425
  12.7 14.4 %collective-permute-start.2 = (bf16[28,32,128]{2,1,0:T(8,128)(2,1)S(1)}, bf16[28,32,128]{2,1,0:T(8,128)(2,1)S(1)}, u32[]{:S(2)}, u32[]{:S(2)}) collective-permute-start(bf16[28,32,128]{2,1,0:T(8,128)(2,1)S(1)} %get-tuple-element.21.part_a.part_0), channel_id=1, source_target_pairs={{0,2},{1,3},{2,0},{3,1},{4,7},{5,6},{6,5},{7,4},{8,10},{9,11},{10,... | collective-permute-start | bytes 688136 | tf_op jit(solution)/shard_map/ppermute | solution.py:424
  27.0 5.3 %collective-permute-start.4 = (bf16[28,32,128]{2,1,0:T(8,128)(2,1)S(1)}, bf16[28,32,128]{2,1,0:T(8,128)(2,1)S(1)}, u32[]{:S(2)}, u32[]{:S(2)}) collective-permute-start(bf16[28,32,128]{2,1,0:T(8,128)(2,1)S(1)} %collective-permute-done.2.part_a.part_2), channel_id=1, source_target_pairs={{0,4},{4,0},{8,12},{12,8},{16,20},{20,16},{24,28},{28,24},{1,5},{5... | collective-permute-start | bytes 688136 | tf_op jit(solution)/shard_map/ppermute | solution.py:400
  31.2 14.0 %collective-permute-start.5 = (bf16[8,64,256]{2,1,0:T(8,128)(2,1)S(1)}, bf16[8,64,256]{2,1,0:T(8,128)(2,1)S(1)}, u32[]{:S(2)}, u32[]{:S(2)}) collective-permute-start(bf16[8,64,256]{2,1,0:T(8,128)(2,1)S(1)} %get-tuple-element.27.after.last_a), channel_id=1, source_target_pairs={{0,4},{4,0},{8,12},{12,8},{16,20},{20,16},{24,28},{28,24},{1,5},{5... | collective-permute-start | bytes 786440 | tf_op jit(solution)/shard_map/ppermute | solution.py:400
  40.6 4.6 %collective-permute-start.6 = (bf16[8,64,256]{2,1,0:T(8,128)(2,1)S(1)}, bf16[8,64,256]{2,1,0:T(8,128)(2,1)S(1)}, u32[]{:S(2)}, u32[]{:S(2)}) collective-permute-start(bf16[8,64,256]{2,1,0:T(8,128)(2,1)S(1)} %get-tuple-element.29.last_b), channel_id=1, source_target_pairs={{0,4},{4,0},{8,12},{12,8},{16,20},{20,16},{24,28},{28,24},{1,5},{5... | collective-permute-start | bytes 786440 | tf_op jit(solution)/shard_map/ppermute | solution.py:400

commit v2 on v1

--- a/solution.py
+++ b/solution.py
@@ -49,16 +49,21 @@
     return jnp.sum(jnp.where(same, wide, 0.0), axis=1, keepdims=True)
 
 
-def prepare_kernel(heights, weights, bias, features, packed, fields, cross, mate, bias_here, stored, sems):
+def pack_kernel(weights, bias, packed):
+    taps, rows, lanes = weights.shape
+    packed[:taps] = weights[...]
+    column = as_column(bias[...])
+    lane = lax.broadcasted_iota(jnp.int32, (rows, lanes), 1)
+    extra = jnp.zeros((rows, lanes), F32)
+    for at in range(3):
+        piece = column.astype(BF16).astype(F32)
+        extra = jnp.where(lane == at, piece, extra)
+        column = column - piece
+    packed[taps] = extra.astype(BF16)
+
+
+def arrange_kernel(heights, features, after, fields, cross, mate):
     _, channels, width, _, depth = features.shape
-    taps, rows, lanes = weights.shape
-    copies = [
-        pltpu.make_async_copy(bias, bias_here, sems.at[width]),
-        pltpu.make_async_copy(weights, packed.at[pl.ds(0, taps)], sems.at[width + 1]),
-    ]
-    copies += [pltpu.make_async_copy(features.at[0, :, x], stored.at[x], sems.at[x]) for x in range(width)]
-    for copy in copies:
-        copy.start()
     place = Place(heights)
     group = 256 // COL_Y
     row = lax.broadcasted_iota(jnp.int32, (256, 256), 0)
@@ -67,22 +72,9 @@
     y = jnp.where(place.odd == 1, COL_Y - 1 - u, u)
     swap = (column == lax.rem(row, group) * COL_Y + y).astype(F32).astype(BF16)
     live = lax.broadcasted_iota(jnp.int32, (1, depth), 1) < place.top()
-
-    copies[0].wait()
-    column = as_column(bias_here[...])
-    lane = lax.broadcasted_iota(jnp.int32, (rows, lanes), 1)
-    extra = jnp.zeros((rows, lanes), F32)
-    for at in range(3):
-        piece = column.astype(BF16).astype(F32)
-        extra = jnp.where(lane == at, piece, extra)
-        column = column - piece
-    packed[taps] = extra.astype(BF16)
-    copies[1].wait()
-
     for x in range(width):
-        copies[2 + x].wait()
         for first in range(0, channels, group):
-            tile = stored[x, first : first + group].reshape(256, depth)
+            tile = features[0, first : first + group, x].reshape(256, depth)
             moved = jnp.dot(swap, tile, preferred_element_type=F32)
             moved = jnp.where(live, moved, 0.0).astype(BF16).reshape(COL_Y, group, depth)
             fields[:, x, first : first + group] = moved
@@ -142,26 +134,45 @@
     return value.reshape(-1, value.shape[-1])
 
 
-def first_inner_kernel(halo, heights, own, mate, part_a, part_b, after, out, out_last, matrix, low_matrix, high_matrix, bias, *, far):
-    place = Place(heights)
-    slots = place.slots[2:] if far else place.slots[:2]
-    fill_first([part_a, part_b], slots, place.odd, matrix, low_matrix, high_matrix, bias)
-    matrices, width = (matrix, low_matrix, high_matrix), own.shape[1]
-
+def inner_rows(own, out, halo, matrices, bias, top):
     def pair(step, _):
         for more in range(2):
             u = step * 2 + more
-            for x, done in first_row(lambda j, a, b: span_of(own, u + j, a, b), width, halo, matrices, bias, place.top):
+            for x, done in first_row(lambda j, a, b: span_of(own, u + j, a, b), own.shape[1], halo, matrices, bias, top):
                 out[u, x] = done
         return 0
 
     lax.fori_loop(0, (COL_Y - 2) // 2, pair, 0)
 
+
+def first_near_kernel(halo, heights, own, part_a, part_b, after, out, matrix, low_matrix, high_matrix, bias):
+    place = Place(heights)
+    fill_first([part_a, part_b], place.slots[:2], place.odd, matrix, low_matrix, high_matrix, bias)
+    inner_rows(own, out, halo, (matrix, low_matrix, high_matrix), bias, place.top)
+
+
+def first_far_kernel(
+    halo, heights, own, mate, part_a, part_b, near, low_near, high_near, bias_near, after,
+    out, out_last, matrix, low_matrix, high_matrix, bias,
+):
+    place = Place(heights)
+    fill_first([part_a, part_b], place.slots[2:], place.odd, matrix, low_matrix, high_matrix, bias)
+    far = (matrix, low_matrix, high_matrix)
+    inner_rows(own, out, halo, far, bias, place.top)
+
     def get(j, a, b):
         return span_of(mate, a, b) if j == 2 else span_of(own, COL_Y - 2 + j, a, b)
 
-    for x, done in first_row(get, width, halo, matrices, bias, place.top):
-        out_last[x] = done
+    whole_row(get, own.shape[1], halo, ((near, low_near, high_near), bias_near), (far, bias), place.top, out_last)
+
+
+def whole_row(get, stored, halo, near, far, top, out, *at):
+    half = near[1].shape[0]
+    levels = None
+    for first, (matrices, bias) in ((0, near), (half, far)):
+        for x, done in first_row(get, stored, halo, matrices, bias, top):
+            levels = done.shape[1]
+            out[(*at, x, slice(first, first + half), slice(0, levels))] = done
 
 
 def fill_second(weights, place, matrix, low_matrix, high_matrix):
@@ -214,7 +225,7 @@
     fill_bias(bias, both)
 
 
-def second_inner_kernel(halo, heights, inner_a, inner_b, last_a, last_b, matrix, low_matrix, high_matrix, both, out):
+def second_inner_kernel(halo, heights, inner_a, inner_b, row_seven, matrix, low_matrix, high_matrix, both, out):
     place = Place(heights)
     matrices, width, top = (matrix, low_matrix, high_matrix), inner_a.shape[1], place.top()
 
@@ -229,7 +240,7 @@
     lax.fori_loop(0, 2, pair, 0)
 
     def row(u, a, b):
-        return halves(inner_a, inner_b, u - 1, a, b) if u < 7 else halves(last_a, last_b, a, b)
+        return halves(inner_a, inner_b, u - 1, a, b) if u < 7 else [row_seven[x] for x in range(a, b)]
 
     for x, here, beside in second_row(lambda j, a, b: row(5 + j, a, b), width, halo, matrices, both[:, 0:1], top):
         out[4, x] = here
@@ -237,13 +248,12 @@
 
 
 def last_kernel(
-    halo, heights, own, cross, part_0, part_1, part_2, part_3, inner_a, inner_b, last_a, last_b, mate_a, mate_b,
-    done_inner, matrix_two, low_two, high_two, both, out, matrix, low_matrix, high_matrix, bias_one, edge, done_edge,
+    halo, heights, own, cross, near, low_near, high_near, bias_near, far, low_far, high_far, bias_far,
+    inner_a, inner_b, row_seven, mate, done_inner, matrix_two, low_two, high_two, both, out, edge, done_edge,
 ):
     place = Place(heights)
-    fill_first([part_0, part_1, part_2, part_3], [place.slots[0], place.slots[1], 2 + place.slots[2], 2 + place.slots[3]], place.odd, matrix, low_matrix, high_matrix, bias_one)
     width, depth = own.shape[1], own.shape[3]
-    matrices = (matrix, low_matrix, high_matrix)
+    near, far = ((near, low_near, high_near), bias_near), ((far, low_far, high_far), bias_far)
 
     def fields(u, a, b):
         return span_of(own, u, a, b) if u >= 0 else span_of(cross, -1 - u, a, b)
@@ -255,10 +265,9 @@
         def get(j, a, b):
             return fields(u - 1 + j, a, b)[:, :levels]
 
-        for x, done in first_row(get, width, halo, matrices, bias_one, top):
-            edge[u + 1, x, :, :levels] = done
-            if levels < depth:
-                edge[u + 1, x, :, levels:] = jnp.zeros((done.shape[0], depth - levels), BF16)
+        whole_row(get, width, halo, near, far, top, edge, u + 1)
+        if levels < depth:
+            edge[u + 1, :, :, levels:] = jnp.zeros((*edge.shape[1:3], depth - levels), BF16)
 
     part = depth // 2 if depth % 256 == 0 else depth
     highest = place.top(0, across=True)
@@ -281,7 +290,7 @@
             return [edge[u + 1, x] for x in range(a, b)]
         if u < 7:
             return halves(inner_a, inner_b, u - 1, a, b)
-        return halves(last_a, last_b, a, b) if u == 7 else halves(mate_a, mate_b, a, b)
+        return [(row_seven if u == 7 else mate)[x] for x in range(a, b)]
 
     for at, u in enumerate((0, 1, 7)):
         for x, here, beside in second_row(
@@ -308,42 +317,38 @@
         out[0, :, x] = moved.reshape(quarter, COL_Y, depth)
 
 
-def call(kernel, name, inputs, outputs, scratch, flops, *args, kinds=None, vmem=16):
-    nbytes = sum(2 * a.size for a in args)
+SHORT, LONG = 2**6, 2**27
+
+
+def call(kernel, name, inputs, outputs, scratch, nbytes, *args, kinds=None):
     return pl.pallas_call(
         kernel,
         out_shape=[jax.ShapeDtypeStruct(*each) for each in zip(outputs, kinds or [BF16] * len(outputs))],
         in_specs=inputs,
         out_specs=[WHOLE] * len(outputs),
         scratch_shapes=scratch,
-        compiler_params=pltpu.CompilerParams(vmem_limit_bytes=vmem * 2**20),
-        cost_estimate=pl.CostEstimate(flops=0, bytes_accessed=0, transcendentals=0),
+        compiler_params=pltpu.CompilerParams(vmem_limit_bytes=16 * 2**20),
+        cost_estimate=pl.CostEstimate(flops=64 * nbytes, bytes_accessed=nbytes, transcendentals=0),
         name=name,
     )(*args)
 
 
-def prepare(heights, weights, bias, features):
+def pack(weights, bias):
+    taps, rows, lanes = weights.shape
+    return call(pack_kernel, "pack", [WHOLE, WHOLE], [(taps + 1, rows, lanes)], [], LONG, weights, bias[None])[0]
+
+
+def arrange(heights, features, after):
     _, channels, width, _, depth = features.shape
-    taps, rows, lanes = weights.shape
     row = (width, channels, depth)
-    outputs = [(taps + 1, rows, lanes), (COL_Y, *row), (2, *row), row]
-    scratch = [
-        pltpu.VMEM((1, rows), F32),
-        pltpu.VMEM((width, channels, COL_Y, depth), BF16),
-        pltpu.SemaphoreType.DMA((width + 2,)),
-    ]
-    inputs = [SCALARS, ANY, ANY, ANY]
-    return call(prepare_kernel, "prepare", inputs, outputs, scratch, 0, heights, weights, bias[None], features, vmem=47)
-
-
-def first_scratch(channels, rows):
+    outputs = [(COL_Y, *row), (2, *row), row]
+    return call(arrange_kernel, "arrange", [SCALARS, WHOLE, ANY], outputs, [], SHORT, heights, features, after)
+
+
+def first_matrices(channels, rows):
     wide = TAPS * channels
-    return [
-        pltpu.VMEM((TAPS * rows, 3 * wide), BF16),
-        pltpu.VMEM((TAPS * rows, 2 * wide), BF16),
-        pltpu.VMEM((TAPS * rows, 2 * wide), BF16),
-        pltpu.VMEM((rows, 128), F32),
-    ]
+    shapes = [(TAPS * rows, 3 * wide), (TAPS * rows, 2 * wide), (TAPS * rows, 2 * wide), (rows, 128)]
+    return shapes, [BF16, BF16, BF16, F32]
 
 
 def fill(heights, weights, bias, after):
@@ -351,40 +356,49 @@
     tall = TAPS * 2 * quarter
     outputs = [(tall, 12 * channels), (tall, 9 * channels), (tall, 9 * channels), (2 * quarter, 128)]
     kinds = [BF16, BF16, BF16, F32]
-    return call(fill_kernel, "fill", [SCALARS, WHOLE, WHOLE, ANY], outputs, [], 0, heights, weights, bias[None], after, kinds=kinds)
-
-
-def first_inner(halo, far, heights, own, mate, part_a, part_b, after):
+    return call(fill_kernel, "fill", [SCALARS, WHOLE, WHOLE, ANY], outputs, [], SHORT, heights, weights, bias[None], after, kinds=kinds)
+
+
+def first_near(halo, heights, own, part_a, part_b, after):
     _, _, channels, depth = own.shape
     half, width = 2 * part_a.shape[1], COL_Y + 2 * halo
-    kernel = functools.partial(first_inner_kernel, halo, far=far)
-    inputs = [SCALARS] + [WHOLE] * 4 + [ANY]
-    outputs = [(COL_Y - 2, width, half, depth), (width, half, depth)]
-    flops = 2 * (COL_Y - 1) * COL_Y * depth * 27 * channels * half
-    name = "first_far" if far else "first_near"
-    return call(kernel, name, inputs, outputs, first_scratch(channels, half), flops, heights, own, mate, part_a, part_b, after)
-
-
-def second_inner(halo, heights, inner_a, inner_b, last_a, last_b, matrices):
-    rows, _, half, depth = inner_a.shape
+    shapes, kinds = first_matrices(channels, half)
+    inner, *matrices = call(
+        functools.partial(first_near_kernel, halo), "first_near", [SCALARS] + [WHOLE] * 3 + [ANY],
+        [(COL_Y - 2, width, half, depth), *shapes], [], LONG, heights, own, part_a, part_b, after, kinds=[BF16, *kinds],
+    )
+    return inner, matrices
+
+
+def first_far(halo, heights, own, mate, part_a, part_b, near, after):
+    _, _, channels, depth = own.shape
+    half, width = 2 * part_a.shape[1], COL_Y + 2 * halo
+    shapes, kinds = first_matrices(channels, half)
+    inner, row_seven, *matrices = call(
+        functools.partial(first_far_kernel, halo), "first_far", [SCALARS] + [WHOLE] * 8 + [ANY],
+        [(COL_Y - 2, width, half, depth), (width, channels, depth), *shapes], [], SHORT,
+        heights, own, mate, part_a, part_b, *near, after, kinds=[BF16, BF16, *kinds],
+    )
+    return inner, row_seven, matrices
+
+
+def second_inner(halo, heights, inner_a, inner_b, row_seven, matrices):
+    rows, _, _, depth = inner_a.shape
     quarter = matrices[-1].shape[0] // 2
+    outputs = [(rows - 1, COL_Y, quarter, depth)]
+    args = (heights, inner_a, inner_b, row_seven, *matrices)
     kernel = functools.partial(second_inner_kernel, halo)
-    flops = 2 * (rows - 1) * COL_Y * depth * 27 * 2 * half * quarter
-    outputs = [(rows - 1, COL_Y, quarter, depth)]
-    args = (heights, inner_a, inner_b, last_a, last_b, *matrices)
-    return call(kernel, "second_inner", [SCALARS] + [WHOLE] * 8, outputs, [], flops, *args)[0]
-
-
-def last(halo, heights, own, cross, parts, hidden, done_inner, matrices):
+    return call(kernel, "second_inner", [SCALARS] + [WHOLE] * (len(args) - 1), outputs, [], SHORT, *args)[0]
+
+
+def last(halo, heights, own, cross, near, far, hidden, done_inner, matrices):
     _, _, channels, depth = own.shape
     quarter, width = matrices[-1].shape[0] // 2, COL_Y + 2 * halo
+    scratch = [pltpu.VMEM((2, width, channels, depth), BF16), pltpu.VMEM((3, COL_Y, quarter, depth), BF16)]
+    outputs = [(1, quarter, COL_Y, COL_Y, depth)]
+    args = (heights, own, cross, *near, *far, *hidden, done_inner, *matrices)
     kernel = functools.partial(last_kernel, halo)
-    scratch = first_scratch(channels, channels)
-    scratch += [pltpu.VMEM((2, width, channels, depth), BF16), pltpu.VMEM((3, COL_Y, quarter, depth), BF16)]
-    flops = 4 * COL_Y * depth * 27 * channels * (channels + quarter)
-    outputs = [(1, quarter, COL_Y, COL_Y, depth)]
-    args = (heights, own, cross, *parts, *hidden, done_inner, *matrices)
-    return call(kernel, "last", [SCALARS] + [WHOLE] * (len(args) - 1), outputs, scratch, flops, *args)[0]
+    return call(kernel, "last", [SCALARS] + [WHOLE] * (len(args) - 1), outputs, scratch, SHORT, *args)[0]
 
 
 def across_pairs(peers):
@@ -420,26 +434,25 @@
     peers, chans = lax.axis_size("space"), lax.axis_size("chan")
     halo = 1 if peers > COL_Y else 0
 
-    own_part, fields, cross, mate = prepare(column_heights, weight_one, bias_one, features)
+    own_part = pack(weight_one, bias_one)
+    near_part = lax.ppermute(own_part, "chan", [(c, c ^ 1) for c in range(chans)])
     far_part = lax.ppermute(own_part, ("space", "chan"), far_pairs(peers, chans))
-    near_part = lax.ppermute(own_part, "chan", [(c, c ^ 1) for c in range(chans)])
+    fields, cross, mate = arrange(column_heights, features, own_part)
     cross = lax.ppermute(cross, "space", across_pairs(peers))
     mate = to_mate(mate)
     if halo:
         fields = with_x_borders(jnp.concatenate([cross, fields, mate[None]], axis=0), peers)
         cross, fields, mate = fields[:2], fields[2:-1], fields[-1]
 
-    matrices = fill(column_heights, weight_two, bias_two, mate)
-    inner_a, last_a = first_inner(halo, False, column_heights, fields, mate, own_part, near_part, matrices[-1])
-    mate_a = to_mate(last_a)
-    far_part, last_a = lax.optimization_barrier((far_part, last_a))
+    matrices = fill(column_heights, weight_two, bias_two, own_part)
+    inner_a, near = first_near(halo, column_heights, fields, own_part, near_part, matrices[-1])
+    far_part, inner_a = lax.optimization_barrier((far_part, inner_a))
     other_part = to_mate(far_part)
-    inner_b, last_b = first_inner(halo, True, column_heights, fields, mate, far_part, other_part, last_a)
-    mate_b = to_mate(last_b)
-    done_inner = second_inner(halo, column_heights, inner_a, inner_b, last_a, last_b, matrices)
-    parts = (own_part, near_part, far_part, other_part)
-    hidden = (inner_a, inner_b, last_a, last_b, mate_a, mate_b)
-    return last(halo, column_heights, fields, cross, parts, hidden, done_inner, matrices)
+    inner_b, row_seven, far = first_far(halo, column_heights, fields, mate, far_part, other_part, near, inner_a)
+    mate = to_mate(row_seven)
+    done_inner = second_inner(halo, column_heights, inner_a, inner_b, row_seven, matrices)
+    hidden = (inner_a, inner_b, row_seven, mate)
+    return last(halo, column_heights, fields, cross, near, far, hidden, done_inner, matrices)
 
 
 def solution(mesh):

time: 53.6 us -> 44.6 us (0.83)
  Pallas kernels: 34.2 us -> 31.2 us
  waiting for transfers between devices: 4.11 us -> 1.39 us
  starting transfers between devices: 12.8 us -> 10.1 us
  local copies, waits for them, and re-layouts: 2.29 us -> 1.61 us
    ppermute x1, waiting for transfers between devices: 3.06 us -> 0.01 us  [on_device(): lax.ppermute(own_part, 'chan', [(c, c ^ 1) for c in range(chans)])]
    pallas_call x6 -> x7, Pallas kernels: 34.2 us -> 31.2 us  [call(): pl.pallas_call(kernel, out_shape=[jax.ShapeDtypeStruct(*each) for each in...]
    ppermute x4 -> x3, starting transfers between devices: 4.74 us -> 2.7 us  [to_mate(): lax.ppermute(value, 'space', [(i, i ^ 1) for i in range(lax.axis_size('sp...]
    ppermute x1, starting transfers between devices: 4.51 us -> 3.01 us  [on_device(): cross = lax.ppermute(cross, 'space', across_pairs(peers))]
    ppermute x1, starting transfers between devices: 1.36 us -> 2.19 us  [on_device(): lax.ppermute(own_part, 'chan', [(c, c ^ 1) for c in range(chans)])]
    unnamed x10 -> x12, local copies, waits for them, and re-layouts: 2.29 us -> 1.61 us
    ppermute x4 -> x3, waiting for transfers between devices: 1.04 us -> 1.12 us  [to_mate(): lax.ppermute(value, 'space', [(i, i ^ 1) for i in range(lax.axis_size('sp...]
  transfers between devices with their start and end apart: 7 -> 6, of which waited for: 2 -> 2; matrix products, arithmetic and copies ran while one was open for 0% -> 0% of each run, Pallas kernels for 40% -> 52%
where the time goes in v2:
time: 44.6 us; the launch traced here: 44.4 us
  Pallas kernels  31.2 us (70%)
  starting transfers between devices  10.1 us (23%)
  local copies, waits for them, and re-layouts  1.61 us (4%)
  waiting for transfers between devices  1.39 us (3%)
    pallas_call x7, Pallas kernels, call(): pl.pallas_call(kernel, out_shape=[jax.ShapeDtypeStruct(*each) for each in...  31.2 us
    ppermute x1, starting transfers between devices, on_device(): cross = lax.ppermute(cross, 'space', across_pairs(peers))  3.01 us
    ppermute x3, starting transfers between devices, to_mate(): lax.ppermute(value, 'space', [(i, i ^ 1) for i in range(lax.axis_size('sp...  2.7 us
    ppermute x1, starting transfers between devices, on_device(): lax.ppermute(own_part, ('space', 'chan'), far_pairs(peers, chans))  2.19 us
    ppermute x1, starting transfers between devices, on_device(): lax.ppermute(own_part, 'chan', [(c, c ^ 1) for c in range(chans)])  2.19 us
    unnamed x12, local copies, waits for them, and re-layouts  1.61 us
    ppermute x3, waiting for transfers between devices, to_mate(): lax.ppermute(value, 'space', [(i, i ^ 1) for i in range(lax.axis_size('sp...  1.12 us
  transfers between devices with their start and end apart: 6, of which 2 were waited for; matrix products, arithmetic and copies ran while one was open for 0% of the time, Pallas kernels for 52%

profile of v2, /device:TPU:1, one launch (start us, length us, event | category | flops | bytes accessed | tf_op | source)
XLA Modules:
  0.0 44.4 jit_solution(14679387130585348539)
XLA Ops:
  0.0 0.9 %copy-done.4 = bf16[27,32,128]{2,1,0:T(8,128)(2,1)S(1)} copy-done((bf16[27,32,128]{2,1,0:T(8,128)(2,1)S(1)}, bf16[27,32,128]{2,1,0:T(8,128)(2,1)}, u32[]{:S(2)}) %copy-start.4) | copy-done | bytes 221208
  0.9 0.7 %copy-done.5 = f32[32]{0:T(128)S(1)} copy-done((f32[32]{0:T(128)S(1)}, f32[32]{0:T(128)}, u32[]{:S(2)}) %copy-start.5) | copy-done | bytes 152
  1.6 0.1 pack.1.after.part_a
  1.7 0.0 copy-start.1
  1.7 0.0 copy-start.3
  1.7 2.2 %collective-permute-start.1 = (bf16[28,32,128]{2,1,0:T(8,128)(2,1)S(1)}, bf16[28,32,128]{2,1,0:T(8,128)(2,1)S(1)}, u32[]{:S(2)}, u32[]{:S(2)}) collective-permute-start(bf16[28,32,128]{2,1,0:T(8,128)(2,1)S(1)} %pack.1.after.part_a), channel_id=1, source_target_pairs={{0,1},{1,0},{2,3},{3,2},{4,5},{5,4},{6,7},{7,6},{8,9},{9,8},{10,11... | collective-permute-start | bytes 688136 | tf_op jit(solution)/shard_map/ppermute | solution.py:438
  3.9 2.2 %collective-permute-start.3 = (bf16[28,32,128]{2,1,0:T(8,128)(2,1)S(1)}, bf16[28,32,128]{2,1,0:T(8,128)(2,1)S(1)}, u32[]{:S(2)}, u32[]{:S(2)}) collective-permute-start(bf16[28,32,128]{2,1,0:T(8,128)(2,1)S(1)} %pack.1.after.part_a), channel_id=1, source_target_pairs={{0,2},{1,3},{2,0},{3,1},{4,7},{5,6},{6,5},{7,4},{8,10},{9,11},{10,... | collective-permute-start | bytes 688136 | tf_op jit(solution)/shard_map/ppermute | solution.py:439
  6.1 0.0 copy-done.2
  6.1 1.8 %arrange.1 = (bf16[8,8,128,256]{3,2,1,0:T(8,128)(2,1)S(1)}, bf16[2,8,128,256]{3,2,1,0:T(8,128)(2,1)S(1)}, bf16[8,128,256]{2,1,0:T(8,128)(2,1)S(1)}) custom-call(s32[8]{0:T(128)S(1)} %copy-done.2, bf16[1,128,8,8,256]{4,3,2,1,0:T(8,128)(2,1)S(1)} %copy-done, bf16[28,32,128]{2,1,0:T(8,128)(2,1)S(1)} %pack.1.after.part_a), custom_call_target="tpu_custom_call" | custom-call | flops 4096 | bytes 64 | tf_op jit(solution)/shard_map/arrange/pallas_call | solution.py:324
  7.9 1.4 %collective-permute-start.2 = (bf16[8,128,256]{2,1,0:T(8,128)(2,1)S(1)}, bf16[8,128,256]{2,1,0:T(8,128)(2,1)S(1)}, u32[]{:S(2)}, u32[]{:S(2)}) collective-permute-start(bf16[8,128,256]{2,1,0:T(8,128)(2,1)S(1)} %get-tuple-element.32), channel_id=1, source_target_pairs={{0,4},{4,0},{8,12},{12,8},{16,20},{20,16},{24,28},{28,24},{1,5},{5... | collective-permute-start | bytes 1572872 | tf_op jit(solution)/shard_map/ppermute | solution.py:414
  9.3 3.0 %collective-permute-start = (bf16[2,8,128,256]{3,2,1,0:T(8,128)(2,1)S(1)}, bf16[2,8,128,256]{3,2,1,0:T(8,128)(2,1)S(1)}, u32[]{:S(2)}, u32[]{:S(2)}) collective-permute-start(bf16[2,8,128,256]{3,2,1,0:T(8,128)(2,1)S(1)} %get-tuple-element.26), channel_id=1, source_target_pairs={{4,8},{8,4},{12,16},{16,12},{20,24},{24,20},{5,9},{9,5},{13,17},{1... | collective-permute-start | bytes 3145736 | tf_op jit(solution)/shard_map/ppermute | solution.py:441
  12.4 0.8 %fill.1 = (bf16[192,1536]{1,0:T(8,128)(2,1)S(1)}, bf16[192,1152]{1,0:T(8,128)(2,1)S(1)}, bf16[192,1152]{1,0:T(8,128)(2,1)S(1)}, f32[64,128]{1,0:T(8,128)S(1)}) custom-call(s32[8]{0:T(128)S(1)} %copy-done.2, bf16[27,32,128]{2,1,0:T(8,128)(2,1)S(1)} %copy-done.1, f32[1,32]{1,0:T(1,128)S(1)} %bitcast.2, bf16[28,32,128]{2,1,0:T(8,128)(2,1)S(1)} %pack.1.after.part_a), custom_call_target="tpu_custom_call" | custom-call | flops 4096 | bytes 64 | tf_op jit(solution)/shard_map/fill/pallas_call | solution.py:324
  13.2 0.0 collective-permute-done.1.part_b
  13.2 7.1 %first_near.1 = (bf16[6,8,64,256]{3,2,1,0:T(8,128)(2,1)S(1)}, bf16[192,1152]{1,0:T(8,128)(2,1)S(1)}, bf16[192,768]{1,0:T(8,128)(2,1)S(1)}, bf16[192,768]{1,0:T(8,128)(2,1)S(1)}, f32[64,128]{1,0:T(8,128)S(1)}) custom-call(s32[8]{0:T(128)S(1)} %copy-done.2, bf16[8,8,128,256]{3,2,1,0:T(8,128)(2,1)S(1)} %get-tuple-element.25.own, ...), custom_call_target="tpu_custom_call" | custom-call | flops 8589934592 | bytes 134217728 | tf_op jit(solution)/shard_map/first_near/pallas_call | solution.py:324
  20.3 0.0 collective-permute-done.3.part_a
  20.3 0.9 %collective-permute-start.4 = (bf16[28,32,128]{2,1,0:T(8,128)(2,1)S(1)}, bf16[28,32,128]{2,1,0:T(8,128)(2,1)S(1)}, u32[]{:S(2)}, u32[]{:S(2)}) collective-permute-start(bf16[28,32,128]{2,1,0:T(8,128)(2,1)S(1)} %collective-permute-done.3.part_a), channel_id=1, source_target_pairs={{0,4},{4,0},{8,12},{12,8},{16,20},{20,16},{24,28},{28,24},{1,5},{5... | collective-permute-start | bytes 688136 | tf_op jit(solution)/shard_map/ppermute | solution.py:414
  21.2 1.1 %collective-permute-done.4.part_b = bf16[28,32,128]{2,1,0:T(8,128)(2,1)S(1)} collective-permute-done((bf16[28,32,128]{2,1,0:T(8,128)(2,1)S(1)}, bf16[28,32,128]{2,1,0:T(8,128)(2,1)S(1)}, u32[]{:S(2)}, u32[]{:S(2)}) %collective-permute-start.4) | collective-permute-done | bytes 229408 | tf_op jit(solution)/shard_map/ppermute | solution.py:414
  22.3 0.0 collective-permute-done.2.mate
  22.3 9.2 %first_far.1 = (bf16[6,8,64,256]{3,2,1,0:T(8,128)(2,1)S(1)}, bf16[8,128,256]{2,1,0:T(8,128)(2,1)S(1)}, bf16[192,1152]{1,0:T(8,128)(2,1)S(1)}, bf16[192,768]{1,0:...) custom-call(s32[8]{0:T(128)S(1)} %copy-done.2, ...), custom_call_target="tpu_custom_call" | custom-call | flops 4096 | bytes 64 | tf_op jit(solution)/shard_map/first_far/pallas_call | solution.py:324
  31.5 0.4 collective-permute-start.5
  32.0 4.2 %second_inner.1.done_inner = bf16[5,8,32,256]{3,2,1,0:T(8,128)(2,1)S(1)} custom-call(s32[8]{0:T(128)S(1)} %copy-done.2, bf16[6,8,64,256]{3,2,1,0:T(8,128)(2,1)S(1)} %get-tuple-element.35.after.inner_a, bf16[6,8,64,256]{3,2,1,0:T(8,128)(2,1)S(1)} %get-tuple-element.40.inner_b, bf16[8,128,256]{2,1,0:T(8,128)(2,1)S(1)} %get-tuple-element.41.row_seven, ...), custom_call_target="tpu_custom_call" | custom-call | flops 4096 | bytes 64 | tf_op jit(solution)/shard_map/second_inner/pallas_call | solution.py:324
  36.1 0.3 collective-permute-done.cross
  36.4 0.0 collective-permute-done.5.mate
  36.4 8.0 %last.1 = bf16[1,32,8,8,256]{4,3,2,1,0:T(8,128)(2,1)} custom-call(s32[8]{0:T(128)S(1)} %copy-done.2, bf16[8,8,128,256]{3,2,1,0:T(8,128)(2,1)S(1)} %get-tuple-element.25.own, bf16[2,8,128,256]{3,2,1,0:T(8,128)(2,1)S(1)} %collective-permute-done.cross, bf16[192,1152]{1,0:T(8,128)(2,1)S(1)} %get-tuple-element.28.near, ...), custom_call_target="tpu_custom_call" | custom-call | flops 4096 | bytes 64 | tf_op jit(solution)/shard_map/last/pallas_call | solution.py:324
  (7 shorter events, 0.0 us)
Async XLA Ops:
  0.0 0.9 %copy-start.4 = (bf16[27,32,128]{2,1,0:T(8,128)(2,1)S(1)}, bf16[27,32,128]{2,1,0:T(8,128)(2,1)}, u32[]{:S(2)}) copy-start(bf16[27,32,128]{2,1,0:T(8,128)(2,1)} %weights.2) | copy-start | bytes 663556
  0.9 0.7 %copy-start.5 = (f32[32]{0:T(128)S(1)}, f32[32]{0:T(128)}, u32[]{:S(2)}) copy-start(f32[32]{0:T(128)} %param.9) | copy-start | bytes 388
  1.6 4.5 %copy-start = (bf16[1,128,8,8,256]{4,3,2,1,0:T(8,128)(2,1)S(1)}, bf16[1,128,8,8,256]{4,3,2,1,0:T(8,128)(2,1)}, u32[]{:S(2)}) copy-start(bf16[1,128,8,8,256]{4,3,2,1,0:T(8,128)(2,1)} %features.1) | copy-start | bytes 12582916
  1.6 4.5 %copy-start.2 = (s32[8]{0:T(128)S(1)}, s32[8]{0:T(128)}, u32[]{:S(2)}) copy-start(s32[8]{0:T(128)} %heights.11) | copy-start | bytes 100
  1.7 10.7 %copy-start.1 = (bf16[27,32,128]{2,1,0:T(8,128)(2,1)S(1)}, bf16[27,32,128]{2,1,0:T(8,128)(2,1)}, u32[]{:S(2)}) copy-start(bf16[27,32,128]{2,1,0:T(8,128)(2,1)} %weights.3) | copy-start | bytes 663556
  1.7 10.7 %copy-start.3 = (f32[32]{0:T(128)S(1)}, f32[32]{0:T(128)}, u32[]{:S(2)}) copy-start(f32[32]{0:T(128)} %param.11) | copy-start | bytes 388
  1.7 11.5 %collective-permute-start.1 = (bf16[28,32,128]{2,1,0:T(8,128)(2,1)S(1)}, bf16[28,32,128]{2,1,0:T(8,128)(2,1)S(1)}, u32[]{:S(2)}, u32[]{:S(2)}) collective-permute-start(bf16[28,32,128]{2,1,0:T(8,128)(2,1)S(1)} %pack.1.after.part_a), channel_id=1, source_target_pairs={{0,1},{1,0},{2,3},{3,2},{4,5},{5,4},{6,7},{7,6},{8,9},{9,8},{10,11... | collective-permute-start | bytes 688136 | tf_op jit(solution)/shard_map/ppermute | solution.py:438
  3.9 16.4 %collective-permute-start.3 = (bf16[28,32,128]{2,1,0:T(8,128)(2,1)S(1)}, bf16[28,32,128]{2,1,0:T(8,128)(2,1)S(1)}, u32[]{:S(2)}, u32[]{:S(2)}) collective-permute-start(bf16[28,32,128]{2,1,0:T(8,128)(2,1)S(1)} %pack.1.after.part_a), channel_id=1, source_target_pairs={{0,2},{1,3},{2,0},{3,1},{4,7},{5,6},{6,5},{7,4},{8,10},{9,11},{10,... | collective-permute-start | bytes 688136 | tf_op jit(solution)/shard_map/ppermute | solution.py:439
  7.9 14.4 %collective-permute-start.2 = (bf16[8,128,256]{2,1,0:T(8,128)(2,1)S(1)}, bf16[8,128,256]{2,1,0:T(8,128)(2,1)S(1)}, u32[]{:S(2)}, u32[]{:S(2)}) collective-permute-start(bf16[8,128,256]{2,1,0:T(8,128)(2,1)S(1)} %get-tuple-element.32), channel_id=1, source_target_pairs={{0,4},{4,0},{8,12},{12,8},{16,20},{20,16},{24,28},{28,24},{1,5},{5... | collective-permute-start | bytes 1572872 | tf_op jit(solution)/shard_map/ppermute | solution.py:414
  9.3 27.1 %collective-permute-start = (bf16[2,8,128,256]{3,2,1,0:T(8,128)(2,1)S(1)}, bf16[2,8,128,256]{3,2,1,0:T(8,128)(2,1)S(1)}, u32[]{:S(2)}, u32[]{:S(2)}) collective-permute-start(bf16[2,8,128,256]{3,2,1,0:T(8,128)(2,1)S(1)} %get-tuple-element.26), channel_id=1, source_target_pairs={{4,8},{8,4},{12,16},{16,12},{20,24},{24,20},{5,9},{9,5},{13,17},{1... | collective-permute-start | bytes 3145736 | tf_op jit(solution)/shard_map/ppermute | solution.py:441
  20.3 2.0 %collective-permute-start.4 = (bf16[28,32,128]{2,1,0:T(8,128)(2,1)S(1)}, bf16[28,32,128]{2,1,0:T(8,128)(2,1)S(1)}, u32[]{:S(2)}, u32[]{:S(2)}) collective-permute-start(bf16[28,32,128]{2,1,0:T(8,128)(2,1)S(1)} %collective-permute-done.3.part_a), channel_id=1, source_target_pairs={{0,4},{4,0},{8,12},{12,8},{16,20},{20,16},{24,28},{28,24},{1,5},{5... | collective-permute-start | bytes 688136 | tf_op jit(solution)/shard_map/ppermute | solution.py:414
  31.5 4.8 %collective-permute-start.5 = (bf16[8,128,256]{2,1,0:T(8,128)(2,1)S(1)}, bf16[8,128,256]{2,1,0:T(8,128)(2,1)S(1)}, u32[]{:S(2)}, u32[]{:S(2)}) collective-permute-start(bf16[8,128,256]{2,1,0:T(8,128)(2,1)S(1)} %get-tuple-element.41.row_seven), channel_id=1, source_target_pairs={{0,4},{4,0},{8,12},{12,8},{16,20},{20,16},{24,28},{28,24},{1,5},{5... | collective-permute-start | bytes 1572872 | tf_op jit(solution)/shard_map/ppermute | solution.py:414

commit v3 on v2

--- a/solution.py
+++ b/solution.py
@@ -49,52 +49,47 @@
     return jnp.sum(jnp.where(same, wide, 0.0), axis=1, keepdims=True)
 
 
-def pack_kernel(weights, bias, packed):
-    taps, rows, lanes = weights.shape
-    packed[:taps] = weights[...]
-    column = as_column(bias[...])
-    lane = lax.broadcasted_iota(jnp.int32, (rows, lanes), 1)
-    extra = jnp.zeros((rows, lanes), F32)
-    for at in range(3):
-        piece = column.astype(BF16).astype(F32)
-        extra = jnp.where(lane == at, piece, extra)
-        column = column - piece
-    packed[taps] = extra.astype(BF16)
-
-
-def arrange_kernel(heights, features, after, fields, cross, mate):
+def order_kernel(swap):
+    odd = lax.rem(lax.axis_index("space"), 2)
+    group = swap.shape[0] // COL_Y
+    row = lax.broadcasted_iota(jnp.int32, swap.shape, 0)
+    column = lax.broadcasted_iota(jnp.int32, swap.shape, 1)
+    u = lax.div(row, group)
+    y = jnp.where(odd == 1, COL_Y - 1 - u, u)
+    swap[...] = (column == lax.rem(row, group) * COL_Y + y).astype(F32).astype(BF16)
+
+
+def arrange_kernel(heights, features, swap, fields, cross, mate):
     _, channels, width, _, depth = features.shape
     place = Place(heights)
     group = 256 // COL_Y
-    row = lax.broadcasted_iota(jnp.int32, (256, 256), 0)
-    column = lax.broadcasted_iota(jnp.int32, (256, 256), 1)
-    u = lax.div(row, group)
-    y = jnp.where(place.odd == 1, COL_Y - 1 - u, u)
-    swap = (column == lax.rem(row, group) * COL_Y + y).astype(F32).astype(BF16)
     live = lax.broadcasted_iota(jnp.int32, (1, depth), 1) < place.top()
     for x in range(width):
         for first in range(0, channels, group):
             tile = features[0, first : first + group, x].reshape(256, depth)
-            moved = jnp.dot(swap, tile, preferred_element_type=F32)
+            moved = jnp.dot(swap[...], tile, preferred_element_type=F32)
             moved = jnp.where(live, moved, 0.0).astype(BF16).reshape(COL_Y, group, depth)
             fields[:, x, first : first + group] = moved
             cross[:, x, first : first + group] = moved[:2]
             mate[x, first : first + group] = moved[COL_Y - 1]
 
 
-def finish(partial, bias, live_top):
-    rows, depth = partial.shape[0] // TAPS, partial.shape[1]
-    z = lax.broadcasted_iota(jnp.int32, (rows, depth), 1)
+def finish(partial, bias, live_top, columns=1):
+    rows, lanes = partial.shape[0] // TAPS, partial.shape[1]
+    depth = lanes // columns
+    z = lax.broadcasted_iota(jnp.int32, (rows, lanes), 1)
+    if columns > 1:
+        z = lax.rem(z, depth)
     below = jnp.where(z == 0, 0.0, pltpu.roll(partial[:rows], 1, 1))
-    above = jnp.where(z == depth - 1, 0.0, pltpu.roll(partial[2 * rows :], depth - 1, 1))
+    above = jnp.where(z == depth - 1, 0.0, pltpu.roll(partial[2 * rows :], lanes - 1, 1))
     total = jnp.maximum(below + partial[rows : 2 * rows] + above + bias, 0.0)
     return jnp.where(z < live_top, total, 0.0).astype(BF16)
 
 
-def fill_first(parts, slots, odd, matrix, low_matrix, high_matrix, bias):
+def fill_first(parts, biases, slots, odd, matrix, low_matrix, high_matrix, bias):
     quarter, channels = parts[0].shape[1], parts[0].shape[2]
     block = quarter * len(parts)
-    for part, slot in zip(parts, slots, strict=True):
+    for part, given, slot in zip(parts, biases, slots, strict=True):
         at = slot * quarter
         for k in range(TAPS):
             span = pl.ds(pl.multiple_of(k * block + at, quarter), quarter)
@@ -107,8 +102,7 @@
                         low_matrix[span, pl.ds((j * 2 + i - 1) * channels, channels)] = tile
                     if i < 2:
                         high_matrix[span, pl.ds((j * 2 + i) * channels, channels)] = tile
-        extra = part[27].astype(F32)
-        value = extra[:, 0:1] + extra[:, 1:2] + extra[:, 2:3]
+        value = as_column(given[...])
         bias[pl.ds(pl.multiple_of(at, quarter), quarter), :] = jnp.broadcast_to(value, (quarter, bias.shape[1]))
 
 
@@ -128,6 +122,25 @@
         yield x + halo, finish(partial, bias[:, 0:1], top(side))
 
 
+def first_row_low(get, stored, halo, matrices, bias, top, levels):
+    channels = matrices[0].shape[1] // TAPS**2
+
+    def field(j, x):
+        return get(j, x, x + 1)[:, :levels] if 0 <= x < stored else jnp.zeros((channels, levels), BF16)
+
+    for x in range(-halo, COL_Y + halo, 2):
+        at = x + 2 * halo
+        taken = [
+            jnp.concatenate([field(j, at + more + i - 1) for j in range(TAPS) for i in range(TAPS)], axis=0) for more in range(2)
+        ]
+        partial = jnp.dot(matrices[0][...], jnp.concatenate(taken, axis=1), preferred_element_type=F32)
+        sides = [-1 if each < 0 else 1 if each >= COL_Y else 0 for each in (x, x + 1)]
+        tops = jnp.where(lax.broadcasted_iota(jnp.int32, (1, 2 * levels), 1) < levels, top(sides[0]), top(sides[1]))
+        done = finish(partial, bias[:, 0:1], tops, columns=2)
+        yield x + halo, done[:, :levels]
+        yield x + halo + 1, done[:, levels:]
+
+
 def span_of(ref, *at):
     *lead, low, high = at
     value = ref[(*lead, slice(low, high))]
@@ -145,18 +158,18 @@
     lax.fori_loop(0, (COL_Y - 2) // 2, pair, 0)
 
 
-def first_near_kernel(halo, heights, own, part_a, part_b, after, out, matrix, low_matrix, high_matrix, bias):
+def first_near_kernel(halo, heights, own, part_a, part_b, bias_a, bias_b, bias_c, bias_d, out, matrix, low_matrix, high_matrix, bias):
     place = Place(heights)
-    fill_first([part_a, part_b], place.slots[:2], place.odd, matrix, low_matrix, high_matrix, bias)
+    fill_first([part_a, part_b], [bias_a, bias_b], place.slots[:2], place.odd, matrix, low_matrix, high_matrix, bias)
     inner_rows(own, out, halo, (matrix, low_matrix, high_matrix), bias, place.top)
 
 
 def first_far_kernel(
-    halo, heights, own, mate, part_a, part_b, near, low_near, high_near, bias_near, after,
+    halo, heights, own, mate, part_a, part_b, bias_a, bias_b, near, low_near, high_near, bias_near, after,
     out, out_last, matrix, low_matrix, high_matrix, bias,
 ):
     place = Place(heights)
-    fill_first([part_a, part_b], place.slots[2:], place.odd, matrix, low_matrix, high_matrix, bias)
+    fill_first([part_a, part_b], [bias_a, bias_b], place.slots[2:], place.odd, matrix, low_matrix, high_matrix, bias)
     far = (matrix, low_matrix, high_matrix)
     inner_rows(own, out, halo, far, bias, place.top)
 
@@ -166,13 +179,15 @@
     whole_row(get, own.shape[1], halo, ((near, low_near, high_near), bias_near), (far, bias), place.top, out_last)
 
 
-def whole_row(get, stored, halo, near, far, top, out, *at):
+def whole_row(get, stored, halo, near, far, top, out, *at, levels=None):
     half = near[1].shape[0]
-    levels = None
     for first, (matrices, bias) in ((0, near), (half, far)):
-        for x, done in first_row(get, stored, halo, matrices, bias, top):
-            levels = done.shape[1]
-            out[(*at, x, slice(first, first + half), slice(0, levels))] = done
+        if levels is None:
+            for x, done in first_row(get, stored, halo, matrices, bias, top):
+                out[(*at, x, slice(first, first + half))] = done
+        else:
+            for x, done in first_row_low(get, stored, halo, matrices, bias, top, levels):
+                out[(*at, x, slice(first, first + half), slice(0, levels))] = done
 
 
 def fill_second(weights, place, matrix, low_matrix, high_matrix):
@@ -249,7 +264,7 @@
 
 def last_kernel(
     halo, heights, own, cross, near, low_near, high_near, bias_near, far, low_far, high_far, bias_far,
-    inner_a, inner_b, row_seven, mate, done_inner, matrix_two, low_two, high_two, both, out, edge, done_edge,
+    inner_a, inner_b, row_seven, mate, done_inner, matrix_two, low_two, high_two, both, out, edge, done_edge, result, sems,
 ):
     place = Place(heights)
     width, depth = own.shape[1], own.shape[3]
@@ -258,32 +273,29 @@
     def fields(u, a, b):
         return span_of(own, u, a, b) if u >= 0 else span_of(cross, -1 - u, a, b)
 
-    def edge_row(u, levels):
+    def edge_row(u, levels=None):
         def top(side):
             return place.top(side, across=u < 0)
 
-        def get(j, a, b):
-            return fields(u - 1 + j, a, b)[:, :levels]
-
-        whole_row(get, width, halo, near, far, top, edge, u + 1)
-        if levels < depth:
-            edge[u + 1, :, :, levels:] = jnp.zeros((*edge.shape[1:3], depth - levels), BF16)
-
-    part = depth // 2 if depth % 256 == 0 else depth
-    highest = place.top(0, across=True)
+        whole_row(lambda j, a, b: fields(u - 1 + j, a, b), width, halo, near, far, top, edge, u + 1, levels=levels)
+
+    part = 128
+    needed = jnp.minimum(place.top(0, across=True), place.top() + 1)
     if halo:
-        highest = jnp.maximum(highest, jnp.maximum(place.top(-1, across=True), place.top(1, across=True)))
-    low = highest < part
+        wide = jnp.maximum(place.top(-1, across=True), place.top(1, across=True))
+        needed = jnp.maximum(needed, jnp.minimum(wide, place.top() + 1))
+    low = needed < part if depth > part else False
 
     @pl.when(low)
     def _():
         edge_row(-1, part)
+        edge[0, :, :, part:] = jnp.zeros((*edge.shape[1:3], depth - part), BF16)
 
     @pl.when(jnp.logical_not(low))
     def _():
-        edge_row(-1, depth)
-
-    edge_row(0, depth)
+        edge_row(-1)
+
+    edge_row(0)
 
     def row(u, a, b):
         if u < 1:
@@ -314,18 +326,21 @@
         tiles = [done_edge[0, x], done_edge[1, x]] + [done_inner[v, x] for v in range(COL_Y - 3)] + [done_edge[2, x]]
         tile = jnp.concatenate(tiles, axis=0)
         moved = jnp.dot(swap, tile, preferred_element_type=F32).astype(BF16)
-        out[0, :, x] = moved.reshape(quarter, COL_Y, depth)
+        result[x] = moved.reshape(quarter, COL_Y, depth)
+        pltpu.make_async_copy(result.at[x], out.at[0, :, x], sems.at[x]).start()
+    for x in range(COL_Y):
+        pltpu.make_async_copy(result.at[x], out.at[0, :, x], sems.at[x]).wait()
 
 
 SHORT, LONG = 2**6, 2**27
 
 
-def call(kernel, name, inputs, outputs, scratch, nbytes, *args, kinds=None):
+def call(kernel, name, inputs, outputs, scratch, nbytes, *args, kinds=None, place=WHOLE):
     return pl.pallas_call(
         kernel,
         out_shape=[jax.ShapeDtypeStruct(*each) for each in zip(outputs, kinds or [BF16] * len(outputs))],
         in_specs=inputs,
-        out_specs=[WHOLE] * len(outputs),
+        out_specs=[place] * len(outputs),
         scratch_shapes=scratch,
         compiler_params=pltpu.CompilerParams(vmem_limit_bytes=16 * 2**20),
         cost_estimate=pl.CostEstimate(flops=64 * nbytes, bytes_accessed=nbytes, transcendentals=0),
@@ -333,16 +348,12 @@
     )(*args)
 
 
-def pack(weights, bias):
-    taps, rows, lanes = weights.shape
-    return call(pack_kernel, "pack", [WHOLE, WHOLE], [(taps + 1, rows, lanes)], [], LONG, weights, bias[None])[0]
-
-
-def arrange(heights, features, after):
+def arrange(heights, features):
     _, channels, width, _, depth = features.shape
     row = (width, channels, depth)
     outputs = [(COL_Y, *row), (2, *row), row]
-    return call(arrange_kernel, "arrange", [SCALARS, WHOLE, ANY], outputs, [], SHORT, heights, features, after)
+    swap = call(order_kernel, "order", [], [(256, 256)], [], LONG)[0]
+    return call(arrange_kernel, "arrange", [SCALARS, WHOLE, WHOLE], outputs, [], SHORT, heights, features, swap)
 
 
 def first_matrices(channels, rows):
@@ -359,25 +370,25 @@
     return call(fill_kernel, "fill", [SCALARS, WHOLE, WHOLE, ANY], outputs, [], SHORT, heights, weights, bias[None], after, kinds=kinds)
 
 
-def first_near(halo, heights, own, part_a, part_b, after):
+def first_near(halo, heights, own, part_a, part_b, biases):
     _, _, channels, depth = own.shape
     half, width = 2 * part_a.shape[1], COL_Y + 2 * halo
     shapes, kinds = first_matrices(channels, half)
     inner, *matrices = call(
-        functools.partial(first_near_kernel, halo), "first_near", [SCALARS] + [WHOLE] * 3 + [ANY],
-        [(COL_Y - 2, width, half, depth), *shapes], [], LONG, heights, own, part_a, part_b, after, kinds=[BF16, *kinds],
+        functools.partial(first_near_kernel, halo), "first_near", [SCALARS] + [WHOLE] * 7,
+        [(COL_Y - 2, width, half, depth), *shapes], [], LONG, heights, own, part_a, part_b, *biases, kinds=[BF16, *kinds],
     )
     return inner, matrices
 
 
-def first_far(halo, heights, own, mate, part_a, part_b, near, after):
+def first_far(halo, heights, own, mate, part_a, part_b, bias_a, bias_b, near, after):
     _, _, channels, depth = own.shape
     half, width = 2 * part_a.shape[1], COL_Y + 2 * halo
     shapes, kinds = first_matrices(channels, half)
     inner, row_seven, *matrices = call(
-        functools.partial(first_far_kernel, halo), "first_far", [SCALARS] + [WHOLE] * 8 + [ANY],
+        functools.partial(first_far_kernel, halo), "first_far", [SCALARS] + [WHOLE] * 10 + [ANY],
         [(COL_Y - 2, width, half, depth), (width, channels, depth), *shapes], [], SHORT,
-        heights, own, mate, part_a, part_b, *near, after, kinds=[BF16, BF16, *kinds],
+        heights, own, mate, part_a, part_b, bias_a, bias_b, *near, after, kinds=[BF16, BF16, *kinds],
     )
     return inner, row_seven, matrices
 
@@ -395,10 +406,11 @@
     _, _, channels, depth = own.shape
     quarter, width = matrices[-1].shape[0] // 2, COL_Y + 2 * halo
     scratch = [pltpu.VMEM((2, width, channels, depth), BF16), pltpu.VMEM((3, COL_Y, quarter, depth), BF16)]
+    scratch += [pltpu.VMEM((COL_Y, quarter, COL_Y, depth), BF16), pltpu.SemaphoreType.DMA((COL_Y,))]
     outputs = [(1, quarter, COL_Y, COL_Y, depth)]
     args = (heights, own, cross, *near, *far, *hidden, done_inner, *matrices)
     kernel = functools.partial(last_kernel, halo)
-    return call(kernel, "last", [SCALARS] + [WHOLE] * (len(args) - 1), outputs, scratch, SHORT, *args)[0]
+    return call(kernel, "last", [SCALARS] + [WHOLE] * (len(args) - 1), outputs, scratch, SHORT, *args, place=ANY)[0]
 
 
 def across_pairs(peers):
@@ -414,12 +426,8 @@
     return lax.ppermute(value, "space", [(i, i ^ 1) for i in range(lax.axis_size("space"))])
 
 
-def far_pairs(peers, chans):
-    pairs = []
-    for i in range(peers):
-        for c in range(chans):
-            pairs.append((i * chans + c, i * chans + (c ^ (3 if i % 2 else 2))))
-    return pairs
+def far_pairs(peers, chans, even, odd):
+    return [(i * chans + c, i * chans + (c ^ (odd if i % 2 else even))) for i in range(peers) for c in range(chans)]
 
 
 def with_x_borders(rows, peers):
@@ -434,21 +442,27 @@
     peers, chans = lax.axis_size("space"), lax.axis_size("chan")
     halo = 1 if peers > COL_Y else 0
 
-    own_part = pack(weight_one, bias_one)
-    near_part = lax.ppermute(own_part, "chan", [(c, c ^ 1) for c in range(chans)])
-    far_part = lax.ppermute(own_part, ("space", "chan"), far_pairs(peers, chans))
-    fields, cross, mate = arrange(column_heights, features, own_part)
+    near_pairs, distant_pairs = [(c, c ^ 1) for c in range(chans)], far_pairs(peers, chans, 2, 3)
+    near_part = lax.ppermute(weight_one, "chan", near_pairs)
+    far_part = lax.ppermute(weight_one, ("space", "chan"), distant_pairs)
+    own_bias = bias_one[None]
+    near_bias = lax.ppermute(own_bias, "chan", near_pairs)
+    far_bias = lax.ppermute(own_bias, ("space", "chan"), distant_pairs)
+    other_bias = lax.ppermute(own_bias, ("space", "chan"), far_pairs(peers, chans, 3, 2))
+    fields, cross, mate = arrange(column_heights, features)
     cross = lax.ppermute(cross, "space", across_pairs(peers))
     mate = to_mate(mate)
     if halo:
         fields = with_x_borders(jnp.concatenate([cross, fields, mate[None]], axis=0), peers)
         cross, fields, mate = fields[:2], fields[2:-1], fields[-1]
 
-    matrices = fill(column_heights, weight_two, bias_two, own_part)
-    inner_a, near = first_near(halo, column_heights, fields, own_part, near_part, matrices[-1])
+    inner_a, near = first_near(halo, column_heights, fields, weight_one, near_part, (own_bias, near_bias, far_bias, other_bias))
     far_part, inner_a = lax.optimization_barrier((far_part, inner_a))
     other_part = to_mate(far_part)
-    inner_b, row_seven, far = first_far(halo, column_heights, fields, mate, far_part, other_part, near, inner_a)
+    matrices = fill(column_heights, weight_two, bias_two, inner_a)
+    inner_b, row_seven, far = first_far(
+        halo, column_heights, fields, mate, far_part, other_part, far_bias, other_bias, near, matrices[-1]
+    )
     mate = to_mate(row_seven)
     done_inner = second_inner(halo, column_heights, inner_a, inner_b, row_seven, matrices)
     hidden = (inner_a, inner_b, row_seven, mate)

time: 44.6 us -> 47.4 us (1.063)
  starting transfers between devices: 10.1 us -> 15.4 us
  local copies, waits for them, and re-layouts: 1.61 us -> 0.03 us
  waiting for transfers between devices: 1.39 us -> 0.3 us
  Pallas kernels: 31.2 us -> 30.7 us
    ppermute x2 -> x5, starting transfers between devices: 4.39 us -> 7.87 us  [the longest x1 3.14 us: on_device(): lax.ppermute(own_bias, ('space', 'chan'), far_pairs(peers, chans, 3, 2))]
    ppermute x3, starting transfers between devices: 2.7 us -> 4.51 us  [to_mate(): lax.ppermute(value, 'space', [(i, i ^ 1) for i in range(lax.axis_size('sp...]
    unnamed x12, local copies, waits for them, and re-layouts: 1.61 us -> 0.03 us
    ppermute x3, waiting for transfers between devices: 1.12 us -> 0.29 us  [to_mate(): lax.ppermute(value, 'space', [(i, i ^ 1) for i in range(lax.axis_size('sp...]
  transfers between devices with their start and end apart: 6 -> 9, of which waited for: 2 -> 1; matrix products, arithmetic and copies ran while one was open for 0% -> 0% of each run, Pallas kernels for 52% -> 51%
where the time goes in v3:
time: 47.4 us; the launch traced here: 46.8 us
  Pallas kernels  30.7 us (65%)
  starting transfers between devices  15.4 us (32%)
    pallas_call x7, Pallas kernels, call(): pl.pallas_call(kernel, out_shape=[jax.ShapeDtypeStruct(*each) for each in...  30.7 us
    ppermute x3, starting transfers between devices, to_mate(): lax.ppermute(value, 'space', [(i, i ^ 1) for i in range(lax.axis_size('sp...  4.51 us
    ppermute x1, starting transfers between devices, on_device(): lax.ppermute(own_bias, ('space', 'chan'), far_pairs(peers, chans, 3, 2))  3.14 us
    ppermute x1, starting transfers between devices, on_device(): cross = lax.ppermute(cross, 'space', across_pairs(peers))  3.02 us
    ppermute x1, starting transfers between devices, on_device(): far_part = lax.ppermute(weight_one, ('space', 'chan'), distant_pairs)  2.18 us
    ppermute x1, starting transfers between devices, on_device(): near_part = lax.ppermute(weight_one, 'chan', near_pairs)  1.26 us
    ppermute x1, starting transfers between devices, on_device(): far_bias = lax.ppermute(own_bias, ('space', 'chan'), distant_pairs)  1.09 us
  transfers between devices with their start and end apart: 9, of which 1 were waited for; matrix products, arithmetic and copies ran while one was open for 0% of the time, Pallas kernels for 51%

profile of v3, /device:TPU:1, one launch (start us, length us, event | category | flops | bytes accessed | tf_op | source)
XLA Modules:
  0.0 46.8 jit_solution(402506357702482641)
XLA Ops:
  0.0 3.1 %collective-permute-start.4 = (f32[1,32]{1,0:T(1,128)}, f32[1,32]{1,0:T(1,128)S(1)}, u32[]{:S(2)}, u32[]{:S(2)}) collective-permute-start(f32[1,32]{1,0:T(1,128)} %bitcast.3), channel_id=1, source_target_pairs={{0,3},{1,2},{2,1},{3,0},{4,6},{5,7},{6,4},{7,5},{8,11},{9,10},{10,... | collective-permute-start | bytes 392 | tf_op jit(solution)/shard_map/ppermute | solution.py:451
  3.1 1.1 %collective-permute-start.3 = (f32[1,32]{1,0:T(1,128)}, f32[1,32]{1,0:T(1,128)S(1)}, u32[]{:S(2)}, u32[]{:S(2)}) collective-permute-start(f32[1,32]{1,0:T(1,128)} %bitcast.4), channel_id=1, source_target_pairs={{0,2},{1,3},{2,0},{3,1},{4,7},{5,6},{6,5},{7,4},{8,10},{9,11},{10,... | collective-permute-start | bytes 392 | tf_op jit(solution)/shard_map/ppermute | solution.py:450
  4.2 0.2 collective-permute-start.2
  4.4 1.3 %collective-permute-start.1 = (bf16[27,32,128]{2,1,0:T(8,128)(2,1)}, bf16[27,32,128]{2,1,0:T(8,128)(2,1)S(1)}, u32[]{:S(2)}, u32[]{:S(2)}) collective-permute-start(bf16[27,32,128]{2,1,0:T(8,128)(2,1)} %part_a.1), channel_id=1, source_target_pairs={{0,1},{1,0},{2,3},{3,2},{4,5},{5,4},{6,7},{7,6},{8,9},{9,8},{10,11... | collective-permute-start | bytes 663560 | tf_op jit(solution)/shard_map/ppermute | solution.py:446
  5.7 2.2 %collective-permute-start.6 = (bf16[27,32,128]{2,1,0:T(8,128)(2,1)}, bf16[27,32,128]{2,1,0:T(8,128)(2,1)S(1)}, u32[]{:S(2)}, u32[]{:S(2)}) collective-permute-start(bf16[27,32,128]{2,1,0:T(8,128)(2,1)} %part_a.1), channel_id=1, source_target_pairs={{0,2},{1,3},{2,0},{3,1},{4,7},{5,6},{6,5},{7,4},{8,10},{9,11},{10,... | collective-permute-start | bytes 663560 | tf_op jit(solution)/shard_map/ppermute | solution.py:447
  7.9 0.1 order.1.swap
  8.0 0.0 copy-start.4
  8.0 0.0 copy-start.5
  8.0 1.8 %arrange.1 = (bf16[8,8,128,256]{3,2,1,0:T(8,128)(2,1)S(1)}, bf16[2,8,128,256]{3,2,1,0:T(8,128)(2,1)S(1)}, bf16[8,128,256]{2,1,0:T(8,128)(2,1)S(1)}) custom-call(s32[8]{0:T(128)S(1)} %copy-done.2, bf16[1,128,8,8,256]{4,3,2,1,0:T(8,128)(2,1)S(1)} %copy-done, bf16[256,256]{1,0:T(8,128)(2,1)S(1)} %order.1.swap), custom_call_target="tpu_custom_call" | custom-call | flops 4096 | bytes 64 | tf_op jit(solution)/shard_map/arrange/pallas_call | solution.py:339
  9.8 2.3 %collective-permute-start.5 = (bf16[8,128,256]{2,1,0:T(8,128)(2,1)S(1)}, bf16[8,128,256]{2,1,0:T(8,128)(2,1)S(1)}, u32[]{:S(2)}, u32[]{:S(2)}) collective-permute-start(bf16[8,128,256]{2,1,0:T(8,128)(2,1)S(1)} %get-tuple-element.31), channel_id=1, source_target_pairs={{0,4},{4,0},{8,12},{12,8},{16,20},{20,16},{24,28},{28,24},{1,5},{5... | collective-permute-start | bytes 1572872 | tf_op jit(solution)/shard_map/ppermute | solution.py:426
  12.1 3.0 %collective-permute-start = (bf16[2,8,128,256]{3,2,1,0:T(8,128)(2,1)S(1)}, bf16[2,8,128,256]{3,2,1,0:T(8,128)(2,1)S(1)}, u32[]{:S(2)}, u32[]{:S(2)}) collective-permute-start(bf16[2,8,128,256]{3,2,1,0:T(8,128)(2,1)S(1)} %get-tuple-element.26), channel_id=1, source_target_pairs={{4,8},{8,4},{12,16},{16,12},{20,24},{24,20},{5,9},{9,5},{13,17},{1... | collective-permute-start | bytes 3145736 | tf_op jit(solution)/shard_map/ppermute | solution.py:453
  15.2 0.0 copy-start.1
  15.2 0.0 copy-start.3
  15.2 7.5 %first_near.1 = (bf16[6,8,64,256]{3,2,1,0:T(8,128)(2,1)S(1)}, bf16[192,1152]{1,0:T(8,128)(2,1)S(1)}, bf16[192,768]{1,0:T(8,128)(2,1)S(1)}, bf16[192,768]{1,0:T(8,128)(2,1)S(1)}, f32[64,128]{1,0:T(8,128)S(1)}) custom-call(s32[8]{0:T(128)S(1)} %copy-done.2, bf16[8,8,128,256]{3,2,1,0:T(8,128)(2,1)S(1)} %get-tuple-element.25.own, ...), custom_call_target="tpu_custom_call" | custom-call | flops 8589934592 | bytes 134217728 | tf_op jit(solution)/shard_map/first_near/pallas_call | solution.py:339
  22.7 0.0 collective-permute-done.6.part_a
  22.7 1.8 %collective-permute-start.7 = (bf16[27,32,128]{2,1,0:T(8,128)(2,1)S(1)}, bf16[27,32,128]{2,1,0:T(8,128)(2,1)S(1)}, u32[]{:S(2)}, u32[]{:S(2)}) collective-permute-start(bf16[27,32,128]{2,1,0:T(8,128)(2,1)S(1)} %collective-permute-done.6.part_a), channel_id=1, source_target_pairs={{0,4},{4,0},{8,12},{12,8},{16,20},{20,16},{24,28},{28,24},{1,5},{5... | collective-permute-start | bytes 663560 | tf_op jit(solution)/shard_map/ppermute | solution.py:426
  24.5 0.8 %fill.1 = (bf16[192,1536]{1,0:T(8,128)(2,1)S(1)}, bf16[192,1152]{1,0:T(8,128)(2,1)S(1)}, bf16[192,1152]{1,0:T(8,128)(2,1)S(1)}, f32[64,128]{1,0:T(8,128)S(1)}) custom-call(s32[8]{0:T(128)S(1)} %copy-done.2, bf16[27,32,128]{2,1,0:T(8,128)(2,1)S(1)} %copy-done.1, f32[1,32]{1,0:T(1,128)S(1)} %bitcast.2, bf16[6,8,64,256]{3,2,1,0:T(8,128)(2,1)S(1)} %get-tuple-element.34.after.inner_a), custom_call_target="tpu_custom_call" | custom-call | flops 4096 | bytes 64 | tf_op jit(solution)/shard_map/fill/pallas_call | solution.py:339
  25.3 0.3 collective-permute-done.7.part_b
  25.6 0.0 collective-permute-done.5.mate
  25.6 9.2 %first_far.1 = (bf16[6,8,64,256]{3,2,1,0:T(8,128)(2,1)S(1)}, bf16[8,128,256]{2,1,0:T(8,128)(2,1)S(1)}, bf16[192,1152]{1,0:T(8,128)(2,1)S(1)}, bf16[192,768]{1,0:...) custom-call(s32[8]{0:T(128)S(1)} %copy-done.2, ...), custom_call_target="tpu_custom_call" | custom-call | flops 4096 | bytes 64 | tf_op jit(solution)/shard_map/first_far/pallas_call | solution.py:339
  34.9 0.5 collective-permute-start.8
  35.3 4.2 %second_inner.1.done_inner = bf16[5,8,32,256]{3,2,1,0:T(8,128)(2,1)S(1)} custom-call(s32[8]{0:T(128)S(1)} %copy-done.2, bf16[6,8,64,256]{3,2,1,0:T(8,128)(2,1)S(1)} %get-tuple-element.34.after.inner_a, bf16[6,8,64,256]{3,2,1,0:T(8,128)(2,1)S(1)} %get-tuple-element.40.inner_b, bf16[8,128,256]{2,1,0:T(8,128)(2,1)S(1)} %get-tuple-element.41.row_seven, ...), custom_call_target="tpu_custom_call" | custom-call | flops 4096 | bytes 64 | tf_op jit(solution)/shard_map/second_inner/pallas_call | solution.py:339
  39.5 0.0 collective-permute-done.cross
  39.6 7.1 %last.1 = bf16[1,32,8,8,256]{4,3,2,1,0:T(8,128)(2,1)} custom-call(s32[8]{0:T(128)S(1)} %copy-done.2, bf16[8,8,128,256]{3,2,1,0:T(8,128)(2,1)S(1)} %get-tuple-element.25.own, bf16[2,8,128,256]{3,2,1,0:T(8,128)(2,1)S(1)} %collective-permute-done.cross, bf16[192,1152]{1,0:T(8,128)(2,1)S(1)} %get-tuple-element.27.near, ...), custom_call_target="tpu_custom_call" | custom-call | flops 4096 | bytes 64 | tf_op jit(solution)/shard_map/last/pallas_call | solution.py:339
  (13 shorter events, 0.0 us)
Async XLA Ops:
  0.0 7.9 %copy-start = (bf16[1,128,8,8,256]{4,3,2,1,0:T(8,128)(2,1)S(1)}, bf16[1,128,8,8,256]{4,3,2,1,0:T(8,128)(2,1)}, u32[]{:S(2)}) copy-start(bf16[1,128,8,8,256]{4,3,2,1,0:T(8,128)(2,1)} %features.1) | copy-start | bytes 12582916
  0.0 8.0 %copy-start.2 = (s32[8]{0:T(128)S(1)}, s32[8]{0:T(128)}, u32[]{:S(2)}) copy-start(s32[8]{0:T(128)} %heights.11) | copy-start | bytes 100
  0.0 9.8 %collective-permute-start.4 = (f32[1,32]{1,0:T(1,128)}, f32[1,32]{1,0:T(1,128)S(1)}, u32[]{:S(2)}, u32[]{:S(2)}) collective-permute-start(f32[1,32]{1,0:T(1,128)} %bitcast.3), channel_id=1, source_target_pairs={{0,3},{1,2},{2,1},{3,0},{4,6},{5,7},{6,4},{7,5},{8,11},{9,10},{10,... | collective-permute-start | bytes 392 | tf_op jit(solution)/shard_map/ppermute | solution.py:451
  3.1 9.0 %collective-permute-start.3 = (f32[1,32]{1,0:T(1,128)}, f32[1,32]{1,0:T(1,128)S(1)}, u32[]{:S(2)}, u32[]{:S(2)}) collective-permute-start(f32[1,32]{1,0:T(1,128)} %bitcast.4), channel_id=1, source_target_pairs={{0,2},{1,3},{2,0},{3,1},{4,7},{5,6},{6,5},{7,4},{8,10},{9,11},{10,... | collective-permute-start | bytes 392 | tf_op jit(solution)/shard_map/ppermute | solution.py:450
  4.2 10.9 %collective-permute-start.2 = (f32[1,32]{1,0:T(1,128)}, f32[1,32]{1,0:T(1,128)S(1)}, u32[]{:S(2)}, u32[]{:S(2)}) collective-permute-start(f32[1,32]{1,0:T(1,128)} %bitcast.5), channel_id=1, source_target_pairs={{0,1},{1,0},{2,3},{3,2},{4,5},{5,4},{6,7},{7,6},{8,9},{9,8},{10,11... | collective-permute-start | bytes 392 | tf_op jit(solution)/shard_map/ppermute | solution.py:449
  4.4 10.7 %collective-permute-start.1 = (bf16[27,32,128]{2,1,0:T(8,128)(2,1)}, bf16[27,32,128]{2,1,0:T(8,128)(2,1)S(1)}, u32[]{:S(2)}, u32[]{:S(2)}) collective-permute-start(bf16[27,32,128]{2,1,0:T(8,128)(2,1)} %part_a.1), channel_id=1, source_target_pairs={{0,1},{1,0},{2,3},{3,2},{4,5},{5,4},{6,7},{7,6},{8,9},{9,8},{10,11... | collective-permute-start | bytes 663560 | tf_op jit(solution)/shard_map/ppermute | solution.py:446
  5.7 17.0 %collective-permute-start.6 = (bf16[27,32,128]{2,1,0:T(8,128)(2,1)}, bf16[27,32,128]{2,1,0:T(8,128)(2,1)S(1)}, u32[]{:S(2)}, u32[]{:S(2)}) collective-permute-start(bf16[27,32,128]{2,1,0:T(8,128)(2,1)} %part_a.1), channel_id=1, source_target_pairs={{0,2},{1,3},{2,0},{3,1},{4,7},{5,6},{6,5},{7,4},{8,10},{9,11},{10,... | collective-permute-start | bytes 663560 | tf_op jit(solution)/shard_map/ppermute | solution.py:447
  8.0 7.2 %copy-start.4 = (bf16[27,32,128]{2,1,0:T(8,128)(2,1)S(1)}, bf16[27,32,128]{2,1,0:T(8,128)(2,1)}, u32[]{:S(2)}) copy-start(bf16[27,32,128]{2,1,0:T(8,128)(2,1)} %part_a.1) | copy-start | bytes 663556
  8.0 7.2 %copy-start.5 = (f32[32]{0:T(128)S(1)}, f32[32]{0:T(128)}, u32[]{:S(2)}) copy-start(f32[32]{0:T(128)} %param.9) | copy-start | bytes 388
  9.8 15.8 %collective-permute-start.5 = (bf16[8,128,256]{2,1,0:T(8,128)(2,1)S(1)}, bf16[8,128,256]{2,1,0:T(8,128)(2,1)S(1)}, u32[]{:S(2)}, u32[]{:S(2)}) collective-permute-start(bf16[8,128,256]{2,1,0:T(8,128)(2,1)S(1)} %get-tuple-element.31), channel_id=1, source_target_pairs={{0,4},{4,0},{8,12},{12,8},{16,20},{20,16},{24,28},{28,24},{1,5},{5... | collective-permute-start | bytes 1572872 | tf_op jit(solution)/shard_map/ppermute | solution.py:426
  12.1 27.5 %collective-permute-start = (bf16[2,8,128,256]{3,2,1,0:T(8,128)(2,1)S(1)}, bf16[2,8,128,256]{3,2,1,0:T(8,128)(2,1)S(1)}, u32[]{:S(2)}, u32[]{:S(2)}) collective-permute-start(bf16[2,8,128,256]{3,2,1,0:T(8,128)(2,1)S(1)} %get-tuple-element.26), channel_id=1, source_target_pairs={{4,8},{8,4},{12,16},{16,12},{20,24},{24,20},{5,9},{9,5},{13,17},{1... | collective-permute-start | bytes 3145736 | tf_op jit(solution)/shard_map/ppermute | solution.py:453
  15.2 9.3 %copy-start.1 = (bf16[27,32,128]{2,1,0:T(8,128)(2,1)S(1)}, bf16[27,32,128]{2,1,0:T(8,128)(2,1)}, u32[]{:S(2)}) copy-start(bf16[27,32,128]{2,1,0:T(8,128)(2,1)} %weights.1) | copy-start | bytes 663556
  15.2 9.3 %copy-start.3 = (f32[32]{0:T(128)S(1)}, f32[32]{0:T(128)}, u32[]{:S(2)}) copy-start(f32[32]{0:T(128)} %param.11) | copy-start | bytes 388
  22.7 2.9 %collective-permute-start.7 = (bf16[27,32,128]{2,1,0:T(8,128)(2,1)S(1)}, bf16[27,32,128]{2,1,0:T(8,128)(2,1)S(1)}, u32[]{:S(2)}, u32[]{:S(2)}) collective-permute-start(bf16[27,32,128]{2,1,0:T(8,128)(2,1)S(1)} %collective-permute-done.6.part_a), channel_id=1, source_target_pairs={{0,4},{4,0},{8,12},{12,8},{16,20},{20,16},{24,28},{28,24},{1,5},{5... | collective-permute-start | bytes 663560 | tf_op jit(solution)/shard_map/ppermute | solution.py:426
  34.9 4.7 %collective-permute-start.8 = (bf16[8,128,256]{2,1,0:T(8,128)(2,1)S(1)}, bf16[8,128,256]{2,1,0:T(8,128)(2,1)S(1)}, u32[]{:S(2)}, u32[]{:S(2)}) collective-permute-start(bf16[8,128,256]{2,1,0:T(8,128)(2,1)S(1)} %get-tuple-element.41.row_seven), channel_id=1, source_target_pairs={{0,4},{4,0},{8,12},{12,8},{16,20},{20,16},{24,28},{28,24},{1,5},{5... | collective-permute-start | bytes 1572872 | tf_op jit(solution)/shard_map/ppermute | solution.py:426

commit v4 on v3

--- a/solution.py
+++ b/solution.py
@@ -59,7 +59,20 @@
     swap[...] = (column == lax.rem(row, group) * COL_Y + y).astype(F32).astype(BF16)
 
 
-def arrange_kernel(heights, features, swap, fields, cross, mate):
+def pack_kernel(weights, bias, after, packed):
+    taps, rows, lanes = weights.shape
+    packed[:taps] = weights[...]
+    column = as_column(bias[...])
+    lane = lax.broadcasted_iota(jnp.int32, (rows, lanes), 1)
+    extra = jnp.zeros((rows, lanes), F32)
+    for at in range(3):
+        piece = column.astype(BF16).astype(F32)
+        extra = jnp.where(lane == at, piece, extra)
+        column = column - piece
+    packed[taps] = extra.astype(BF16)
+
+
+def arrange_kernel(heights, features, swap, after, fields, cross, mate):
     _, channels, width, _, depth = features.shape
     place = Place(heights)
     group = 256 // COL_Y
@@ -86,10 +99,10 @@
     return jnp.where(z < live_top, total, 0.0).astype(BF16)
 
 
-def fill_first(parts, biases, slots, odd, matrix, low_matrix, high_matrix, bias):
+def fill_first(parts, slots, odd, matrix, low_matrix, high_matrix, bias):
     quarter, channels = parts[0].shape[1], parts[0].shape[2]
     block = quarter * len(parts)
-    for part, given, slot in zip(parts, biases, slots, strict=True):
+    for part, slot in zip(parts, slots, strict=True):
         at = slot * quarter
         for k in range(TAPS):
             span = pl.ds(pl.multiple_of(k * block + at, quarter), quarter)
@@ -102,7 +115,8 @@
                         low_matrix[span, pl.ds((j * 2 + i - 1) * channels, channels)] = tile
                     if i < 2:
                         high_matrix[span, pl.ds((j * 2 + i) * channels, channels)] = tile
-        value = as_column(given[...])
+        extra = part[27].astype(F32)
+        value = extra[:, 0:1] + extra[:, 1:2] + extra[:, 2:3]
         bias[pl.ds(pl.multiple_of(at, quarter), quarter), :] = jnp.broadcast_to(value, (quarter, bias.shape[1]))
 
 
@@ -158,18 +172,18 @@
     lax.fori_loop(0, (COL_Y - 2) // 2, pair, 0)
 
 
-def first_near_kernel(halo, heights, own, part_a, part_b, bias_a, bias_b, bias_c, bias_d, out, matrix, low_matrix, high_matrix, bias):
+def first_near_kernel(halo, heights, own, part_a, part_b, out, matrix, low_matrix, high_matrix, bias):
     place = Place(heights)
-    fill_first([part_a, part_b], [bias_a, bias_b], place.slots[:2], place.odd, matrix, low_matrix, high_matrix, bias)
+    fill_first([part_a, part_b], place.slots[:2], place.odd, matrix, low_matrix, high_matrix, bias)
     inner_rows(own, out, halo, (matrix, low_matrix, high_matrix), bias, place.top)
 
 
 def first_far_kernel(
-    halo, heights, own, mate, part_a, part_b, bias_a, bias_b, near, low_near, high_near, bias_near, after,
+    halo, heights, own, mate, part_a, part_b, near, low_near, high_near, bias_near, after,
     out, out_last, matrix, low_matrix, high_matrix, bias,
 ):
     place = Place(heights)
-    fill_first([part_a, part_b], [bias_a, bias_b], place.slots[2:], place.odd, matrix, low_matrix, high_matrix, bias)
+    fill_first([part_a, part_b], place.slots[2:], place.odd, matrix, low_matrix, high_matrix, bias)
     far = (matrix, low_matrix, high_matrix)
     inner_rows(own, out, halo, far, bias, place.top)
 
@@ -348,12 +362,21 @@
     )(*args)
 
 
-def arrange(heights, features):
+def order():
+    return call(order_kernel, "order", [], [(256, 256)], [], LONG)[0]
+
+
+def pack(weights, bias, after):
+    taps, rows, lanes = weights.shape
+    outputs = [(taps + 1, rows, lanes)]
+    return call(pack_kernel, "pack", [WHOLE, WHOLE, ANY], outputs, [], LONG, weights, bias[None], after)[0]
+
+
+def arrange(heights, features, swap, after):
     _, channels, width, _, depth = features.shape
     row = (width, channels, depth)
     outputs = [(COL_Y, *row), (2, *row), row]
-    swap = call(order_kernel, "order", [], [(256, 256)], [], LONG)[0]
-    return call(arrange_kernel, "arrange", [SCALARS, WHOLE, WHOLE], outputs, [], SHORT, heights, features, swap)
+    return call(arrange_kernel, "arrange", [SCALARS, WHOLE, WHOLE, ANY], outputs, [], SHORT, heights, features, swap, after)
 
 
 def first_matrices(channels, rows):
@@ -370,25 +393,25 @@
     return call(fill_kernel, "fill", [SCALARS, WHOLE, WHOLE, ANY], outputs, [], SHORT, heights, weights, bias[None], after, kinds=kinds)
 
 
-def first_near(halo, heights, own, part_a, part_b, biases):
+def first_near(halo, heights, own, part_a, part_b):
     _, _, channels, depth = own.shape
     half, width = 2 * part_a.shape[1], COL_Y + 2 * halo
     shapes, kinds = first_matrices(channels, half)
     inner, *matrices = call(
-        functools.partial(first_near_kernel, halo), "first_near", [SCALARS] + [WHOLE] * 7,
-        [(COL_Y - 2, width, half, depth), *shapes], [], LONG, heights, own, part_a, part_b, *biases, kinds=[BF16, *kinds],
+        functools.partial(first_near_kernel, halo), "first_near", [SCALARS] + [WHOLE] * 3,
+        [(COL_Y - 2, width, half, depth), *shapes], [], LONG, heights, own, part_a, part_b, kinds=[BF16, *kinds],
     )
     return inner, matrices
 
 
-def first_far(halo, heights, own, mate, part_a, part_b, bias_a, bias_b, near, after):
+def first_far(halo, heights, own, mate, part_a, part_b, near, after):
     _, _, channels, depth = own.shape
     half, width = 2 * part_a.shape[1], COL_Y + 2 * halo
     shapes, kinds = first_matrices(channels, half)
     inner, row_seven, *matrices = call(
-        functools.partial(first_far_kernel, halo), "first_far", [SCALARS] + [WHOLE] * 10 + [ANY],
+        functools.partial(first_far_kernel, halo), "first_far", [SCALARS] + [WHOLE] * 8 + [ANY],
         [(COL_Y - 2, width, half, depth), (width, channels, depth), *shapes], [], SHORT,
-        heights, own, mate, part_a, part_b, bias_a, bias_b, *near, after, kinds=[BF16, BF16, *kinds],
+        heights, own, mate, part_a, part_b, *near, after, kinds=[BF16, BF16, *kinds],
     )
     return inner, row_seven, matrices
 
@@ -426,8 +449,8 @@
     return lax.ppermute(value, "space", [(i, i ^ 1) for i in range(lax.axis_size("space"))])
 
 
-def far_pairs(peers, chans, even, odd):
-    return [(i * chans + c, i * chans + (c ^ (odd if i % 2 else even))) for i in range(peers) for c in range(chans)]
+def far_pairs(peers, chans):
+    return [(i * chans + c, i * chans + (c ^ (3 if i % 2 else 2))) for i in range(peers) for c in range(chans)]
 
 
 def with_x_borders(rows, peers):
@@ -442,27 +465,22 @@
     peers, chans = lax.axis_size("space"), lax.axis_size("chan")
     halo = 1 if peers > COL_Y else 0
 
-    near_pairs, distant_pairs = [(c, c ^ 1) for c in range(chans)], far_pairs(peers, chans, 2, 3)
-    near_part = lax.ppermute(weight_one, "chan", near_pairs)
-    far_part = lax.ppermute(weight_one, ("space", "chan"), distant_pairs)
-    own_bias = bias_one[None]
-    near_bias = lax.ppermute(own_bias, "chan", near_pairs)
-    far_bias = lax.ppermute(own_bias, ("space", "chan"), distant_pairs)
-    other_bias = lax.ppermute(own_bias, ("space", "chan"), far_pairs(peers, chans, 3, 2))
-    fields, cross, mate = arrange(column_heights, features)
+    swap = order()
+    own_part = pack(weight_one, bias_one, swap)
+    near_part = lax.ppermute(own_part, "chan", [(c, c ^ 1) for c in range(chans)])
+    far_part = lax.ppermute(own_part, ("space", "chan"), far_pairs(peers, chans))
+    fields, cross, mate = arrange(column_heights, features, swap, own_part)
     cross = lax.ppermute(cross, "space", across_pairs(peers))
     mate = to_mate(mate)
     if halo:
         fields = with_x_borders(jnp.concatenate([cross, fields, mate[None]], axis=0), peers)
         cross, fields, mate = fields[:2], fields[2:-1], fields[-1]
 
-    inner_a, near = first_near(halo, column_heights, fields, weight_one, near_part, (own_bias, near_bias, far_bias, other_bias))
+    inner_a, near = first_near(halo, column_heights, fields, own_part, near_part)
     far_part, inner_a = lax.optimization_barrier((far_part, inner_a))
     other_part = to_mate(far_part)
     matrices = fill(column_heights, weight_two, bias_two, inner_a)
-    inner_b, row_seven, far = first_far(
-        halo, column_heights, fields, mate, far_part, other_part, far_bias, other_bias, near, matrices[-1]
-    )
+    inner_b, row_seven, far = first_far(halo, column_heights, fields, mate, far_part, other_part, near, matrices[-1])
     mate = to_mate(row_seven)
     done_inner = second_inner(halo, column_heights, inner_a, inner_b, row_seven, matrices)
     hidden = (inner_a, inner_b, row_seven, mate)

time: 47.4 us -> 43.6 us (0.920); the launches traced: 46.8 us -> 43.8 us
  starting transfers between devices: 15.4 us -> 10.9 us
  local copies, waits for them, and re-layouts: 0.03 us -> 0.9 us
  Pallas kernels: 30.7 us -> 31.4 us
    ppermute x5 -> x2, starting transfers between devices: 7.87 us -> 4.39 us  [the longest x1 2.19 us: on_device(): lax.ppermute(own_part, ('space', 'chan'), far_pairs(peers, chans))]
    ppermute x3, starting transfers between devices: 4.51 us -> 3.47 us  [to_mate(): lax.ppermute(value, 'space', [(i, i ^ 1) for i in range(lax.axis_size('sp...]
    unnamed x12, local copies, waits for them, and re-layouts: 0.03 us -> 0.9 us
    pallas_call x7 -> x8, Pallas kernels: 30.7 us -> 31.4 us  [call(): pl.pallas_call(kernel, out_shape=[jax.ShapeDtypeStruct(*each) for each in...]
  transfers between devices with their start and end apart: 9 -> 6, of which waited for: 1 -> 2; matrix products, arithmetic and copies ran while one was open for 0% -> 0% of each run, Pallas kernels for 51% -> 53%
where the time goes in v4:
time: 43.6 us; the launch traced here: 43.8 us
  Pallas kernels  31.4 us (72%)
  starting transfers between devices  10.9 us (25%)
  local copies, waits for them, and re-layouts  0.9 us (2%)
    pallas_call x8, Pallas kernels, call(): pl.pallas_call(kernel, out_shape=[jax.ShapeDtypeStruct(*each) for each in...  31.4 us
    ppermute x3, starting transfers between devices, to_mate(): lax.ppermute(value, 'space', [(i, i ^ 1) for i in range(lax.axis_size('sp...  3.47 us
    ppermute x1, starting transfers between devices, on_device(): cross = lax.ppermute(cross, 'space', across_pairs(peers))  3.02 us
    ppermute x1, starting transfers between devices, on_device(): lax.ppermute(own_part, ('space', 'chan'), far_pairs(peers, chans))  2.19 us
    ppermute x1, starting transfers between devices, on_device(): lax.ppermute(own_part, 'chan', [(c, c ^ 1) for c in range(chans)])  2.19 us
    unnamed x12, local copies, waits for them, and re-layouts  0.9 us
  transfers between devices with their start and end apart: 6, of which 2 were waited for; matrix products, arithmetic and copies ran while one was open for 0% of the time, Pallas kernels for 53%

profile of v4, /device:TPU:1, one launch (start us, length us, event | category | flops | bytes accessed | tf_op | source)
XLA Modules:
  0.0 43.8 jit_solution(14975774366700213539)
XLA Ops:
  0.0 0.1 order.1.after.swap
  0.1 0.6 %copy-done.5 = f32[32]{0:T(128)S(1)} copy-done((f32[32]{0:T(128)S(1)}, f32[32]{0:T(128)}, u32[]{:S(2)}) %copy-start.5) | copy-done | bytes 152
  0.7 0.3 copy-done.4
  1.0 0.1 pack.1.after.part_a
  1.1 2.2 %collective-permute-start.1 = (bf16[28,32,128]{2,1,0:T(8,128)(2,1)S(1)}, bf16[28,32,128]{2,1,0:T(8,128)(2,1)S(1)}, u32[]{:S(2)}, u32[]{:S(2)}) collective-permute-start(bf16[28,32,128]{2,1,0:T(8,128)(2,1)S(1)} %pack.1.after.part_a), channel_id=1, source_target_pairs={{0,1},{1,0},{2,3},{3,2},{4,5},{5,4},{6,7},{7,6},{8,9},{9,8},{10,11... | collective-permute-start | bytes 688136 | tf_op jit(solution)/shard_map/ppermute | solution.py:470
  3.2 2.2 %collective-permute-start.3 = (bf16[28,32,128]{2,1,0:T(8,128)(2,1)S(1)}, bf16[28,32,128]{2,1,0:T(8,128)(2,1)S(1)}, u32[]{:S(2)}, u32[]{:S(2)}) collective-permute-start(bf16[28,32,128]{2,1,0:T(8,128)(2,1)S(1)} %pack.1.after.part_a), channel_id=1, source_target_pairs={{0,2},{1,3},{2,0},{3,1},{4,7},{5,6},{6,5},{7,4},{8,10},{9,11},{10,... | collective-permute-start | bytes 688136 | tf_op jit(solution)/shard_map/ppermute | solution.py:471
  5.4 1.9 %arrange.1 = (bf16[8,8,128,256]{3,2,1,0:T(8,128)(2,1)S(1)}, bf16[2,8,128,256]{3,2,1,0:T(8,128)(2,1)S(1)}, bf16[8,128,256]{2,1,0:T(8,128)(2,1)S(1)}) custom-call(s32[8]{0:T(128)S(1)} %copy-done.2, bf16[1,128,8,8,256]{4,3,2,1,0:T(8,128)(2,1)S(1)} %copy-done, bf16[256,256]{1,0:T(8,128)(2,1)S(1)} %order.1.after.swap, bf16[28,32,128]{2,1,0:T(8,128)(2,1)S(1)} %pack.1.after.part_a), custom_call_target="tpu_custom_call" | custom-call | flops 4096 | bytes 64 | tf_op jit(solution)/shard_map/arrange/pallas_call | solution.py:353
  7.3 1.4 %collective-permute-start.2 = (bf16[8,128,256]{2,1,0:T(8,128)(2,1)S(1)}, bf16[8,128,256]{2,1,0:T(8,128)(2,1)S(1)}, u32[]{:S(2)}, u32[]{:S(2)}) collective-permute-start(bf16[8,128,256]{2,1,0:T(8,128)(2,1)S(1)} %get-tuple-element.31), channel_id=1, source_target_pairs={{0,4},{4,0},{8,12},{12,8},{16,20},{20,16},{24,28},{28,24},{1,5},{5... | collective-permute-start | bytes 1572872 | tf_op jit(solution)/shard_map/ppermute | solution.py:449
  8.7 3.0 %collective-permute-start = (bf16[2,8,128,256]{3,2,1,0:T(8,128)(2,1)S(1)}, bf16[2,8,128,256]{3,2,1,0:T(8,128)(2,1)S(1)}, u32[]{:S(2)}, u32[]{:S(2)}) collective-permute-start(bf16[2,8,128,256]{3,2,1,0:T(8,128)(2,1)S(1)} %get-tuple-element.26), channel_id=1, source_target_pairs={{4,8},{8,4},{12,16},{16,12},{20,24},{24,20},{5,9},{9,5},{13,17},{1... | collective-permute-start | bytes 3145736 | tf_op jit(solution)/shard_map/ppermute | solution.py:473
  11.8 0.0 collective-permute-done.1.part_b
  11.8 0.0 copy-start.1
  11.8 0.0 copy-start.3
  11.8 7.2 %first_near.1 = (bf16[6,8,64,256]{3,2,1,0:T(8,128)(2,1)S(1)}, bf16[192,1152]{1,0:T(8,128)(2,1)S(1)}, bf16[192,768]{1,0:T(8,128)(2,1)S(1)}, bf16[192,768]{1,0:T(8,128)(2,1)S(1)}, f32[64,128]{1,0:T(8,128)S(1)}) custom-call(s32[8]{0:T(128)S(1)} %copy-done.2, bf16[8,8,128,256]{3,2,1,0:T(8,128)(2,1)S(1)} %get-tuple-element.25.own, ...), custom_call_target="tpu_custom_call" | custom-call | flops 8589934592 | bytes 134217728 | tf_op jit(solution)/shard_map/first_near/pallas_call | solution.py:353
  19.0 0.0 collective-permute-done.3.part_a
  19.1 1.6 %collective-permute-start.4 = (bf16[28,32,128]{2,1,0:T(8,128)(2,1)S(1)}, bf16[28,32,128]{2,1,0:T(8,128)(2,1)S(1)}, u32[]{:S(2)}, u32[]{:S(2)}) collective-permute-start(bf16[28,32,128]{2,1,0:T(8,128)(2,1)S(1)} %collective-permute-done.3.part_a), channel_id=1, source_target_pairs={{0,4},{4,0},{8,12},{12,8},{16,20},{20,16},{24,28},{28,24},{1,5},{5... | collective-permute-start | bytes 688136 | tf_op jit(solution)/shard_map/ppermute | solution.py:449
  20.7 0.8 %fill.1 = (bf16[192,1536]{1,0:T(8,128)(2,1)S(1)}, bf16[192,1152]{1,0:T(8,128)(2,1)S(1)}, bf16[192,1152]{1,0:T(8,128)(2,1)S(1)}, f32[64,128]{1,0:T(8,128)S(1)}) custom-call(s32[8]{0:T(128)S(1)} %copy-done.2, bf16[27,32,128]{2,1,0:T(8,128)(2,1)S(1)} %copy-done.1, f32[1,32]{1,0:T(1,128)S(1)} %bitcast.2, bf16[6,8,64,256]{3,2,1,0:T(8,128)(2,1)S(1)} %get-tuple-element.34.after.inner_a), custom_call_target="tpu_custom_call" | custom-call | flops 4096 | bytes 64 | tf_op jit(solution)/shard_map/fill/pallas_call | solution.py:353
  21.5 0.3 collective-permute-done.4.part_b
  21.8 0.0 collective-permute-done.2.mate
  21.8 9.2 %first_far.1 = (bf16[6,8,64,256]{3,2,1,0:T(8,128)(2,1)S(1)}, bf16[8,128,256]{2,1,0:T(8,128)(2,1)S(1)}, bf16[192,1152]{1,0:T(8,128)(2,1)S(1)}, bf16[192,768]{1,0:...) custom-call(s32[8]{0:T(128)S(1)} %copy-done.2, ...), custom_call_target="tpu_custom_call" | custom-call | flops 4096 | bytes 64 | tf_op jit(solution)/shard_map/first_far/pallas_call | solution.py:353
  31.0 0.4 collective-permute-start.5
  31.5 4.2 %second_inner.1.done_inner = bf16[5,8,32,256]{3,2,1,0:T(8,128)(2,1)S(1)} custom-call(s32[8]{0:T(128)S(1)} %copy-done.2, bf16[6,8,64,256]{3,2,1,0:T(8,128)(2,1)S(1)} %get-tuple-element.34.after.inner_a, bf16[6,8,64,256]{3,2,1,0:T(8,128)(2,1)S(1)} %get-tuple-element.40.inner_b, bf16[8,128,256]{2,1,0:T(8,128)(2,1)S(1)} %get-tuple-element.41.row_seven, ...), custom_call_target="tpu_custom_call" | custom-call | flops 4096 | bytes 64 | tf_op jit(solution)/shard_map/second_inner/pallas_call | solution.py:353
  35.7 0.1 collective-permute-done.cross
  35.8 0.0 collective-permute-done.5.mate
  35.8 7.9 %last.1 = bf16[1,32,8,8,256]{4,3,2,1,0:T(8,128)(2,1)} custom-call(s32[8]{0:T(128)S(1)} %copy-done.2, bf16[8,8,128,256]{3,2,1,0:T(8,128)(2,1)S(1)} %get-tuple-element.25.own, bf16[2,8,128,256]{3,2,1,0:T(8,128)(2,1)S(1)} %collective-permute-done.cross, bf16[192,1152]{1,0:T(8,128)(2,1)S(1)} %get-tuple-element.27.near, ...), custom_call_target="tpu_custom_call" | custom-call | flops 4096 | bytes 64 | tf_op jit(solution)/shard_map/last/pallas_call | solution.py:353
  (8 shorter events, 0.0 us)
Async XLA Ops:
  0.0 0.7 %copy-start.5 = (f32[32]{0:T(128)S(1)}, f32[32]{0:T(128)}, u32[]{:S(2)}) copy-start(f32[32]{0:T(128)} %param.9) | copy-start | bytes 388
  0.0 0.9 %copy-start.4 = (bf16[27,32,128]{2,1,0:T(8,128)(2,1)S(1)}, bf16[27,32,128]{2,1,0:T(8,128)(2,1)}, u32[]{:S(2)}) copy-start(bf16[27,32,128]{2,1,0:T(8,128)(2,1)} %weights.2) | copy-start | bytes 663556
  1.0 4.5 %copy-start = (bf16[1,128,8,8,256]{4,3,2,1,0:T(8,128)(2,1)S(1)}, bf16[1,128,8,8,256]{4,3,2,1,0:T(8,128)(2,1)}, u32[]{:S(2)}) copy-start(bf16[1,128,8,8,256]{4,3,2,1,0:T(8,128)(2,1)} %features.1) | copy-start | bytes 12582916
  1.0 4.5 %copy-start.2 = (s32[8]{0:T(128)S(1)}, s32[8]{0:T(128)}, u32[]{:S(2)}) copy-start(s32[8]{0:T(128)} %heights.11) | copy-start | bytes 100
  1.1 10.7 %collective-permute-start.1 = (bf16[28,32,128]{2,1,0:T(8,128)(2,1)S(1)}, bf16[28,32,128]{2,1,0:T(8,128)(2,1)S(1)}, u32[]{:S(2)}, u32[]{:S(2)}) collective-permute-start(bf16[28,32,128]{2,1,0:T(8,128)(2,1)S(1)} %pack.1.after.part_a), channel_id=1, source_target_pairs={{0,1},{1,0},{2,3},{3,2},{4,5},{5,4},{6,7},{7,6},{8,9},{9,8},{10,11... | collective-permute-start | bytes 688136 | tf_op jit(solution)/shard_map/ppermute | solution.py:470
  3.2 15.8 %collective-permute-start.3 = (bf16[28,32,128]{2,1,0:T(8,128)(2,1)S(1)}, bf16[28,32,128]{2,1,0:T(8,128)(2,1)S(1)}, u32[]{:S(2)}, u32[]{:S(2)}) collective-permute-start(bf16[28,32,128]{2,1,0:T(8,128)(2,1)S(1)} %pack.1.after.part_a), channel_id=1, source_target_pairs={{0,2},{1,3},{2,0},{3,1},{4,7},{5,6},{6,5},{7,4},{8,10},{9,11},{10,... | collective-permute-start | bytes 688136 | tf_op jit(solution)/shard_map/ppermute | solution.py:471
  7.3 14.5 %collective-permute-start.2 = (bf16[8,128,256]{2,1,0:T(8,128)(2,1)S(1)}, bf16[8,128,256]{2,1,0:T(8,128)(2,1)S(1)}, u32[]{:S(2)}, u32[]{:S(2)}) collective-permute-start(bf16[8,128,256]{2,1,0:T(8,128)(2,1)S(1)} %get-tuple-element.31), channel_id=1, source_target_pairs={{0,4},{4,0},{8,12},{12,8},{16,20},{20,16},{24,28},{28,24},{1,5},{5... | collective-permute-start | bytes 1572872 | tf_op jit(solution)/shard_map/ppermute | solution.py:449
  8.7 27.0 %collective-permute-start = (bf16[2,8,128,256]{3,2,1,0:T(8,128)(2,1)S(1)}, bf16[2,8,128,256]{3,2,1,0:T(8,128)(2,1)S(1)}, u32[]{:S(2)}, u32[]{:S(2)}) collective-permute-start(bf16[2,8,128,256]{3,2,1,0:T(8,128)(2,1)S(1)} %get-tuple-element.26), channel_id=1, source_target_pairs={{4,8},{8,4},{12,16},{16,12},{20,24},{24,20},{5,9},{9,5},{13,17},{1... | collective-permute-start | bytes 3145736 | tf_op jit(solution)/shard_map/ppermute | solution.py:473
  11.8 8.9 %copy-start.1 = (bf16[27,32,128]{2,1,0:T(8,128)(2,1)S(1)}, bf16[27,32,128]{2,1,0:T(8,128)(2,1)}, u32[]{:S(2)}) copy-start(bf16[27,32,128]{2,1,0:T(8,128)(2,1)} %weights.3) | copy-start | bytes 663556
  11.8 8.9 %copy-start.3 = (f32[32]{0:T(128)S(1)}, f32[32]{0:T(128)}, u32[]{:S(2)}) copy-start(f32[32]{0:T(128)} %param.11) | copy-start | bytes 388
  19.1 2.7 %collective-permute-start.4 = (bf16[28,32,128]{2,1,0:T(8,128)(2,1)S(1)}, bf16[28,32,128]{2,1,0:T(8,128)(2,1)S(1)}, u32[]{:S(2)}, u32[]{:S(2)}) collective-permute-start(bf16[28,32,128]{2,1,0:T(8,128)(2,1)S(1)} %collective-permute-done.3.part_a), channel_id=1, source_target_pairs={{0,4},{4,0},{8,12},{12,8},{16,20},{20,16},{24,28},{28,24},{1,5},{5... | collective-permute-start | bytes 688136 | tf_op jit(solution)/shard_map/ppermute | solution.py:449
  31.0 4.7 %collective-permute-start.5 = (bf16[8,128,256]{2,1,0:T(8,128)(2,1)S(1)}, bf16[8,128,256]{2,1,0:T(8,128)(2,1)S(1)}, u32[]{:S(2)}, u32[]{:S(2)}) collective-permute-start(bf16[8,128,256]{2,1,0:T(8,128)(2,1)S(1)} %get-tuple-element.41.row_seven), channel_id=1, source_target_pairs={{0,4},{4,0},{8,12},{12,8},{16,20},{20,16},{24,28},{28,24},{1,5},{5... | collective-permute-start | bytes 1572872 | tf_op jit(solution)/shard_map/ppermute | solution.py:449

commit v5 on v4

--- a/solution.py
+++ b/solution.py
@@ -193,15 +193,26 @@
     whole_row(get, own.shape[1], halo, ((near, low_near, high_near), bias_near), (far, bias), place.top, out_last)
 
 
+class Joined:
+    def __init__(self, near, far):
+        self.near, self.far = near, far
+        self.shape = (2 * near.shape[0], near.shape[1])
+
+    def __getitem__(self, _):
+        rows = self.near.shape[0] // TAPS
+        pieces = [ref[k * rows : (k + 1) * rows] for k in range(TAPS) for ref in (self.near, self.far)]
+        return jnp.concatenate(pieces, axis=0)
+
+
 def whole_row(get, stored, halo, near, far, top, out, *at, levels=None):
-    half = near[1].shape[0]
-    for first, (matrices, bias) in ((0, near), (half, far)):
-        if levels is None:
-            for x, done in first_row(get, stored, halo, matrices, bias, top):
-                out[(*at, x, slice(first, first + half))] = done
-        else:
-            for x, done in first_row_low(get, stored, halo, matrices, bias, top, levels):
-                out[(*at, x, slice(first, first + half), slice(0, levels))] = done
+    matrices = [Joined(*each) for each in zip(near[0], far[0], strict=True)]
+    bias = jnp.concatenate([near[1][...], far[1][...]], axis=0)
+    if levels is None:
+        for x, done in first_row(get, stored, halo, matrices, bias, top):
+            out[(*at, x)] = done
+    else:
+        for x, done in first_row_low(get, stored, halo, matrices, bias, top, levels):
+            out[(*at, x, slice(None), slice(0, levels))] = done
 
 
 def fill_second(weights, place, matrix, low_matrix, high_matrix):
@@ -258,22 +269,13 @@
     place = Place(heights)
     matrices, width, top = (matrix, low_matrix, high_matrix), inner_a.shape[1], place.top()
 
-    def pair(step, _):
-        for more in range(2):
-            u = step * 2 + more
-            for x, here, beside in second_row(lambda j, a, b: halves(inner_a, inner_b, u + j, a, b), width, halo, matrices, both[:, 0:1], top):
-                out[u, x] = here
-                out[u, x + 1] = beside
-        return 0
-
-    lax.fori_loop(0, 2, pair, 0)
-
     def row(u, a, b):
         return halves(inner_a, inner_b, u - 1, a, b) if u < 7 else [row_seven[x] for x in range(a, b)]
 
-    for x, here, beside in second_row(lambda j, a, b: row(5 + j, a, b), width, halo, matrices, both[:, 0:1], top):
-        out[4, x] = here
-        out[4, x + 1] = beside
+    for u in range(2, 7):
+        for x, here, beside in second_row(lambda j, a, b: row(u - 1 + j, a, b), width, halo, matrices, both[:, 0:1], top):
+            out[u - 2, x] = here
+            out[u - 2, x + 1] = beside
 
 
 def last_kernel(
@@ -468,9 +470,11 @@
     swap = order()
     own_part = pack(weight_one, bias_one, swap)
     near_part = lax.ppermute(own_part, "chan", [(c, c ^ 1) for c in range(chans)])
-    far_part = lax.ppermute(own_part, ("space", "chan"), far_pairs(peers, chans))
     fields, cross, mate = arrange(column_heights, features, swap, own_part)
+    sent_part, cross = lax.optimization_barrier((own_part, cross))
+    far_part = lax.ppermute(sent_part, ("space", "chan"), far_pairs(peers, chans))
     cross = lax.ppermute(cross, "space", across_pairs(peers))
+    near_part, mate = lax.optimization_barrier((near_part, mate))
     mate = to_mate(mate)
     if halo:
         fields = with_x_borders(jnp.concatenate([cross, fields, mate[None]], axis=0), peers)

time: 43.6 us -> 43.6 us (level)
  waiting for transfers between devices: 0.37 us -> 2.1 us
  Pallas kernels: 31.4 us -> 29.9 us
  starting transfers between devices: 10.9 us -> 10.3 us
    ppermute x3, starting transfers between devices: 3.47 us -> 1.04 us  [to_mate(): lax.ppermute(value, 'space', [(i, i ^ 1) for i in range(lax.axis_size('sp...]
    ppermute x1, starting transfers between devices: 2.19 us -> 4.11 us  [on_device(): lax.ppermute(sent_part, ('space', 'chan'), far_pairs(peers, chans))]
    ppermute x1, waiting for transfers between devices: 0.06 us -> 1.8 us  [on_device(): cross = lax.ppermute(cross, 'space', across_pairs(peers))]
    pallas_call x8, Pallas kernels: 31.4 us -> 29.9 us  [call(): pl.pallas_call(kernel, out_shape=[jax.ShapeDtypeStruct(*each) for each in...]
  transfers between devices with their start and end apart: 6 -> 6, of which waited for: 2 -> 2; matrix products, arithmetic and copies ran while one was open for 0% -> 0% of each run, Pallas kernels for 53% -> 52%
where the time goes in v5:
time: 43.6 us; the launch traced here: 43.5 us
  Pallas kernels  29.9 us (69%)
  starting transfers between devices  10.3 us (24%)
  waiting for transfers between devices  2.1 us (5%)
  local copies, waits for them, and re-layouts  0.9 us (2%)
    pallas_call x8, Pallas kernels, call(): pl.pallas_call(kernel, out_shape=[jax.ShapeDtypeStruct(*each) for each in...  29.9 us
    ppermute x1, starting transfers between devices, on_device(): lax.ppermute(sent_part, ('space', 'chan'), far_pairs(peers, chans))  4.11 us
    ppermute x1, starting transfers between devices, on_device(): cross = lax.ppermute(cross, 'space', across_pairs(peers))  2.94 us
    ppermute x1, starting transfers between devices, on_device(): lax.ppermute(own_part, 'chan', [(c, c ^ 1) for c in range(chans)])  2.19 us
    ppermute x1, waiting for transfers between devices, on_device(): cross = lax.ppermute(cross, 'space', across_pairs(peers))  1.8 us
    ppermute x3, starting transfers between devices, to_mate(): lax.ppermute(value, 'space', [(i, i ^ 1) for i in range(lax.axis_size('sp...  1.04 us
    unnamed x12, local copies, waits for them, and re-layouts  0.9 us
  transfers between devices with their start and end apart: 6, of which 2 were waited for; matrix products, arithmetic and copies ran while one was open for 0% of the time, Pallas kernels for 52%

profile of v5, /device:TPU:1, one launch (start us, length us, event | category | flops | bytes accessed | tf_op | source)
XLA Modules:
  0.0 43.5 jit_solution(11969631343873720426)
XLA Ops:
  0.0 0.1 order.1.after.swap
  0.1 0.6 %copy-done.5 = f32[32]{0:T(128)S(1)} copy-done((f32[32]{0:T(128)S(1)}, f32[32]{0:T(128)}, u32[]{:S(2)}) %copy-start.5) | copy-done | bytes 152
  0.7 0.3 copy-done.4
  1.0 0.1 pack.1.after.part_a
  1.1 2.2 %collective-permute-start.1 = (bf16[28,32,128]{2,1,0:T(8,128)(2,1)S(1)}, bf16[28,32,128]{2,1,0:T(8,128)(2,1)S(1)}, u32[]{:S(2)}, u32[]{:S(2)}) collective-permute-start(bf16[28,32,128]{2,1,0:T(8,128)(2,1)S(1)} %pack.1.after.part_a), channel_id=1, source_target_pairs={{0,1},{1,0},{2,3},{3,2},{4,5},{5,4},{6,7},{7,6},{8,9},{9,8},{10,11... | collective-permute-start | bytes 688136 | tf_op jit(solution)/shard_map/ppermute | solution.py:472
  3.2 1.9 %arrange.1 = (bf16[8,8,128,256]{3,2,1,0:T(8,128)(2,1)S(1)}, bf16[2,8,128,256]{3,2,1,0:T(8,128)(2,1)S(1)}, bf16[8,128,256]{2,1,0:T(8,128)(2,1)S(1)}) custom-call(s32[8]{0:T(128)S(1)} %copy-done.2, bf16[1,128,8,8,256]{4,3,2,1,0:T(8,128)(2,1)S(1)} %copy-done, bf16[256,256]{1,0:T(8,128)(2,1)S(1)} %order.1.after.swap, bf16[28,32,128]{2,1,0:T(8,128)(2,1)S(1)} %pack.1.after.part_a), custom_call_target="tpu_custom_call" | custom-call | flops 4096 | bytes 64 | tf_op jit(solution)/shard_map/arrange/pallas_call | solution.py:355
  5.1 4.1 %collective-permute-start.3 = (bf16[28,32,128]{2,1,0:T(8,128)(2,1)S(1)}, bf16[28,32,128]{2,1,0:T(8,128)(2,1)S(1)}, u32[]{:S(2)}, u32[]{:S(2)}) collective-permute-start(bf16[28,32,128]{2,1,0:T(8,128)(2,1)S(1)} %pack.1.after.part_a), channel_id=1, source_target_pairs={{0,2},{1,3},{2,0},{3,1},{4,7},{5,6},{6,5},{7,4},{8,10},{9,11},{10,... | collective-permute-start | bytes 688136 | tf_op jit(solution)/shard_map/ppermute | solution.py:475
  9.2 2.9 %collective-permute-start = (bf16[2,8,128,256]{3,2,1,0:T(8,128)(2,1)S(1)}, bf16[2,8,128,256]{3,2,1,0:T(8,128)(2,1)S(1)}, u32[]{:S(2)}, u32[]{:S(2)}) collective-permute-start(bf16[2,8,128,256]{3,2,1,0:T(8,128)(2,1)S(1)} %get-tuple-element.31), channel_id=1, source_target_pairs={{4,8},{8,4},{12,16},{16,12},{20,24},{24,20},{5,9},{9,5},{13,17},{1... | collective-permute-start | bytes 3145736 | tf_op jit(solution)/shard_map/ppermute | solution.py:476
  12.2 0.0 collective-permute-done.1.part_b
  12.2 0.1 collective-permute-start.2
  12.3 0.0 copy-start.1
  12.3 0.0 copy-start.3
  12.3 7.2 %first_near.1 = (bf16[6,8,64,256]{3,2,1,0:T(8,128)(2,1)S(1)}, bf16[192,1152]{1,0:T(8,128)(2,1)S(1)}, bf16[192,768]{1,0:T(8,128)(2,1)S(1)}, bf16[192,768]{1,0:T(8,128)(2,1)S(1)}, f32[64,128]{1,0:T(8,128)S(1)}) custom-call(s32[8]{0:T(128)S(1)} %copy-done.2, bf16[8,8,128,256]{3,2,1,0:T(8,128)(2,1)S(1)} %get-tuple-element.29.own, ...), custom_call_target="tpu_custom_call" | custom-call | flops 8589934592 | bytes 134217728 | tf_op jit(solution)/shard_map/first_near/pallas_call | solution.py:355
  19.5 0.0 collective-permute-done.3.part_a
  19.6 0.5 %collective-permute-start.4 = (bf16[28,32,128]{2,1,0:T(8,128)(2,1)S(1)}, bf16[28,32,128]{2,1,0:T(8,128)(2,1)S(1)}, u32[]{:S(2)}, u32[]{:S(2)}) collective-permute-start(bf16[28,32,128]{2,1,0:T(8,128)(2,1)S(1)} %collective-permute-done.3.part_a), channel_id=1, source_target_pairs={{0,4},{4,0},{8,12},{12,8},{16,20},{20,16},{24,28},{28,24},{1,5},{5... | collective-permute-start | bytes 688136 | tf_op jit(solution)/shard_map/ppermute | solution.py:451
  20.1 0.8 %fill.1 = (bf16[192,1536]{1,0:T(8,128)(2,1)S(1)}, bf16[192,1152]{1,0:T(8,128)(2,1)S(1)}, bf16[192,1152]{1,0:T(8,128)(2,1)S(1)}, f32[64,128]{1,0:T(8,128)S(1)}) custom-call(s32[8]{0:T(128)S(1)} %copy-done.2, bf16[27,32,128]{2,1,0:T(8,128)(2,1)S(1)} %copy-done.1, f32[1,32]{1,0:T(1,128)S(1)} %bitcast.2, bf16[6,8,64,256]{3,2,1,0:T(8,128)(2,1)S(1)} %get-tuple-element.42.after.inner_a), custom_call_target="tpu_custom_call" | custom-call | flops 4096 | bytes 64 | tf_op jit(solution)/shard_map/fill/pallas_call | solution.py:355
  20.9 0.3 collective-permute-done.4.part_b
  21.2 0.0 collective-permute-done.2.mate
  21.2 9.2 %first_far.1 = (bf16[6,8,64,256]{3,2,1,0:T(8,128)(2,1)S(1)}, bf16[8,128,256]{2,1,0:T(8,128)(2,1)S(1)}, bf16[192,1152]{1,0:T(8,128)(2,1)S(1)}, bf16[192,768]{1,0:...) custom-call(s32[8]{0:T(128)S(1)} %copy-done.2, ...), custom_call_target="tpu_custom_call" | custom-call | flops 4096 | bytes 64 | tf_op jit(solution)/shard_map/first_far/pallas_call | solution.py:355
  30.4 0.4 collective-permute-start.5
  30.9 3.7 %second_inner.1.done_inner = bf16[5,8,32,256]{3,2,1,0:T(8,128)(2,1)S(1)} custom-call(s32[8]{0:T(128)S(1)} %copy-done.2, bf16[6,8,64,256]{3,2,1,0:T(8,128)(2,1)S(1)} %get-tuple-element.42.after.inner_a, bf16[6,8,64,256]{3,2,1,0:T(8,128)(2,1)S(1)} %get-tuple-element.48.inner_b, bf16[8,128,256]{2,1,0:T(8,128)(2,1)S(1)} %get-tuple-element.49.row_seven, ...), custom_call_target="tpu_custom_call" | custom-call | flops 4096 | bytes 64 | tf_op jit(solution)/shard_map/second_inner/pallas_call | solution.py:355
  34.6 1.8 %collective-permute-done.cross = bf16[2,8,128,256]{3,2,1,0:T(8,128)(2,1)S(1)} collective-permute-done((bf16[2,8,128,256]{3,2,1,0:T(8,128)(2,1)S(1)}, bf16[2,8,128,256]{3,2,1,0:T(8,128)(2,1)S(1)}, u32[]{:S(2)}, u32[]{:S(2)}) %collective-permute-start) | collective-permute-done | bytes 1048608 | tf_op jit(solution)/shard_map/ppermute | solution.py:476
  36.4 0.0 collective-permute-done.5.mate
  36.4 6.9 %last.1 = bf16[1,32,8,8,256]{4,3,2,1,0:T(8,128)(2,1)} custom-call(s32[8]{0:T(128)S(1)} %copy-done.2, bf16[8,8,128,256]{3,2,1,0:T(8,128)(2,1)S(1)} %get-tuple-element.29.own, bf16[2,8,128,256]{3,2,1,0:T(8,128)(2,1)S(1)} %collective-permute-done.cross, bf16[192,1152]{1,0:T(8,128)(2,1)S(1)} %get-tuple-element.34.near, ...), custom_call_target="tpu_custom_call" | custom-call | flops 4096 | bytes 64 | tf_op jit(solution)/shard_map/last/pallas_call | solution.py:355
  (8 shorter events, 0.0 us)
Async XLA Ops:
  0.0 0.7 %copy-start.5 = (f32[32]{0:T(128)S(1)}, f32[32]{0:T(128)}, u32[]{:S(2)}) copy-start(f32[32]{0:T(128)} %param.9) | copy-start | bytes 388
  0.0 0.9 %copy-start.4 = (bf16[27,32,128]{2,1,0:T(8,128)(2,1)S(1)}, bf16[27,32,128]{2,1,0:T(8,128)(2,1)}, u32[]{:S(2)}) copy-start(bf16[27,32,128]{2,1,0:T(8,128)(2,1)} %weights.2) | copy-start | bytes 663556
  1.0 2.3 %copy-start = (bf16[1,128,8,8,256]{4,3,2,1,0:T(8,128)(2,1)S(1)}, bf16[1,128,8,8,256]{4,3,2,1,0:T(8,128)(2,1)}, u32[]{:S(2)}) copy-start(bf16[1,128,8,8,256]{4,3,2,1,0:T(8,128)(2,1)} %features.1) | copy-start | bytes 12582916
  1.0 2.3 %copy-start.2 = (s32[8]{0:T(128)S(1)}, s32[8]{0:T(128)}, u32[]{:S(2)}) copy-start(s32[8]{0:T(128)} %heights.11) | copy-start | bytes 100
  1.1 11.1 %collective-permute-start.1 = (bf16[28,32,128]{2,1,0:T(8,128)(2,1)S(1)}, bf16[28,32,128]{2,1,0:T(8,128)(2,1)S(1)}, u32[]{:S(2)}, u32[]{:S(2)}) collective-permute-start(bf16[28,32,128]{2,1,0:T(8,128)(2,1)S(1)} %pack.1.after.part_a), channel_id=1, source_target_pairs={{0,1},{1,0},{2,3},{3,2},{4,5},{5,4},{6,7},{7,6},{8,9},{9,8},{10,11... | collective-permute-start | bytes 688136 | tf_op jit(solution)/shard_map/ppermute | solution.py:472
  5.1 14.4 %collective-permute-start.3 = (bf16[28,32,128]{2,1,0:T(8,128)(2,1)S(1)}, bf16[28,32,128]{2,1,0:T(8,128)(2,1)S(1)}, u32[]{:S(2)}, u32[]{:S(2)}) collective-permute-start(bf16[28,32,128]{2,1,0:T(8,128)(2,1)S(1)} %pack.1.after.part_a), channel_id=1, source_target_pairs={{0,2},{1,3},{2,0},{3,1},{4,7},{5,6},{6,5},{7,4},{8,10},{9,11},{10,... | collective-permute-start | bytes 688136 | tf_op jit(solution)/shard_map/ppermute | solution.py:475
  9.2 27.1 %collective-permute-start = (bf16[2,8,128,256]{3,2,1,0:T(8,128)(2,1)S(1)}, bf16[2,8,128,256]{3,2,1,0:T(8,128)(2,1)S(1)}, u32[]{:S(2)}, u32[]{:S(2)}) collective-permute-start(bf16[2,8,128,256]{3,2,1,0:T(8,128)(2,1)S(1)} %get-tuple-element.31), channel_id=1, source_target_pairs={{4,8},{8,4},{12,16},{16,12},{20,24},{24,20},{5,9},{9,5},{13,17},{1... | collective-permute-start | bytes 3145736 | tf_op jit(solution)/shard_map/ppermute | solution.py:476
  12.2 9.0 %collective-permute-start.2 = (bf16[8,128,256]{2,1,0:T(8,128)(2,1)S(1)}, bf16[8,128,256]{2,1,0:T(8,128)(2,1)S(1)}, u32[]{:S(2)}, u32[]{:S(2)}) collective-permute-start(bf16[8,128,256]{2,1,0:T(8,128)(2,1)S(1)} %get-tuple-element.38), channel_id=1, source_target_pairs={{0,4},{4,0},{8,12},{12,8},{16,20},{20,16},{24,28},{28,24},{1,5},{5... | collective-permute-start | bytes 1572872 | tf_op jit(solution)/shard_map/ppermute | solution.py:451
  12.3 7.8 %copy-start.1 = (bf16[27,32,128]{2,1,0:T(8,128)(2,1)S(1)}, bf16[27,32,128]{2,1,0:T(8,128)(2,1)}, u32[]{:S(2)}) copy-start(bf16[27,32,128]{2,1,0:T(8,128)(2,1)} %weights.3) | copy-start | bytes 663556
  12.3 7.8 %copy-start.3 = (f32[32]{0:T(128)S(1)}, f32[32]{0:T(128)}, u32[]{:S(2)}) copy-start(f32[32]{0:T(128)} %param.11) | copy-start | bytes 388
  19.6 1.7 %collective-permute-start.4 = (bf16[28,32,128]{2,1,0:T(8,128)(2,1)S(1)}, bf16[28,32,128]{2,1,0:T(8,128)(2,1)S(1)}, u32[]{:S(2)}, u32[]{:S(2)}) collective-permute-start(bf16[28,32,128]{2,1,0:T(8,128)(2,1)S(1)} %collective-permute-done.3.part_a), channel_id=1, source_target_pairs={{0,4},{4,0},{8,12},{12,8},{16,20},{20,16},{24,28},{28,24},{1,5},{5... | collective-permute-start | bytes 688136 | tf_op jit(solution)/shard_map/ppermute | solution.py:451
  30.4 5.9 %collective-permute-start.5 = (bf16[8,128,256]{2,1,0:T(8,128)(2,1)S(1)}, bf16[8,128,256]{2,1,0:T(8,128)(2,1)S(1)}, u32[]{:S(2)}, u32[]{:S(2)}) collective-permute-start(bf16[8,128,256]{2,1,0:T(8,128)(2,1)S(1)} %get-tuple-element.49.row_seven), channel_id=1, source_target_pairs={{0,4},{4,0},{8,12},{12,8},{16,20},{20,16},{24,28},{28,24},{1,5},{5... | collective-permute-start | bytes 1572872 | tf_op jit(solution)/shard_map/ppermute | solution.py:451

commit v6 on v5

--- a/solution.py
+++ b/solution.py
@@ -348,7 +348,7 @@
         pltpu.make_async_copy(result.at[x], out.at[0, :, x], sems.at[x]).wait()
 
 
-SHORT, LONG = 2**6, 2**27
+SHORT, MIDDLE, LONG = 2**6, 2**25, 2**27
 
 
 def call(kernel, name, inputs, outputs, scratch, nbytes, *args, kinds=None, place=WHOLE):
@@ -401,7 +401,7 @@
     shapes, kinds = first_matrices(channels, half)
     inner, *matrices = call(
         functools.partial(first_near_kernel, halo), "first_near", [SCALARS] + [WHOLE] * 3,
-        [(COL_Y - 2, width, half, depth), *shapes], [], LONG, heights, own, part_a, part_b, kinds=[BF16, *kinds],
+        [(COL_Y - 2, width, half, depth), *shapes], [], MIDDLE, heights, own, part_a, part_b, kinds=[BF16, *kinds],
     )
     return inner, matrices
 
@@ -474,7 +474,6 @@
     sent_part, cross = lax.optimization_barrier((own_part, cross))
     far_part = lax.ppermute(sent_part, ("space", "chan"), far_pairs(peers, chans))
     cross = lax.ppermute(cross, "space", across_pairs(peers))
-    near_part, mate = lax.optimization_barrier((near_part, mate))
     mate = to_mate(mate)
     if halo:
         fields = with_x_borders(jnp.concatenate([cross, fields, mate[None]], axis=0), peers)

time: 43.6 us -> 44.9 us (1.030)
  the two profiles are of different devices: /device:TPU:1 before, /device:TPU:5 now
where the time goes in v6:
time: 44.9 us; the launch traced here: 44.5 us
  Pallas kernels  29.9 us (67%)
  starting transfers between devices  12.4 us (28%)
  local copies, waits for them, and re-layouts  1.63 us (4%)
    pallas_call x8, Pallas kernels, call(): pl.pallas_call(kernel, out_shape=[jax.ShapeDtypeStruct(*each) for each in...  29.9 us
    ppermute x3, starting transfers between devices, to_mate(): lax.ppermute(value, 'space', [(i, i ^ 1) for i in range(lax.axis_size('sp...  4.52 us
    ppermute x1, starting transfers between devices, on_device(): lax.ppermute(sent_part, ('space', 'chan'), far_pairs(peers, chans))  3.39 us
    ppermute x1, starting transfers between devices, on_device(): cross = lax.ppermute(cross, 'space', across_pairs(peers))  3.15 us
    unnamed x12, local copies, waits for them, and re-layouts  1.63 us
    ppermute x1, starting transfers between devices, on_device(): lax.ppermute(own_part, 'chan', [(c, c ^ 1) for c in range(chans)])  1.36 us
  transfers between devices with their start and end apart: 6, of which 1 were waited for; matrix products, arithmetic and copies ran while one was open for 0% of the time, Pallas kernels for 51%

profile of v6, /device:TPU:5, one launch (start us, length us, event | category | flops | bytes accessed | tf_op | source)
XLA Modules:
  0.0 44.5 jit_solution(15558725716499942490)
XLA Ops:
  0.0 0.1 order.1.after.swap
  0.1 0.6 %copy-done.5 = f32[32]{0:T(128)S(1)} copy-done((f32[32]{0:T(128)S(1)}, f32[32]{0:T(128)}, u32[]{:S(2)}) %copy-start.5) | copy-done | bytes 152
  0.7 0.3 copy-done.4
  1.0 0.1 pack.1.after.part_a
  1.1 1.4 %collective-permute-start.1 = (bf16[28,32,128]{2,1,0:T(8,128)(2,1)S(1)}, bf16[28,32,128]{2,1,0:T(8,128)(2,1)S(1)}, u32[]{:S(2)}, u32[]{:S(2)}) collective-permute-start(bf16[28,32,128]{2,1,0:T(8,128)(2,1)S(1)} %pack.1.after.part_a), channel_id=1, source_target_pairs={{0,1},{1,0},{2,3},{3,2},{4,5},{5,4},{6,7},{7,6},{8,9},{9,8},{10,11... | collective-permute-start | bytes 688136 | tf_op jit(solution)/shard_map/ppermute | solution.py:472
  2.4 0.7 %copy-done = bf16[1,128,8,8,256]{4,3,2,1,0:T(8,128)(2,1)S(1)} copy-done((bf16[1,128,8,8,256]{4,3,2,1,0:T(8,128)(2,1)S(1)}, bf16[1,128,8,8,256]{4,3,2,1,0:T(8,128)(2,1)}, u32[]{:S(2)}) %copy-start) | copy-done | bytes 4194328
  3.1 1.9 %arrange.1 = (bf16[8,8,128,256]{3,2,1,0:T(8,128)(2,1)S(1)}, bf16[2,8,128,256]{3,2,1,0:T(8,128)(2,1)S(1)}, bf16[8,128,256]{2,1,0:T(8,128)(2,1)S(1)}) custom-call(s32[8]{0:T(128)S(1)} %copy-done.2, bf16[1,128,8,8,256]{4,3,2,1,0:T(8,128)(2,1)S(1)} %copy-done, bf16[256,256]{1,0:T(8,128)(2,1)S(1)} %order.1.after.swap, bf16[28,32,128]{2,1,0:T(8,128)(2,1)S(1)} %pack.1.after.part_a), custom_call_target="tpu_custom_call" | custom-call | flops 4096 | bytes 64 | tf_op jit(solution)/shard_map/arrange/pallas_call | solution.py:355
  5.0 0.0 copy-start.1
  5.0 0.0 copy-start.3
  5.0 0.7 %collective-permute-start.2 = (bf16[8,128,256]{2,1,0:T(8,128)(2,1)S(1)}, bf16[8,128,256]{2,1,0:T(8,128)(2,1)S(1)}, u32[]{:S(2)}, u32[]{:S(2)}) collective-permute-start(bf16[8,128,256]{2,1,0:T(8,128)(2,1)S(1)} %get-tuple-element.34), channel_id=1, source_target_pairs={{0,4},{4,0},{8,12},{12,8},{16,20},{20,16},{24,28},{28,24},{1,5},{5... | collective-permute-start | bytes 1572872 | tf_op jit(solution)/shard_map/ppermute | solution.py:451
  5.8 3.1 %collective-permute-start = (bf16[2,8,128,256]{3,2,1,0:T(8,128)(2,1)S(1)}, bf16[2,8,128,256]{3,2,1,0:T(8,128)(2,1)S(1)}, u32[]{:S(2)}, u32[]{:S(2)}) collective-permute-start(bf16[2,8,128,256]{3,2,1,0:T(8,128)(2,1)S(1)} %get-tuple-element.29), channel_id=1, source_target_pairs={{4,8},{8,4},{12,16},{16,12},{20,24},{24,20},{5,9},{9,5},{13,17},{1... | collective-permute-start | bytes 3145736 | tf_op jit(solution)/shard_map/ppermute | solution.py:476
  8.9 3.4 %collective-permute-start.3 = (bf16[28,32,128]{2,1,0:T(8,128)(2,1)S(1)}, bf16[28,32,128]{2,1,0:T(8,128)(2,1)S(1)}, u32[]{:S(2)}, u32[]{:S(2)}) collective-permute-start(bf16[28,32,128]{2,1,0:T(8,128)(2,1)S(1)} %pack.1.after.part_a), channel_id=1, source_target_pairs={{0,2},{1,3},{2,0},{3,1},{4,7},{5,6},{6,5},{7,4},{8,10},{9,11},{10,... | collective-permute-start | bytes 688136 | tf_op jit(solution)/shard_map/ppermute | solution.py:475
  12.3 7.2 %first_near.1 = (bf16[6,8,64,256]{3,2,1,0:T(8,128)(2,1)S(1)}, bf16[192,1152]{1,0:T(8,128)(2,1)S(1)}, bf16[192,768]{1,0:T(8,128)(2,1)S(1)}, bf16[192,768]{1,0:T(8,128)(2,1)S(1)}, f32[64,128]{1,0:T(8,128)S(1)}) custom-call(s32[8]{0:T(128)S(1)} %copy-done.2, bf16[8,8,128,256]{3,2,1,0:T(8,128)(2,1)S(1)} %get-tuple-element.27.own, ...), custom_call_target="tpu_custom_call" | custom-call | flops 2147483648 | bytes 33554432 | tf_op jit(solution)/shard_map/first_near/pallas_call | solution.py:355
  19.6 0.0 collective-permute-done.3.part_a
  19.6 3.4 %collective-permute-start.4 = (bf16[28,32,128]{2,1,0:T(8,128)(2,1)S(1)}, bf16[28,32,128]{2,1,0:T(8,128)(2,1)S(1)}, u32[]{:S(2)}, u32[]{:S(2)}) collective-permute-start(bf16[28,32,128]{2,1,0:T(8,128)(2,1)S(1)} %collective-permute-done.3.part_a), channel_id=1, source_target_pairs={{0,4},{4,0},{8,12},{12,8},{16,20},{20,16},{24,28},{28,24},{1,5},{5... | collective-permute-start | bytes 688136 | tf_op jit(solution)/shard_map/ppermute | solution.py:451
  22.9 0.8 %fill.1 = (bf16[192,1536]{1,0:T(8,128)(2,1)S(1)}, bf16[192,1152]{1,0:T(8,128)(2,1)S(1)}, bf16[192,1152]{1,0:T(8,128)(2,1)S(1)}, f32[64,128]{1,0:T(8,128)S(1)}) custom-call(s32[8]{0:T(128)S(1)} %copy-done.2, bf16[27,32,128]{2,1,0:T(8,128)(2,1)S(1)} %copy-done.1, f32[1,32]{1,0:T(1,128)S(1)} %bitcast.2, bf16[6,8,64,256]{3,2,1,0:T(8,128)(2,1)S(1)} %get-tuple-element.38.after.inner_a), custom_call_target="tpu_custom_call" | custom-call | flops 4096 | bytes 64 | tf_op jit(solution)/shard_map/fill/pallas_call | solution.py:355
  23.8 0.3 collective-permute-done.4.part_b
  24.1 0.0 collective-permute-done.2.mate
  24.1 9.2 %first_far.1 = (bf16[6,8,64,256]{3,2,1,0:T(8,128)(2,1)S(1)}, bf16[8,128,256]{2,1,0:T(8,128)(2,1)S(1)}, bf16[192,1152]{1,0:T(8,128)(2,1)S(1)}, bf16[192,768]{1,0:...) custom-call(s32[8]{0:T(128)S(1)} %copy-done.2, ...), custom_call_target="tpu_custom_call" | custom-call | flops 4096 | bytes 64 | tf_op jit(solution)/shard_map/first_far/pallas_call | solution.py:355
  33.3 0.4 collective-permute-start.5
  33.7 3.7 %second_inner.1.done_inner = bf16[5,8,32,256]{3,2,1,0:T(8,128)(2,1)S(1)} custom-call(s32[8]{0:T(128)S(1)} %copy-done.2, bf16[6,8,64,256]{3,2,1,0:T(8,128)(2,1)S(1)} %get-tuple-element.38.after.inner_a, bf16[6,8,64,256]{3,2,1,0:T(8,128)(2,1)S(1)} %get-tuple-element.44.inner_b, bf16[8,128,256]{2,1,0:T(8,128)(2,1)S(1)} %get-tuple-element.45.row_seven, ...), custom_call_target="tpu_custom_call" | custom-call | flops 4096 | bytes 64 | tf_op jit(solution)/shard_map/second_inner/pallas_call | solution.py:355
  37.4 0.0 collective-permute-done.cross
  37.4 0.0 collective-permute-done.5.mate
  37.4 7.0 %last.1 = bf16[1,32,8,8,256]{4,3,2,1,0:T(8,128)(2,1)} custom-call(s32[8]{0:T(128)S(1)} %copy-done.2, bf16[8,8,128,256]{3,2,1,0:T(8,128)(2,1)S(1)} %get-tuple-element.27.own, bf16[2,8,128,256]{3,2,1,0:T(8,128)(2,1)S(1)} %collective-permute-done.cross, bf16[192,1152]{1,0:T(8,128)(2,1)S(1)} %get-tuple-element.30.near, ...), custom_call_target="tpu_custom_call" | custom-call | flops 4096 | bytes 64 | tf_op jit(solution)/shard_map/last/pallas_call | solution.py:355
  (8 shorter events, 0.0 us)
Async XLA Ops:
  0.0 0.7 %copy-start.5 = (f32[32]{0:T(128)S(1)}, f32[32]{0:T(128)}, u32[]{:S(2)}) copy-start(f32[32]{0:T(128)} %param.9) | copy-start | bytes 388
  0.0 0.9 %copy-start.4 = (bf16[27,32,128]{2,1,0:T(8,128)(2,1)S(1)}, bf16[27,32,128]{2,1,0:T(8,128)(2,1)}, u32[]{:S(2)}) copy-start(bf16[27,32,128]{2,1,0:T(8,128)(2,1)} %weights.2) | copy-start | bytes 663556
  1.0 2.2 %copy-start = (bf16[1,128,8,8,256]{4,3,2,1,0:T(8,128)(2,1)S(1)}, bf16[1,128,8,8,256]{4,3,2,1,0:T(8,128)(2,1)}, u32[]{:S(2)}) copy-start(bf16[1,128,8,8,256]{4,3,2,1,0:T(8,128)(2,1)} %features.1) | copy-start | bytes 12582916
  1.0 2.2 %copy-start.2 = (s32[8]{0:T(128)S(1)}, s32[8]{0:T(128)}, u32[]{:S(2)}) copy-start(s32[8]{0:T(128)} %heights.11) | copy-start | bytes 100
  1.1 11.3 %collective-permute-start.1 = (bf16[28,32,128]{2,1,0:T(8,128)(2,1)S(1)}, bf16[28,32,128]{2,1,0:T(8,128)(2,1)S(1)}, u32[]{:S(2)}, u32[]{:S(2)}) collective-permute-start(bf16[28,32,128]{2,1,0:T(8,128)(2,1)S(1)} %pack.1.after.part_a), channel_id=1, source_target_pairs={{0,1},{1,0},{2,3},{3,2},{4,5},{5,4},{6,7},{7,6},{8,9},{9,8},{10,11... | collective-permute-start | bytes 688136 | tf_op jit(solution)/shard_map/ppermute | solution.py:472
  5.0 17.9 %copy-start.1 = (bf16[27,32,128]{2,1,0:T(8,128)(2,1)S(1)}, bf16[27,32,128]{2,1,0:T(8,128)(2,1)}, u32[]{:S(2)}) copy-start(bf16[27,32,128]{2,1,0:T(8,128)(2,1)} %weights.3) | copy-start | bytes 663556
  5.0 17.9 %copy-start.3 = (f32[32]{0:T(128)S(1)}, f32[32]{0:T(128)}, u32[]{:S(2)}) copy-start(f32[32]{0:T(128)} %param.11) | copy-start | bytes 388
  5.0 19.0 %collective-permute-start.2 = (bf16[8,128,256]{2,1,0:T(8,128)(2,1)S(1)}, bf16[8,128,256]{2,1,0:T(8,128)(2,1)S(1)}, u32[]{:S(2)}, u32[]{:S(2)}) collective-permute-start(bf16[8,128,256]{2,1,0:T(8,128)(2,1)S(1)} %get-tuple-element.34), channel_id=1, source_target_pairs={{0,4},{4,0},{8,12},{12,8},{16,20},{20,16},{24,28},{28,24},{1,5},{5... | collective-permute-start | bytes 1572872 | tf_op jit(solution)/shard_map/ppermute | solution.py:451
  5.8 31.6 %collective-permute-start = (bf16[2,8,128,256]{3,2,1,0:T(8,128)(2,1)S(1)}, bf16[2,8,128,256]{3,2,1,0:T(8,128)(2,1)S(1)}, u32[]{:S(2)}, u32[]{:S(2)}) collective-permute-start(bf16[2,8,128,256]{3,2,1,0:T(8,128)(2,1)S(1)} %get-tuple-element.29), channel_id=1, source_target_pairs={{4,8},{8,4},{12,16},{16,12},{20,24},{24,20},{5,9},{9,5},{13,17},{1... | collective-permute-start | bytes 3145736 | tf_op jit(solution)/shard_map/ppermute | solution.py:476
  8.9 10.6 %collective-permute-start.3 = (bf16[28,32,128]{2,1,0:T(8,128)(2,1)S(1)}, bf16[28,32,128]{2,1,0:T(8,128)(2,1)S(1)}, u32[]{:S(2)}, u32[]{:S(2)}) collective-permute-start(bf16[28,32,128]{2,1,0:T(8,128)(2,1)S(1)} %pack.1.after.part_a), channel_id=1, source_target_pairs={{0,2},{1,3},{2,0},{3,1},{4,7},{5,6},{6,5},{7,4},{8,10},{9,11},{10,... | collective-permute-start | bytes 688136 | tf_op jit(solution)/shard_map/ppermute | solution.py:475
  19.6 4.5 %collective-permute-start.4 = (bf16[28,32,128]{2,1,0:T(8,128)(2,1)S(1)}, bf16[28,32,128]{2,1,0:T(8,128)(2,1)S(1)}, u32[]{:S(2)}, u32[]{:S(2)}) collective-permute-start(bf16[28,32,128]{2,1,0:T(8,128)(2,1)S(1)} %collective-permute-done.3.part_a), channel_id=1, source_target_pairs={{0,4},{4,0},{8,12},{12,8},{16,20},{20,16},{24,28},{28,24},{1,5},{5... | collective-permute-start | bytes 688136 | tf_op jit(solution)/shard_map/ppermute | solution.py:451
  33.3 4.1 %collective-permute-start.5 = (bf16[8,128,256]{2,1,0:T(8,128)(2,1)S(1)}, bf16[8,128,256]{2,1,0:T(8,128)(2,1)S(1)}, u32[]{:S(2)}, u32[]{:S(2)}) collective-permute-start(bf16[8,128,256]{2,1,0:T(8,128)(2,1)S(1)} %get-tuple-element.45.row_seven), channel_id=1, source_target_pairs={{0,4},{4,0},{8,12},{12,8},{16,20},{20,16},{24,28},{28,24},{1,5},{5... | collective-permute-start | bytes 1572872 | tf_op jit(solution)/shard_map/ppermute | solution.py:451

commit v7 on v5

--- a/solution.py
+++ b/solution.py
@@ -87,14 +87,11 @@
             mate[x, first : first + group] = moved[COL_Y - 1]
 
 
-def finish(partial, bias, live_top, columns=1):
-    rows, lanes = partial.shape[0] // TAPS, partial.shape[1]
-    depth = lanes // columns
-    z = lax.broadcasted_iota(jnp.int32, (rows, lanes), 1)
-    if columns > 1:
-        z = lax.rem(z, depth)
+def finish(partial, bias, live_top):
+    rows, depth = partial.shape[0] // TAPS, partial.shape[1]
+    z = lax.broadcasted_iota(jnp.int32, (rows, depth), 1)
     below = jnp.where(z == 0, 0.0, pltpu.roll(partial[:rows], 1, 1))
-    above = jnp.where(z == depth - 1, 0.0, pltpu.roll(partial[2 * rows :], lanes - 1, 1))
+    above = jnp.where(z == depth - 1, 0.0, pltpu.roll(partial[2 * rows :], depth - 1, 1))
     total = jnp.maximum(below + partial[rows : 2 * rows] + above + bias, 0.0)
     return jnp.where(z < live_top, total, 0.0).astype(BF16)
 
@@ -124,35 +121,25 @@
     return max(x - 1 + pad, 0), min(x + width + 1 + pad, stored)
 
 
-def first_row(get, stored, halo, matrices, bias, top):
+def first_sums(get, stored, halo, matrices, taps=range(TAPS)):
     for x in range(-halo, COL_Y + halo):
         low, high = reach(x, 1, stored, 2 * halo)
         lhs = matrices[0]
         if high - low == 2:
             lhs = matrices[1] if x == 0 else matrices[2]
-        taken = jnp.concatenate([get(j, low, high) for j in range(TAPS)], axis=0)
-        partial = jnp.dot(lhs[...], taken, preferred_element_type=F32)
-        side = -1 if x < 0 else 1 if x >= COL_Y else 0
-        yield x + halo, finish(partial, bias[:, 0:1], top(side))
-
-
-def first_row_low(get, stored, halo, matrices, bias, top, levels):
-    channels = matrices[0].shape[1] // TAPS**2
-
-    def field(j, x):
-        return get(j, x, x + 1)[:, :levels] if 0 <= x < stored else jnp.zeros((channels, levels), BF16)
-
-    for x in range(-halo, COL_Y + halo, 2):
-        at = x + 2 * halo
-        taken = [
-            jnp.concatenate([field(j, at + more + i - 1) for j in range(TAPS) for i in range(TAPS)], axis=0) for more in range(2)
-        ]
-        partial = jnp.dot(matrices[0][...], jnp.concatenate(taken, axis=1), preferred_element_type=F32)
-        sides = [-1 if each < 0 else 1 if each >= COL_Y else 0 for each in (x, x + 1)]
-        tops = jnp.where(lax.broadcasted_iota(jnp.int32, (1, 2 * levels), 1) < levels, top(sides[0]), top(sides[1]))
-        done = finish(partial, bias[:, 0:1], tops, columns=2)
-        yield x + halo, done[:, :levels]
-        yield x + halo + 1, done[:, levels:]
+        wide = lhs.shape[1] // TAPS
+        taken = jnp.concatenate([get(j, low, high) for j in taps], axis=0)
+        columns = slice(taps[0] * wide, (taps[-1] + 1) * wide)
+        yield x, jnp.dot(lhs[:, columns], taken, preferred_element_type=F32)
+
+
+def first_row(get, stored, halo, matrices, bias, top):
+    for x, partial in first_sums(get, stored, halo, matrices):
+        yield x + halo, finish(partial, bias[:, 0:1], top(side_of(x)))
+
+
+def side_of(x):
+    return -1 if x < 0 else 1 if x >= COL_Y else 0
 
 
 def span_of(ref, *at):
@@ -190,7 +177,9 @@
     def get(j, a, b):
         return span_of(mate, a, b) if j == 2 else span_of(own, COL_Y - 2 + j, a, b)
 
-    whole_row(get, own.shape[1], halo, ((near, low_near, high_near), bias_near), (far, bias), place.top, out_last)
+    matrices, biases = join(((near, low_near, high_near), bias_near), (far, bias))
+    for x, done in first_row(get, own.shape[1], halo, matrices, biases, place.top):
+        out_last[x] = done
 
 
 class Joined:
@@ -198,21 +187,15 @@
         self.near, self.far = near, far
         self.shape = (2 * near.shape[0], near.shape[1])
 
-    def __getitem__(self, _):
+    def __getitem__(self, at):
+        columns = at[1]
         rows = self.near.shape[0] // TAPS
-        pieces = [ref[k * rows : (k + 1) * rows] for k in range(TAPS) for ref in (self.near, self.far)]
+        pieces = [ref[k * rows : (k + 1) * rows, columns] for k in range(TAPS) for ref in (self.near, self.far)]
         return jnp.concatenate(pieces, axis=0)
 
 
-def whole_row(get, stored, halo, near, far, top, out, *at, levels=None):
-    matrices = [Joined(*each) for each in zip(near[0], far[0], strict=True)]
-    bias = jnp.concatenate([near[1][...], far[1][...]], axis=0)
-    if levels is None:
-        for x, done in first_row(get, stored, halo, matrices, bias, top):
-            out[(*at, x)] = done
-    else:
-        for x, done in first_row_low(get, stored, halo, matrices, bias, top, levels):
-            out[(*at, x, slice(None), slice(0, levels))] = done
+def join(near, far):
+    return [Joined(*each) for each in zip(near[0], far[0], strict=True)], jnp.concatenate([near[1][...], far[1][...]], axis=0)
 
 
 def fill_second(weights, place, matrix, low_matrix, high_matrix):
@@ -278,59 +261,48 @@
             out[u - 2, x + 1] = beside
 
 
+def ahead_kernel(
+    halo, heights, own, near, low_near, high_near, bias_near, far, low_far, high_far, bias_far,
+    inner_a, inner_b, row_seven, mate, matrix_two, low_two, high_two, both, done_seven, sums_before, sums_zero,
+):
+    matrices, _ = join(((near, low_near, high_near), bias_near), ((far, low_far, high_far), bias_far))
+    width = own.shape[1]
+    for x, sums in first_sums(lambda j, a, b: span_of(own, j - 2, a, b), width, halo, matrices, (2,)):
+        sums_before[x + halo] = sums
+    for x, sums in first_sums(lambda j, a, b: span_of(own, j - 1, a, b), width, halo, matrices, (1, 2)):
+        sums_zero[x + halo] = sums
+
+    def get(j, a, b):
+        return halves(inner_a, inner_b, 5, a, b) if j == 0 else [(row_seven if j == 1 else mate)[x] for x in range(a, b)]
+
+    two = (matrix_two, low_two, high_two)
+    for x, here, beside in second_row(get, inner_a.shape[1], halo, two, both[:, 0:1], Place(heights).top()):
+        done_seven[x] = here
+        done_seven[x + 1] = beside
+
+
 def last_kernel(
-    halo, heights, own, cross, near, low_near, high_near, bias_near, far, low_far, high_far, bias_far,
-    inner_a, inner_b, row_seven, mate, done_inner, matrix_two, low_two, high_two, both, out, edge, done_edge, result, sems,
+    halo, heights, cross, near, low_near, high_near, bias_near, far, low_far, high_far, bias_far, sums_before, sums_zero,
+    inner_a, inner_b, done_inner, done_seven, matrix_two, low_two, high_two, both, out, edge, done_edge, result, sems,
 ):
     place = Place(heights)
-    width, depth = own.shape[1], own.shape[3]
-    near, far = ((near, low_near, high_near), bias_near), ((far, low_far, high_far), bias_far)
-
-    def fields(u, a, b):
-        return span_of(own, u, a, b) if u >= 0 else span_of(cross, -1 - u, a, b)
-
-    def edge_row(u, levels=None):
-        def top(side):
-            return place.top(side, across=u < 0)
-
-        whole_row(lambda j, a, b: fields(u - 1 + j, a, b), width, halo, near, far, top, edge, u + 1, levels=levels)
-
-    part = 128
-    needed = jnp.minimum(place.top(0, across=True), place.top() + 1)
-    if halo:
-        wide = jnp.maximum(place.top(-1, across=True), place.top(1, across=True))
-        needed = jnp.maximum(needed, jnp.minimum(wide, place.top() + 1))
-    low = needed < part if depth > part else False
-
-    @pl.when(low)
-    def _():
-        edge_row(-1, part)
-        edge[0, :, :, part:] = jnp.zeros((*edge.shape[1:3], depth - part), BF16)
-
-    @pl.when(jnp.logical_not(low))
-    def _():
-        edge_row(-1)
-
-    edge_row(0)
+    width, depth = cross.shape[1], cross.shape[3]
+    matrices, biases = join(((near, low_near, high_near), bias_near), ((far, low_far, high_far), bias_far))
+    for u, sums_own, taps in ((-1, sums_before, (0, 1)), (0, sums_zero, (0,))):
+        for x, sums in first_sums(lambda j, a, b: span_of(cross, -u - j, a, b), width, halo, matrices, taps):
+            top = place.top(side_of(x), across=u < 0)
+            edge[u + 1, x + halo] = finish(sums + sums_own[x + halo], biases[:, 0:1], top)
 
     def row(u, a, b):
-        if u < 1:
-            return [edge[u + 1, x] for x in range(a, b)]
-        if u < 7:
-            return halves(inner_a, inner_b, u - 1, a, b)
-        return [(row_seven if u == 7 else mate)[x] for x in range(a, b)]
-
-    for at, u in enumerate((0, 1, 7)):
+        return [edge[u + 1, x] for x in range(a, b)] if u < 1 else halves(inner_a, inner_b, u - 1, a, b)
+
+    two = (matrix_two, low_two, high_two)
+    for u in (0, 1):
         for x, here, beside in second_row(
-            lambda j, a, b: row(u - 1 + j, a, b),
-            inner_a.shape[1],
-            halo,
-            (matrix_two, low_two, high_two),
-            both[:, 0:1],
-            place.top(),
+            lambda j, a, b: row(u - 1 + j, a, b), inner_a.shape[1], halo, two, both[:, 0:1], place.top()
         ):
-            done_edge[at, x] = here
-            done_edge[at, x + 1] = beside
+            done_edge[u, x] = here
+            done_edge[u, x + 1] = beside
     quarter = out.shape[1]
     size = quarter * COL_Y
     at_row = lax.broadcasted_iota(jnp.int32, (size, size), 0)
@@ -339,7 +311,7 @@
     u = jnp.where(place.odd == 1, COL_Y - 1 - y, y)
     swap = (at_column == u * quarter + lax.div(at_row, COL_Y)).astype(F32).astype(BF16)
     for x in range(COL_Y):
-        tiles = [done_edge[0, x], done_edge[1, x]] + [done_inner[v, x] for v in range(COL_Y - 3)] + [done_edge[2, x]]
+        tiles = [done_edge[0, x], done_edge[1, x]] + [done_inner[v, x] for v in range(COL_Y - 3)] + [done_seven[x]]
         tile = jnp.concatenate(tiles, axis=0)
         moved = jnp.dot(swap, tile, preferred_element_type=F32).astype(BF16)
         result[x] = moved.reshape(quarter, COL_Y, depth)
@@ -427,13 +399,23 @@
     return call(kernel, "second_inner", [SCALARS] + [WHOLE] * (len(args) - 1), outputs, [], SHORT, *args)[0]
 
 
-def last(halo, heights, own, cross, near, far, hidden, done_inner, matrices):
+def ahead(halo, heights, own, near, far, hidden, matrices):
     _, _, channels, depth = own.shape
     quarter, width = matrices[-1].shape[0] // 2, COL_Y + 2 * halo
-    scratch = [pltpu.VMEM((2, width, channels, depth), BF16), pltpu.VMEM((3, COL_Y, quarter, depth), BF16)]
+    sums = (width, TAPS * channels, depth)
+    args = (heights, own, *near, *far, *hidden, *matrices)
+    kernel = functools.partial(ahead_kernel, halo)
+    outputs, kinds = [(COL_Y, quarter, depth), sums, sums], [BF16, F32, F32]
+    return call(kernel, "ahead", [SCALARS] + [WHOLE] * (len(args) - 1), outputs, [], SHORT, *args, kinds=kinds)
+
+
+def last(halo, heights, cross, near, far, sums, inner, done, matrices):
+    _, _, channels, depth = cross.shape
+    quarter, width = matrices[-1].shape[0] // 2, COL_Y + 2 * halo
+    scratch = [pltpu.VMEM((2, width, channels, depth), BF16), pltpu.VMEM((2, COL_Y, quarter, depth), BF16)]
     scratch += [pltpu.VMEM((COL_Y, quarter, COL_Y, depth), BF16), pltpu.SemaphoreType.DMA((COL_Y,))]
     outputs = [(1, quarter, COL_Y, COL_Y, depth)]
-    args = (heights, own, cross, *near, *far, *hidden, done_inner, *matrices)
+    args = (heights, cross, *near, *far, *sums, *inner, *done, *matrices)
     kernel = functools.partial(last_kernel, halo)
     return call(kernel, "last", [SCALARS] + [WHOLE] * (len(args) - 1), outputs, scratch, SHORT, *args, place=ANY)[0]
 
@@ -471,8 +453,7 @@
     own_part = pack(weight_one, bias_one, swap)
     near_part = lax.ppermute(own_part, "chan", [(c, c ^ 1) for c in range(chans)])
     fields, cross, mate = arrange(column_heights, features, swap, own_part)
-    sent_part, cross = lax.optimization_barrier((own_part, cross))
-    far_part = lax.ppermute(sent_part, ("space", "chan"), far_pairs(peers, chans))
+    far_part = lax.ppermute(own_part, ("space", "chan"), far_pairs(peers, chans))
     cross = lax.ppermute(cross, "space", across_pairs(peers))
     near_part, mate = lax.optimization_barrier((near_part, mate))
     mate = to_mate(mate)
@@ -487,8 +468,9 @@
     inner_b, row_seven, far = first_far(halo, column_heights, fields, mate, far_part, other_part, near, matrices[-1])
     mate = to_mate(row_seven)
     done_inner = second_inner(halo, column_heights, inner_a, inner_b, row_seven, matrices)
-    hidden = (inner_a, inner_b, row_seven, mate)
-    return last(halo, column_heights, fields, cross, near, far, hidden, done_inner, matrices)
+    done_seven, *sums = ahead(halo, column_heights, fields, near, far, (inner_a, inner_b, row_seven, mate), matrices)
+    done = (done_inner, done_seven)
+    return last(halo, column_heights, cross, near, far, sums, (inner_a, inner_b), done, matrices)
 
 
 def solution(mesh):

time: 43.6 us -> 44.1 us (1.011)
  waiting for transfers between devices: 2.1 us -> 0.65 us
  Pallas kernels: 29.9 us -> 31.2 us
    ppermute x1, starting transfers between devices: 4.11 us -> 2.19 us  [on_device(): lax.ppermute(own_part, ('space', 'chan'), far_pairs(peers, chans))]
    ppermute x1, waiting for transfers between devices: 1.8 us -> 0.01 us  [on_device(): cross = lax.ppermute(cross, 'space', across_pairs(peers))]
    ppermute x1, starting transfers between devices: 2.94 us -> 4.35 us  [on_device(): cross = lax.ppermute(cross, 'space', across_pairs(peers))]
    pallas_call x8 -> x9, Pallas kernels: 29.9 us -> 31.2 us  [call(): pl.pallas_call(kernel, out_shape=[jax.ShapeDtypeStruct(*each) for each in...]
    ppermute x3, starting transfers between devices: 1.04 us -> 1.96 us  [to_mate(): lax.ppermute(value, 'space', [(i, i ^ 1) for i in range(lax.axis_size('sp...]
  transfers between devices with their start and end apart: 6 -> 6, of which waited for: 2 -> 1; matrix products, arithmetic and copies ran while one was open for 0% -> 0% of each run, Pallas kernels for 52% -> 59%
where the time goes in v7:
time: 44.1 us; the launch traced here: 43.7 us
  Pallas kernels  31.2 us (71%)
  starting transfers between devices  10.7 us (24%)
  local copies, waits for them, and re-layouts  0.89 us (2%)
  waiting for transfers between devices  0.65 us (1%)
    pallas_call x9, Pallas kernels, call(): pl.pallas_call(kernel, out_shape=[jax.ShapeDtypeStruct(*each) for each in...  31.2 us
    ppermute x1, starting transfers between devices, on_device(): cross = lax.ppermute(cross, 'space', across_pairs(peers))  4.35 us
    ppermute x1, starting transfers between devices, on_device(): lax.ppermute(own_part, ('space', 'chan'), far_pairs(peers, chans))  2.19 us
    ppermute x1, starting transfers between devices, on_device(): lax.ppermute(own_part, 'chan', [(c, c ^ 1) for c in range(chans)])  2.19 us
    ppermute x3, starting transfers between devices, to_mate(): lax.ppermute(value, 'space', [(i, i ^ 1) for i in range(lax.axis_size('sp...  1.96 us
    unnamed x12, local copies, waits for them, and re-layouts  0.89 us
  transfers between devices with their start and end apart: 6, of which 1 were waited for; matrix products, arithmetic and copies ran while one was open for 0% of the time, Pallas kernels for 59%

profile of v7, /device:TPU:1, one launch (start us, length us, event | category | flops | bytes accessed | tf_op | source)
XLA Modules:
  0.0 43.7 jit_solution(14691579652267656305)
XLA Ops:
  0.0 0.1 order.1.after.swap
  0.1 0.9 %copy-done.4 = bf16[27,32,128]{2,1,0:T(8,128)(2,1)S(1)} copy-done((bf16[27,32,128]{2,1,0:T(8,128)(2,1)S(1)}, bf16[27,32,128]{2,1,0:T(8,128)(2,1)}, u32[]{:S(2)}) %copy-start.4) | copy-done | bytes 221208
  0.9 0.0 copy-done.5
  0.9 0.1 pack.1.after.part_a
  1.0 2.2 %collective-permute-start.1 = (bf16[28,32,128]{2,1,0:T(8,128)(2,1)S(1)}, bf16[28,32,128]{2,1,0:T(8,128)(2,1)S(1)}, u32[]{:S(2)}, u32[]{:S(2)}) collective-permute-start(bf16[28,32,128]{2,1,0:T(8,128)(2,1)S(1)} %pack.1.after.part_a), channel_id=1, source_target_pairs={{0,1},{1,0},{2,3},{3,2},{4,5},{5,4},{6,7},{7,6},{8,9},{9,8},{10,11... | collective-permute-start | bytes 688136 | tf_op jit(solution)/shard_map/ppermute | solution.py:454
  3.2 2.2 %collective-permute-start.3 = (bf16[28,32,128]{2,1,0:T(8,128)(2,1)S(1)}, bf16[28,32,128]{2,1,0:T(8,128)(2,1)S(1)}, u32[]{:S(2)}, u32[]{:S(2)}) collective-permute-start(bf16[28,32,128]{2,1,0:T(8,128)(2,1)S(1)} %pack.1.after.part_a), channel_id=1, source_target_pairs={{0,2},{1,3},{2,0},{3,1},{4,7},{5,6},{6,5},{7,4},{8,10},{9,11},{10,... | collective-permute-start | bytes 688136 | tf_op jit(solution)/shard_map/ppermute | solution.py:456
  5.4 0.0 copy-done.2
  5.4 1.9 %arrange.1 = (bf16[8,8,128,256]{3,2,1,0:T(8,128)(2,1)S(1)}, bf16[2,8,128,256]{3,2,1,0:T(8,128)(2,1)S(1)}, bf16[8,128,256]{2,1,0:T(8,128)(2,1)S(1)}) custom-call(s32[8]{0:T(128)S(1)} %copy-done.2, bf16[1,128,8,8,256]{4,3,2,1,0:T(8,128)(2,1)S(1)} %copy-done, bf16[256,256]{1,0:T(8,128)(2,1)S(1)} %order.1.after.swap, bf16[28,32,128]{2,1,0:T(8,128)(2,1)S(1)} %pack.1.after.part_a), custom_call_target="tpu_custom_call" | custom-call | flops 4096 | bytes 64 | tf_op jit(solution)/shard_map/arrange/pallas_call | solution.py:327
  7.3 4.4 %collective-permute-start = (bf16[2,8,128,256]{3,2,1,0:T(8,128)(2,1)S(1)}, bf16[2,8,128,256]{3,2,1,0:T(8,128)(2,1)S(1)}, u32[]{:S(2)}, u32[]{:S(2)}) collective-permute-start(bf16[2,8,128,256]{3,2,1,0:T(8,128)(2,1)S(1)} %get-tuple-element.30), channel_id=1, source_target_pairs={{4,8},{8,4},{12,16},{16,12},{20,24},{24,20},{5,9},{9,5},{13,17},{1... | collective-permute-start | bytes 3145736 | tf_op jit(solution)/shard_map/ppermute | solution.py:457
  11.7 0.0 collective-permute-done.1.part_b
  11.7 1.7 %collective-permute-start.2 = (bf16[8,128,256]{2,1,0:T(8,128)(2,1)S(1)}, bf16[8,128,256]{2,1,0:T(8,128)(2,1)S(1)}, u32[]{:S(2)}, u32[]{:S(2)}) collective-permute-start(bf16[8,128,256]{2,1,0:T(8,128)(2,1)S(1)} %get-tuple-element.38), channel_id=1, source_target_pairs={{0,4},{4,0},{8,12},{12,8},{16,20},{20,16},{24,28},{28,24},{1,5},{5... | collective-permute-start | bytes 1572872 | tf_op jit(solution)/shard_map/ppermute | solution.py:433
  13.3 7.1 %first_near.1 = (bf16[6,8,64,256]{3,2,1,0:T(8,128)(2,1)S(1)}, bf16[192,1152]{1,0:T(8,128)(2,1)S(1)}, bf16[192,768]{1,0:T(8,128)(2,1)S(1)}, bf16[192,768]{1,0:T(8,128)(2,1)S(1)}, f32[64,128]{1,0:T(8,128)S(1)}) custom-call(s32[8]{0:T(128)S(1)} %copy-done.2, bf16[8,8,128,256]{3,2,1,0:T(8,128)(2,1)S(1)} %get-tuple-element.31.own, ...), custom_call_target="tpu_custom_call" | custom-call | flops 8589934592 | bytes 134217728 | tf_op jit(solution)/shard_map/first_near/pallas_call | solution.py:327
  20.5 0.0 collective-permute-done.3.part_a
  20.5 0.1 collective-permute-start.4
  20.6 0.8 %fill.1 = (bf16[192,1536]{1,0:T(8,128)(2,1)S(1)}, bf16[192,1152]{1,0:T(8,128)(2,1)S(1)}, bf16[192,1152]{1,0:T(8,128)(2,1)S(1)}, f32[64,128]{1,0:T(8,128)S(1)}) custom-call(s32[8]{0:T(128)S(1)} %copy-done.2, bf16[27,32,128]{2,1,0:T(8,128)(2,1)S(1)} %copy-done.1, f32[1,32]{1,0:T(1,128)S(1)} %bitcast.2, bf16[6,8,64,256]{3,2,1,0:T(8,128)(2,1)S(1)} %get-tuple-element.41.after.inner_a), custom_call_target="tpu_custom_call" | custom-call | flops 4096 | bytes 64 | tf_op jit(solution)/shard_map/fill/pallas_call | solution.py:327
  21.4 0.6 %collective-permute-done.4.part_b = bf16[28,32,128]{2,1,0:T(8,128)(2,1)S(1)} collective-permute-done((bf16[28,32,128]{2,1,0:T(8,128)(2,1)S(1)}, bf16[28,32,128]{2,1,0:T(8,128)(2,1)S(1)}, u32[]{:S(2)}, u32[]{:S(2)}) %collective-permute-start.4) | collective-permute-done | bytes 229408 | tf_op jit(solution)/shard_map/ppermute | solution.py:433
  22.0 0.0 collective-permute-done.2.mate
  22.0 9.3 %first_far.1 = (bf16[6,8,64,256]{3,2,1,0:T(8,128)(2,1)S(1)}, bf16[8,128,256]{2,1,0:T(8,128)(2,1)S(1)}, bf16[192,1152]{1,0:T(8,128)(2,1)S(1)}, bf16[192,768]{1,0:...) custom-call(s32[8]{0:T(128)S(1)} %copy-done.2, ...), custom_call_target="tpu_custom_call" | custom-call | flops 4096 | bytes 64 | tf_op jit(solution)/shard_map/first_far/pallas_call | solution.py:327
  31.4 0.2 collective-permute-start.5
  31.6 3.6 %second_inner.1.done_inner = bf16[5,8,32,256]{3,2,1,0:T(8,128)(2,1)S(1)} custom-call(s32[8]{0:T(128)S(1)} %copy-done.2, bf16[6,8,64,256]{3,2,1,0:T(8,128)(2,1)S(1)} %get-tuple-element.41.after.inner_a, bf16[6,8,64,256]{3,2,1,0:T(8,128)(2,1)S(1)} %get-tuple-element.47.inner_b, bf16[8,128,256]{2,1,0:T(8,128)(2,1)S(1)} %get-tuple-element.48.row_seven, ...), custom_call_target="tpu_custom_call" | custom-call | flops 4096 | bytes 64 | tf_op jit(solution)/shard_map/second_inner/pallas_call | solution.py:327
  35.2 0.0 collective-permute-done.5.mate
  35.2 3.2 %ahead.1 = (bf16[8,32,256]{2,1,0:T(8,128)(2,1)S(1)}, f32[8,384,256]{2,1,0:T(8,128)S(1)}, f32[8,384,256]{2,1,0:T(8,128)S(1)}) custom-call(s32[8]{0:T(128)S(1)} %copy-done.2, bf16[8,8,128,256]{3,2,1,0:T(8,128)(2,1)S(1)} %get-tuple-element.31.own, bf16[192,1152]{1,0:T(8,128)(2,1)S(1)} %get-tuple-element.34.near, ...), custom_call_target="tpu_custom_call" | custom-call | flops 4096 | bytes 64 | tf_op jit(solution)/shard_map/ahead/pallas_call | solution.py:327
  38.5 0.0 collective-permute-done.cross
  38.5 5.0 %last.1 = bf16[1,32,8,8,256]{4,3,2,1,0:T(8,128)(2,1)} custom-call(s32[8]{0:T(128)S(1)} %copy-done.2, bf16[2,8,128,256]{3,2,1,0:T(8,128)(2,1)S(1)} %collective-permute-done.cross, bf16[192,1152]{1,0:T(8,128)(2,1)S(1)} %get-tuple-element.34.near, bf16[192,768]{1,0:T(8,128)(2,1)S(1)} %get-tuple-element.35.low_near, ...), custom_call_target="tpu_custom_call" | custom-call | flops 4096 | bytes 64 | tf_op jit(solution)/shard_map/last/pallas_call | solution.py:327
  (9 shorter events, 0.0 us)
Async XLA Ops:
  0.0 0.9 %copy-start.4 = (bf16[27,32,128]{2,1,0:T(8,128)(2,1)S(1)}, bf16[27,32,128]{2,1,0:T(8,128)(2,1)}, u32[]{:S(2)}) copy-start(bf16[27,32,128]{2,1,0:T(8,128)(2,1)} %weights.2) | copy-start | bytes 663556
  0.0 0.9 %copy-start.5 = (f32[32]{0:T(128)S(1)}, f32[32]{0:T(128)}, u32[]{:S(2)}) copy-start(f32[32]{0:T(128)} %param.9) | copy-start | bytes 388
  0.9 4.5 %copy-start = (bf16[1,128,8,8,256]{4,3,2,1,0:T(8,128)(2,1)S(1)}, bf16[1,128,8,8,256]{4,3,2,1,0:T(8,128)(2,1)}, u32[]{:S(2)}) copy-start(bf16[1,128,8,8,256]{4,3,2,1,0:T(8,128)(2,1)} %features.1) | copy-start | bytes 12582916
  0.9 4.5 %copy-start.2 = (s32[8]{0:T(128)S(1)}, s32[8]{0:T(128)}, u32[]{:S(2)}) copy-start(s32[8]{0:T(128)} %heights.13) | copy-start | bytes 100
  1.0 10.6 %collective-permute-start.1 = (bf16[28,32,128]{2,1,0:T(8,128)(2,1)S(1)}, bf16[28,32,128]{2,1,0:T(8,128)(2,1)S(1)}, u32[]{:S(2)}, u32[]{:S(2)}) collective-permute-start(bf16[28,32,128]{2,1,0:T(8,128)(2,1)S(1)} %pack.1.after.part_a), channel_id=1, source_target_pairs={{0,1},{1,0},{2,3},{3,2},{4,5},{5,4},{6,7},{7,6},{8,9},{9,8},{10,11... | collective-permute-start | bytes 688136 | tf_op jit(solution)/shard_map/ppermute | solution.py:454
  3.2 17.2 %collective-permute-start.3 = (bf16[28,32,128]{2,1,0:T(8,128)(2,1)S(1)}, bf16[28,32,128]{2,1,0:T(8,128)(2,1)S(1)}, u32[]{:S(2)}, u32[]{:S(2)}) collective-permute-start(bf16[28,32,128]{2,1,0:T(8,128)(2,1)S(1)} %pack.1.after.part_a), channel_id=1, source_target_pairs={{0,2},{1,3},{2,0},{3,1},{4,7},{5,6},{6,5},{7,4},{8,10},{9,11},{10,... | collective-permute-start | bytes 688136 | tf_op jit(solution)/shard_map/ppermute | solution.py:456
  7.3 31.2 %collective-permute-start = (bf16[2,8,128,256]{3,2,1,0:T(8,128)(2,1)S(1)}, bf16[2,8,128,256]{3,2,1,0:T(8,128)(2,1)S(1)}, u32[]{:S(2)}, u32[]{:S(2)}) collective-permute-start(bf16[2,8,128,256]{3,2,1,0:T(8,128)(2,1)S(1)} %get-tuple-element.30), channel_id=1, source_target_pairs={{4,8},{8,4},{12,16},{16,12},{20,24},{24,20},{5,9},{9,5},{13,17},{1... | collective-permute-start | bytes 3145736 | tf_op jit(solution)/shard_map/ppermute | solution.py:457
  11.7 10.4 %collective-permute-start.2 = (bf16[8,128,256]{2,1,0:T(8,128)(2,1)S(1)}, bf16[8,128,256]{2,1,0:T(8,128)(2,1)S(1)}, u32[]{:S(2)}, u32[]{:S(2)}) collective-permute-start(bf16[8,128,256]{2,1,0:T(8,128)(2,1)S(1)} %get-tuple-element.38), channel_id=1, source_target_pairs={{0,4},{4,0},{8,12},{12,8},{16,20},{20,16},{24,28},{28,24},{1,5},{5... | collective-permute-start | bytes 1572872 | tf_op jit(solution)/shard_map/ppermute | solution.py:433
  13.3 7.2 %copy-start.1 = (bf16[27,32,128]{2,1,0:T(8,128)(2,1)S(1)}, bf16[27,32,128]{2,1,0:T(8,128)(2,1)}, u32[]{:S(2)}) copy-start(bf16[27,32,128]{2,1,0:T(8,128)(2,1)} %weights.3) | copy-start | bytes 663556
  13.3 7.2 %copy-start.3 = (f32[32]{0:T(128)S(1)}, f32[32]{0:T(128)}, u32[]{:S(2)}) copy-start(f32[32]{0:T(128)} %param.11) | copy-start | bytes 388
  20.5 1.6 %collective-permute-start.4 = (bf16[28,32,128]{2,1,0:T(8,128)(2,1)S(1)}, bf16[28,32,128]{2,1,0:T(8,128)(2,1)S(1)}, u32[]{:S(2)}, u32[]{:S(2)}) collective-permute-start(bf16[28,32,128]{2,1,0:T(8,128)(2,1)S(1)} %collective-permute-done.3.part_a), channel_id=1, source_target_pairs={{0,4},{4,0},{8,12},{12,8},{16,20},{20,16},{24,28},{28,24},{1,5},{5... | collective-permute-start | bytes 688136 | tf_op jit(solution)/shard_map/ppermute | solution.py:433
  31.4 3.9 %collective-permute-start.5 = (bf16[8,128,256]{2,1,0:T(8,128)(2,1)S(1)}, bf16[8,128,256]{2,1,0:T(8,128)(2,1)S(1)}, u32[]{:S(2)}, u32[]{:S(2)}) collective-permute-start(bf16[8,128,256]{2,1,0:T(8,128)(2,1)S(1)} %get-tuple-element.48.row_seven), channel_id=1, source_target_pairs={{0,4},{4,0},{8,12},{12,8},{16,20},{20,16},{24,28},{28,24},{1,5},{5... | collective-permute-start | bytes 1572872 | tf_op jit(solution)/shard_map/ppermute | solution.py:433

commit v8 on v7

--- a/solution.py
+++ b/solution.py
@@ -248,23 +248,21 @@
     fill_bias(bias, both)
 
 
-def second_inner_kernel(halo, heights, inner_a, inner_b, row_seven, matrix, low_matrix, high_matrix, both, out):
-    place = Place(heights)
-    matrices, width, top = (matrix, low_matrix, high_matrix), inner_a.shape[1], place.top()
+def second_inner_kernel(
+    halo, heights, own, near, low_near, high_near, bias_near, far, low_far, high_far, bias_far,
+    inner_a, inner_b, row_seven, matrix, low_matrix, high_matrix, both, out, sums_before, sums_zero,
+):
+    top = Place(heights).top()
+    two = (matrix, low_matrix, high_matrix)
 
     def row(u, a, b):
         return halves(inner_a, inner_b, u - 1, a, b) if u < 7 else [row_seven[x] for x in range(a, b)]
 
     for u in range(2, 7):
-        for x, here, beside in second_row(lambda j, a, b: row(u - 1 + j, a, b), width, halo, matrices, both[:, 0:1], top):
+        for x, here, beside in second_row(lambda j, a, b: row(u - 1 + j, a, b), inner_a.shape[1], halo, two, both[:, 0:1], top):
             out[u - 2, x] = here
             out[u - 2, x + 1] = beside
 
-
-def ahead_kernel(
-    halo, heights, own, near, low_near, high_near, bias_near, far, low_far, high_far, bias_far,
-    inner_a, inner_b, row_seven, mate, matrix_two, low_two, high_two, both, done_seven, sums_before, sums_zero,
-):
     matrices, _ = join(((near, low_near, high_near), bias_near), ((far, low_far, high_far), bias_far))
     width = own.shape[1]
     for x, sums in first_sums(lambda j, a, b: span_of(own, j - 2, a, b), width, halo, matrices, (2,)):
@@ -272,18 +270,10 @@
     for x, sums in first_sums(lambda j, a, b: span_of(own, j - 1, a, b), width, halo, matrices, (1, 2)):
         sums_zero[x + halo] = sums
 
-    def get(j, a, b):
-        return halves(inner_a, inner_b, 5, a, b) if j == 0 else [(row_seven if j == 1 else mate)[x] for x in range(a, b)]
-
-    two = (matrix_two, low_two, high_two)
-    for x, here, beside in second_row(get, inner_a.shape[1], halo, two, both[:, 0:1], Place(heights).top()):
-        done_seven[x] = here
-        done_seven[x + 1] = beside
-
 
 def last_kernel(
-    halo, heights, cross, near, low_near, high_near, bias_near, far, low_far, high_far, bias_far, sums_before, sums_zero,
-    inner_a, inner_b, done_inner, done_seven, matrix_two, low_two, high_two, both, out, edge, done_edge, result, sems,
+    halo, heights, own, cross, near, low_near, high_near, bias_near, far, low_far, high_far, bias_far, sums_before, sums_zero,
+    inner_a, inner_b, row_seven, mate, done_inner, matrix_two, low_two, high_two, both, out, edge, done_edge, result, sems,
 ):
     place = Place(heights)
     width, depth = cross.shape[1], cross.shape[3]
@@ -294,15 +284,17 @@
             edge[u + 1, x + halo] = finish(sums + sums_own[x + halo], biases[:, 0:1], top)
 
     def row(u, a, b):
-        return [edge[u + 1, x] for x in range(a, b)] if u < 1 else halves(inner_a, inner_b, u - 1, a, b)
+        if 0 < u < 7:
+            return halves(inner_a, inner_b, u - 1, a, b)
+        return [edge[u + 1, x] if u < 1 else (row_seven if u == 7 else mate)[x] for x in range(a, b)]
 
     two = (matrix_two, low_two, high_two)
-    for u in (0, 1):
+    for at, u in enumerate((0, 1, 7)):
         for x, here, beside in second_row(
             lambda j, a, b: row(u - 1 + j, a, b), inner_a.shape[1], halo, two, both[:, 0:1], place.top()
         ):
-            done_edge[u, x] = here
-            done_edge[u, x + 1] = beside
+            done_edge[at, x] = here
+            done_edge[at, x + 1] = beside
     quarter = out.shape[1]
     size = quarter * COL_Y
     at_row = lax.broadcasted_iota(jnp.int32, (size, size), 0)
@@ -311,7 +303,7 @@
     u = jnp.where(place.odd == 1, COL_Y - 1 - y, y)
     swap = (at_column == u * quarter + lax.div(at_row, COL_Y)).astype(F32).astype(BF16)
     for x in range(COL_Y):
-        tiles = [done_edge[0, x], done_edge[1, x]] + [done_inner[v, x] for v in range(COL_Y - 3)] + [done_seven[x]]
+        tiles = [done_edge[0, x], done_edge[1, x]] + [done_inner[v, x] for v in range(COL_Y - 3)] + [done_edge[2, x]]
         tile = jnp.concatenate(tiles, axis=0)
         moved = jnp.dot(swap, tile, preferred_element_type=F32).astype(BF16)
         result[x] = moved.reshape(quarter, COL_Y, depth)
@@ -390,32 +382,25 @@
     return inner, row_seven, matrices
 
 
-def second_inner(halo, heights, inner_a, inner_b, row_seven, matrices):
+def second_inner(halo, heights, own, near, far, inner_a, inner_b, row_seven, matrices):
     rows, _, _, depth = inner_a.shape
+    channels, width = own.shape[2], COL_Y + 2 * halo
     quarter = matrices[-1].shape[0] // 2
-    outputs = [(rows - 1, COL_Y, quarter, depth)]
-    args = (heights, inner_a, inner_b, row_seven, *matrices)
+    sums = (width, TAPS * channels, depth)
+    outputs, kinds = [(rows - 1, COL_Y, quarter, depth), sums, sums], [BF16, F32, F32]
+    args = (heights, own, *near, *far, inner_a, inner_b, row_seven, *matrices)
     kernel = functools.partial(second_inner_kernel, halo)
-    return call(kernel, "second_inner", [SCALARS] + [WHOLE] * (len(args) - 1), outputs, [], SHORT, *args)[0]
-
-
-def ahead(halo, heights, own, near, far, hidden, matrices):
-    _, _, channels, depth = own.shape
-    quarter, width = matrices[-1].shape[0] // 2, COL_Y + 2 * halo
-    sums = (width, TAPS * channels, depth)
-    args = (heights, own, *near, *far, *hidden, *matrices)
-    kernel = functools.partial(ahead_kernel, halo)
-    outputs, kinds = [(COL_Y, quarter, depth), sums, sums], [BF16, F32, F32]
-    return call(kernel, "ahead", [SCALARS] + [WHOLE] * (len(args) - 1), outputs, [], SHORT, *args, kinds=kinds)
-
-
-def last(halo, heights, cross, near, far, sums, inner, done, matrices):
+    done, *sums = call(kernel, "second_inner", [SCALARS] + [WHOLE] * (len(args) - 1), outputs, [], SHORT, *args, kinds=kinds)
+    return done, sums
+
+
+def last(halo, heights, own, cross, near, far, sums, hidden, done_inner, matrices):
     _, _, channels, depth = cross.shape
     quarter, width = matrices[-1].shape[0] // 2, COL_Y + 2 * halo
-    scratch = [pltpu.VMEM((2, width, channels, depth), BF16), pltpu.VMEM((2, COL_Y, quarter, depth), BF16)]
+    scratch = [pltpu.VMEM((2, width, channels, depth), BF16), pltpu.VMEM((3, COL_Y, quarter, depth), BF16)]
     scratch += [pltpu.VMEM((COL_Y, quarter, COL_Y, depth), BF16), pltpu.SemaphoreType.DMA((COL_Y,))]
     outputs = [(1, quarter, COL_Y, COL_Y, depth)]
-    args = (heights, cross, *near, *far, *sums, *inner, *done, *matrices)
+    args = (heights, own, cross, *near, *far, *sums, *hidden, done_inner, *matrices)
     kernel = functools.partial(last_kernel, halo)
     return call(kernel, "last", [SCALARS] + [WHOLE] * (len(args) - 1), outputs, scratch, SHORT, *args, place=ANY)[0]
 
@@ -453,7 +438,8 @@
     own_part = pack(weight_one, bias_one, swap)
     near_part = lax.ppermute(own_part, "chan", [(c, c ^ 1) for c in range(chans)])
     fields, cross, mate = arrange(column_heights, features, swap, own_part)
-    far_part = lax.ppermute(own_part, ("space", "chan"), far_pairs(peers, chans))
+    sent_part, cross = lax.optimization_barrier((own_part, cross))
+    far_part = lax.ppermute(sent_part, ("space", "chan"), far_pairs(peers, chans))
     cross = lax.ppermute(cross, "space", across_pairs(peers))
     near_part, mate = lax.optimization_barrier((near_part, mate))
     mate = to_mate(mate)
@@ -467,10 +453,9 @@
     matrices = fill(column_heights, weight_two, bias_two, inner_a)
     inner_b, row_seven, far = first_far(halo, column_heights, fields, mate, far_part, other_part, near, matrices[-1])
     mate = to_mate(row_seven)
-    done_inner = second_inner(halo, column_heights, inner_a, inner_b, row_seven, matrices)
-    done_seven, *sums = ahead(halo, column_heights, fields, near, far, (inner_a, inner_b, row_seven, mate), matrices)
-    done = (done_inner, done_seven)
-    return last(halo, column_heights, cross, near, far, sums, (inner_a, inner_b), done, matrices)
+    done_inner, sums = second_inner(halo, column_heights, fields, near, far, inner_a, inner_b, row_seven, matrices)
+    hidden = (inner_a, inner_b, row_seven, mate)
+    return last(halo, column_heights, fields, cross, near, far, sums, hidden, done_inner, matrices)
 
 
 def solution(mesh):

time: 44.1 us -> 42.3 us (0.959)
  Pallas kernels: 31.2 us -> 30.2 us
    ppermute x1, starting transfers between devices: 2.19 us -> 4.12 us  [on_device(): lax.ppermute(sent_part, ('space', 'chan'), far_pairs(peers, chans))]
    ppermute x1, starting transfers between devices: 4.35 us -> 2.94 us  [on_device(): cross = lax.ppermute(cross, 'space', across_pairs(peers))]
    pallas_call x9 -> x8, Pallas kernels: 31.2 us -> 30.2 us  [call(): pl.pallas_call(kernel, out_shape=[jax.ShapeDtypeStruct(*each) for each in...]
    ppermute x3, starting transfers between devices: 1.96 us -> 1.06 us  [to_mate(): lax.ppermute(value, 'space', [(i, i ^ 1) for i in range(lax.axis_size('sp...]
  transfers between devices with their start and end apart: 6 -> 6, of which waited for: 1 -> 1; matrix products, arithmetic and copies ran while one was open for 0% -> 0% of each run, Pallas kernels for 59% -> 58%
where the time goes in v8:
time: 42.3 us; the launch traced here: 42 us
  Pallas kernels  30.2 us (71%)
  starting transfers between devices  10.3 us (24%)
  local copies, waits for them, and re-layouts  0.9 us (2%)
    pallas_call x8, Pallas kernels, call(): pl.pallas_call(kernel, out_shape=[jax.ShapeDtypeStruct(*each) for each in...  30.2 us
    ppermute x1, starting transfers between devices, on_device(): lax.ppermute(sent_part, ('space', 'chan'), far_pairs(peers, chans))  4.12 us
    ppermute x1, starting transfers between devices, on_device(): cross = lax.ppermute(cross, 'space', across_pairs(peers))  2.94 us
    ppermute x1, starting transfers between devices, on_device(): lax.ppermute(own_part, 'chan', [(c, c ^ 1) for c in range(chans)])  2.19 us
    ppermute x3, starting transfers between devices, to_mate(): lax.ppermute(value, 'space', [(i, i ^ 1) for i in range(lax.axis_size('sp...  1.06 us
    unnamed x12, local copies, waits for them, and re-layouts  0.9 us
  transfers between devices with their start and end apart: 6, of which 1 were waited for; matrix products, arithmetic and copies ran while one was open for 0% of the time, Pallas kernels for 58%

profile of v8, /device:TPU:1, one launch (start us, length us, event | category | flops | bytes accessed | tf_op | source)
XLA Modules:
  0.0 42.0 jit_solution(11504914419480928579)
XLA Ops:
  0.0 0.1 order.1.after.swap
  0.1 0.6 %copy-done.5 = f32[32]{0:T(128)S(1)} copy-done((f32[32]{0:T(128)S(1)}, f32[32]{0:T(128)}, u32[]{:S(2)}) %copy-start.5) | copy-done | bytes 152
  0.7 0.3 copy-done.4
  1.0 0.1 pack.1.after.part_a
  1.1 2.2 %collective-permute-start.1 = (bf16[28,32,128]{2,1,0:T(8,128)(2,1)S(1)}, bf16[28,32,128]{2,1,0:T(8,128)(2,1)S(1)}, u32[]{:S(2)}, u32[]{:S(2)}) collective-permute-start(bf16[28,32,128]{2,1,0:T(8,128)(2,1)S(1)} %pack.1.after.part_a), channel_id=1, source_target_pairs={{0,1},{1,0},{2,3},{3,2},{4,5},{5,4},{6,7},{7,6},{8,9},{9,8},{10,11... | collective-permute-start | bytes 688136 | tf_op jit(solution)/shard_map/ppermute | solution.py:439
  3.2 1.8 %arrange.1 = (bf16[8,8,128,256]{3,2,1,0:T(8,128)(2,1)S(1)}, bf16[2,8,128,256]{3,2,1,0:T(8,128)(2,1)S(1)}, bf16[8,128,256]{2,1,0:T(8,128)(2,1)S(1)}) custom-call(s32[8]{0:T(128)S(1)} %copy-done.2, bf16[1,128,8,8,256]{4,3,2,1,0:T(8,128)(2,1)S(1)} %copy-done, bf16[256,256]{1,0:T(8,128)(2,1)S(1)} %order.1.after.swap, bf16[28,32,128]{2,1,0:T(8,128)(2,1)S(1)} %pack.1.after.part_a), custom_call_target="tpu_custom_call" | custom-call | flops 4096 | bytes 64 | tf_op jit(solution)/shard_map/arrange/pallas_call | solution.py:319
  5.1 4.1 %collective-permute-start.3 = (bf16[28,32,128]{2,1,0:T(8,128)(2,1)S(1)}, bf16[28,32,128]{2,1,0:T(8,128)(2,1)S(1)}, u32[]{:S(2)}, u32[]{:S(2)}) collective-permute-start(bf16[28,32,128]{2,1,0:T(8,128)(2,1)S(1)} %pack.1.after.part_a), channel_id=1, source_target_pairs={{0,2},{1,3},{2,0},{3,1},{4,7},{5,6},{6,5},{7,4},{8,10},{9,11},{10,... | collective-permute-start | bytes 688136 | tf_op jit(solution)/shard_map/ppermute | solution.py:442
  9.2 2.9 %collective-permute-start = (bf16[2,8,128,256]{3,2,1,0:T(8,128)(2,1)S(1)}, bf16[2,8,128,256]{3,2,1,0:T(8,128)(2,1)S(1)}, u32[]{:S(2)}, u32[]{:S(2)}) collective-permute-start(bf16[2,8,128,256]{3,2,1,0:T(8,128)(2,1)S(1)} %get-tuple-element.34), channel_id=1, source_target_pairs={{4,8},{8,4},{12,16},{16,12},{20,24},{24,20},{5,9},{9,5},{13,17},{1... | collective-permute-start | bytes 3145736 | tf_op jit(solution)/shard_map/ppermute | solution.py:443
  12.1 0.0 collective-permute-done.1.part_b
  12.1 0.1 collective-permute-start.2
  12.2 0.0 copy-start.1
  12.2 0.0 copy-start.3
  12.2 7.1 %first_near.1 = (bf16[6,8,64,256]{3,2,1,0:T(8,128)(2,1)S(1)}, bf16[192,1152]{1,0:T(8,128)(2,1)S(1)}, bf16[192,768]{1,0:T(8,128)(2,1)S(1)}, bf16[192,768]{1,0:T(8,128)(2,1)S(1)}, f32[64,128]{1,0:T(8,128)S(1)}) custom-call(s32[8]{0:T(128)S(1)} %copy-done.2, bf16[8,8,128,256]{3,2,1,0:T(8,128)(2,1)S(1)} %get-tuple-element.32.own, ...), custom_call_target="tpu_custom_call" | custom-call | flops 8589934592 | bytes 134217728 | tf_op jit(solution)/shard_map/first_near/pallas_call | solution.py:319
  19.4 0.0 collective-permute-done.3.part_a
  19.4 0.6 %collective-permute-start.4 = (bf16[28,32,128]{2,1,0:T(8,128)(2,1)S(1)}, bf16[28,32,128]{2,1,0:T(8,128)(2,1)S(1)}, u32[]{:S(2)}, u32[]{:S(2)}) collective-permute-start(bf16[28,32,128]{2,1,0:T(8,128)(2,1)S(1)} %collective-permute-done.3.part_a), channel_id=1, source_target_pairs={{0,4},{4,0},{8,12},{12,8},{16,20},{20,16},{24,28},{28,24},{1,5},{5... | collective-permute-start | bytes 688136 | tf_op jit(solution)/shard_map/ppermute | solution.py:418
  19.9 0.8 %fill.1 = (bf16[192,1536]{1,0:T(8,128)(2,1)S(1)}, bf16[192,1152]{1,0:T(8,128)(2,1)S(1)}, bf16[192,1152]{1,0:T(8,128)(2,1)S(1)}, f32[64,128]{1,0:T(8,128)S(1)}) custom-call(s32[8]{0:T(128)S(1)} %copy-done.2, bf16[27,32,128]{2,1,0:T(8,128)(2,1)S(1)} %copy-done.1, f32[1,32]{1,0:T(1,128)S(1)} %bitcast.2, bf16[6,8,64,256]{3,2,1,0:T(8,128)(2,1)S(1)} %get-tuple-element.45.after.inner_a), custom_call_target="tpu_custom_call" | custom-call | flops 4096 | bytes 64 | tf_op jit(solution)/shard_map/fill/pallas_call | solution.py:319
  20.8 0.3 collective-permute-done.4.part_b
  21.1 0.0 collective-permute-done.2.mate
  21.1 9.4 %first_far.1 = (bf16[6,8,64,256]{3,2,1,0:T(8,128)(2,1)S(1)}, bf16[8,128,256]{2,1,0:T(8,128)(2,1)S(1)}, bf16[192,1152]{1,0:T(8,128)(2,1)S(1)}, bf16[192,768]{1,0:...) custom-call(s32[8]{0:T(128)S(1)} %copy-done.2, ...), custom_call_target="tpu_custom_call" | custom-call | flops 4096 | bytes 64 | tf_op jit(solution)/shard_map/first_far/pallas_call | solution.py:319
  30.4 0.4 %collective-permute-start.5 = (bf16[8,128,256]{2,1,0:T(8,128)(2,1)S(1)}, bf16[8,128,256]{2,1,0:T(8,128)(2,1)S(1)}, u32[]{:S(2)}, u32[]{:S(2)}) collective-permute-start(bf16[8,128,256]{2,1,0:T(8,128)(2,1)S(1)} %get-tuple-element.52.row_seven), channel_id=1, source_target_pairs={{0,4},{4,0},{8,12},{12,8},{16,20},{20,16},{24,28},{28,24},{1,5},{5... | collective-permute-start | bytes 1572872 | tf_op jit(solution)/shard_map/ppermute | solution.py:418
  30.9 5.4 %second_inner.1 = (bf16[5,8,32,256]{3,2,1,0:T(8,128)(2,1)S(1)}, f32[8,384,256]{2,1,0:T(8,128)S(1)}, f32[8,384,256]{2,1,0:T(8,128)S(1)}) custom-call(s32[8]{0:T(128)S(1)} %copy-done.2, bf16[8,8,128,256]{3,2,1,0:T(8,128)(2,1)S(1)} %get-tuple-element.32.own, bf16[192,1152]{1,0:T(8,128)(2,1)S(1)} %get-tuple-element.37.near, ...), custom_call_target="tpu_custom_call" | custom-call | flops 4096 | bytes 64 | tf_op jit(solution)/shard_map/second_inner/pallas_call | solution.py:319
  36.3 0.0 collective-permute-done.cross
  36.3 0.0 collective-permute-done.5.mate
  36.3 5.5 %last.1 = bf16[1,32,8,8,256]{4,3,2,1,0:T(8,128)(2,1)} custom-call(s32[8]{0:T(128)S(1)} %copy-done.2, bf16[8,8,128,256]{3,2,1,0:T(8,128)(2,1)S(1)} %get-tuple-element.32.own, bf16[2,8,128,256]{3,2,1,0:T(8,128)(2,1)S(1)} %collective-permute-done.cross, bf16[192,1152]{1,0:T(8,128)(2,1)S(1)} %get-tuple-element.37.near, ...), custom_call_target="tpu_custom_call" | custom-call | flops 4096 | bytes 64 | tf_op jit(solution)/shard_map/last/pallas_call | solution.py:319
  (8 shorter events, 0.0 us)
Async XLA Ops:
  0.0 0.7 %copy-start.5 = (f32[32]{0:T(128)S(1)}, f32[32]{0:T(128)}, u32[]{:S(2)}) copy-start(f32[32]{0:T(128)} %param.9) | copy-start | bytes 388
  0.0 0.9 %copy-start.4 = (bf16[27,32,128]{2,1,0:T(8,128)(2,1)S(1)}, bf16[27,32,128]{2,1,0:T(8,128)(2,1)}, u32[]{:S(2)}) copy-start(bf16[27,32,128]{2,1,0:T(8,128)(2,1)} %weights.2) | copy-start | bytes 663556
  1.0 2.3 %copy-start = (bf16[1,128,8,8,256]{4,3,2,1,0:T(8,128)(2,1)S(1)}, bf16[1,128,8,8,256]{4,3,2,1,0:T(8,128)(2,1)}, u32[]{:S(2)}) copy-start(bf16[1,128,8,8,256]{4,3,2,1,0:T(8,128)(2,1)} %features.1) | copy-start | bytes 12582916
  1.0 2.3 %copy-start.2 = (s32[8]{0:T(128)S(1)}, s32[8]{0:T(128)}, u32[]{:S(2)}) copy-start(s32[8]{0:T(128)} %heights.11) | copy-start | bytes 100
  1.1 11.1 %collective-permute-start.1 = (bf16[28,32,128]{2,1,0:T(8,128)(2,1)S(1)}, bf16[28,32,128]{2,1,0:T(8,128)(2,1)S(1)}, u32[]{:S(2)}, u32[]{:S(2)}) collective-permute-start(bf16[28,32,128]{2,1,0:T(8,128)(2,1)S(1)} %pack.1.after.part_a), channel_id=1, source_target_pairs={{0,1},{1,0},{2,3},{3,2},{4,5},{5,4},{6,7},{7,6},{8,9},{9,8},{10,11... | collective-permute-start | bytes 688136 | tf_op jit(solution)/shard_map/ppermute | solution.py:439
  5.1 14.3 %collective-permute-start.3 = (bf16[28,32,128]{2,1,0:T(8,128)(2,1)S(1)}, bf16[28,32,128]{2,1,0:T(8,128)(2,1)S(1)}, u32[]{:S(2)}, u32[]{:S(2)}) collective-permute-start(bf16[28,32,128]{2,1,0:T(8,128)(2,1)S(1)} %pack.1.after.part_a), channel_id=1, source_target_pairs={{0,2},{1,3},{2,0},{3,1},{4,7},{5,6},{6,5},{7,4},{8,10},{9,11},{10,... | collective-permute-start | bytes 688136 | tf_op jit(solution)/shard_map/ppermute | solution.py:442
  9.2 27.1 %collective-permute-start = (bf16[2,8,128,256]{3,2,1,0:T(8,128)(2,1)S(1)}, bf16[2,8,128,256]{3,2,1,0:T(8,128)(2,1)S(1)}, u32[]{:S(2)}, u32[]{:S(2)}) collective-permute-start(bf16[2,8,128,256]{3,2,1,0:T(8,128)(2,1)S(1)} %get-tuple-element.34), channel_id=1, source_target_pairs={{4,8},{8,4},{12,16},{16,12},{20,24},{24,20},{5,9},{9,5},{13,17},{1... | collective-permute-start | bytes 3145736 | tf_op jit(solution)/shard_map/ppermute | solution.py:443
  12.1 8.9 %collective-permute-start.2 = (bf16[8,128,256]{2,1,0:T(8,128)(2,1)S(1)}, bf16[8,128,256]{2,1,0:T(8,128)(2,1)S(1)}, u32[]{:S(2)}, u32[]{:S(2)}) collective-permute-start(bf16[8,128,256]{2,1,0:T(8,128)(2,1)S(1)} %get-tuple-element.41), channel_id=1, source_target_pairs={{0,4},{4,0},{8,12},{12,8},{16,20},{20,16},{24,28},{28,24},{1,5},{5... | collective-permute-start | bytes 1572872 | tf_op jit(solution)/shard_map/ppermute | solution.py:418
  12.2 7.7 %copy-start.1 = (bf16[27,32,128]{2,1,0:T(8,128)(2,1)S(1)}, bf16[27,32,128]{2,1,0:T(8,128)(2,1)}, u32[]{:S(2)}) copy-start(bf16[27,32,128]{2,1,0:T(8,128)(2,1)} %weights.3) | copy-start | bytes 663556
  12.2 7.7 %copy-start.3 = (f32[32]{0:T(128)S(1)}, f32[32]{0:T(128)}, u32[]{:S(2)}) copy-start(f32[32]{0:T(128)} %param.11) | copy-start | bytes 388
  19.4 1.7 %collective-permute-start.4 = (bf16[28,32,128]{2,1,0:T(8,128)(2,1)S(1)}, bf16[28,32,128]{2,1,0:T(8,128)(2,1)S(1)}, u32[]{:S(2)}, u32[]{:S(2)}) collective-permute-start(bf16[28,32,128]{2,1,0:T(8,128)(2,1)S(1)} %collective-permute-done.3.part_a), channel_id=1, source_target_pairs={{0,4},{4,0},{8,12},{12,8},{16,20},{20,16},{24,28},{28,24},{1,5},{5... | collective-permute-start | bytes 688136 | tf_op jit(solution)/shard_map/ppermute | solution.py:418
  30.4 5.9 %collective-permute-start.5 = (bf16[8,128,256]{2,1,0:T(8,128)(2,1)S(1)}, bf16[8,128,256]{2,1,0:T(8,128)(2,1)S(1)}, u32[]{:S(2)}, u32[]{:S(2)}) collective-permute-start(bf16[8,128,256]{2,1,0:T(8,128)(2,1)S(1)} %get-tuple-element.52.row_seven), channel_id=1, source_target_pairs={{0,4},{4,0},{8,12},{12,8},{16,20},{20,16},{24,28},{28,24},{1,5},{5... | collective-permute-start | bytes 1572872 | tf_op jit(solution)/shard_map/ppermute | solution.py:418

commit v9 on v8

--- a/solution.py
+++ b/solution.py
@@ -149,14 +149,9 @@
 
 
 def inner_rows(own, out, halo, matrices, bias, top):
-    def pair(step, _):
-        for more in range(2):
-            u = step * 2 + more
-            for x, done in first_row(lambda j, a, b: span_of(own, u + j, a, b), own.shape[1], halo, matrices, bias, top):
-                out[u, x] = done
-        return 0
-
-    lax.fori_loop(0, (COL_Y - 2) // 2, pair, 0)
+    for u in range(COL_Y - 2):
+        for x, done in first_row(lambda j, a, b: span_of(own, u + j, a, b), own.shape[1], halo, matrices, bias, top):
+            out[u, x] = done
 
 
 def first_near_kernel(halo, heights, own, part_a, part_b, out, matrix, low_matrix, high_matrix, bias):

time: 42.3 us -> 42.2 us (level)
  Pallas kernels: 30.2 us -> 28.7 us
  waiting for transfers between devices: 0.34 us -> 1.3 us
  starting transfers between devices: 10.3 us -> 10.8 us
    pallas_call x8, Pallas kernels: 30.2 us -> 28.7 us  [call(): pl.pallas_call(kernel, out_shape=[jax.ShapeDtypeStruct(*each) for each in...]
    ppermute x1, waiting for transfers between devices: 0.03 us -> 0.99 us  [on_device(): cross = lax.ppermute(cross, 'space', across_pairs(peers))]
    ppermute x3, starting transfers between devices: 1.06 us -> 1.57 us  [to_mate(): lax.ppermute(value, 'space', [(i, i ^ 1) for i in range(lax.axis_size('sp...]
  transfers between devices with their start and end apart: 6 -> 6, of which waited for: 1 -> 2; matrix products, arithmetic and copies ran while one was open for 0% -> 0% of each run, Pallas kernels for 58% -> 55%
where the time goes in v9:
time: 42.2 us; the launch traced here: 42 us
  Pallas kernels  28.7 us (68%)
  starting transfers between devices  10.8 us (26%)
  waiting for transfers between devices  1.3 us (3%)
  local copies, waits for them, and re-layouts  0.9 us (2%)
    pallas_call x8, Pallas kernels, call(): pl.pallas_call(kernel, out_shape=[jax.ShapeDtypeStruct(*each) for each in...  28.7 us
    ppermute x1, starting transfers between devices, on_device(): lax.ppermute(sent_part, ('space', 'chan'), far_pairs(peers, chans))  4.12 us
    ppermute x1, starting transfers between devices, on_device(): cross = lax.ppermute(cross, 'space', across_pairs(peers))  2.94 us
    ppermute x1, starting transfers between devices, on_device(): lax.ppermute(own_part, 'chan', [(c, c ^ 1) for c in range(chans)])  2.19 us
    ppermute x3, starting transfers between devices, to_mate(): lax.ppermute(value, 'space', [(i, i ^ 1) for i in range(lax.axis_size('sp...  1.57 us
    ppermute x1, waiting for transfers between devices, on_device(): cross = lax.ppermute(cross, 'space', across_pairs(peers))  0.99 us
    unnamed x12, local copies, waits for them, and re-layouts  0.9 us
  transfers between devices with their start and end apart: 6, of which 2 were waited for; matrix products, arithmetic and copies ran while one was open for 0% of the time, Pallas kernels for 55%

profile of v9, /device:TPU:1, one launch (start us, length us, event | category | flops | bytes accessed | tf_op | source)
XLA Modules:
  0.0 42.0 jit_solution(13276496107041740505)
XLA Ops:
  0.0 0.1 order.1.after.swap
  0.1 0.6 %copy-done.5 = f32[32]{0:T(128)S(1)} copy-done((f32[32]{0:T(128)S(1)}, f32[32]{0:T(128)}, u32[]{:S(2)}) %copy-start.5) | copy-done | bytes 152
  0.7 0.3 copy-done.4
  1.0 0.1 pack.1.after.part_a
  1.1 2.2 %collective-permute-start.1 = (bf16[28,32,128]{2,1,0:T(8,128)(2,1)S(1)}, bf16[28,32,128]{2,1,0:T(8,128)(2,1)S(1)}, u32[]{:S(2)}, u32[]{:S(2)}) collective-permute-start(bf16[28,32,128]{2,1,0:T(8,128)(2,1)S(1)} %pack.1.after.part_a), channel_id=1, source_target_pairs={{0,1},{1,0},{2,3},{3,2},{4,5},{5,4},{6,7},{7,6},{8,9},{9,8},{10,11... | collective-permute-start | bytes 688136 | tf_op jit(solution)/shard_map/ppermute | solution.py:434
  3.2 1.8 %arrange.1 = (bf16[8,8,128,256]{3,2,1,0:T(8,128)(2,1)S(1)}, bf16[2,8,128,256]{3,2,1,0:T(8,128)(2,1)S(1)}, bf16[8,128,256]{2,1,0:T(8,128)(2,1)S(1)}) custom-call(s32[8]{0:T(128)S(1)} %copy-done.2, bf16[1,128,8,8,256]{4,3,2,1,0:T(8,128)(2,1)S(1)} %copy-done, bf16[256,256]{1,0:T(8,128)(2,1)S(1)} %order.1.after.swap, bf16[28,32,128]{2,1,0:T(8,128)(2,1)S(1)} %pack.1.after.part_a), custom_call_target="tpu_custom_call" | custom-call | flops 4096 | bytes 64 | tf_op jit(solution)/shard_map/arrange/pallas_call | solution.py:314
  5.1 4.1 %collective-permute-start.3 = (bf16[28,32,128]{2,1,0:T(8,128)(2,1)S(1)}, bf16[28,32,128]{2,1,0:T(8,128)(2,1)S(1)}, u32[]{:S(2)}, u32[]{:S(2)}) collective-permute-start(bf16[28,32,128]{2,1,0:T(8,128)(2,1)S(1)} %pack.1.after.part_a), channel_id=1, source_target_pairs={{0,2},{1,3},{2,0},{3,1},{4,7},{5,6},{6,5},{7,4},{8,10},{9,11},{10,... | collective-permute-start | bytes 688136 | tf_op jit(solution)/shard_map/ppermute | solution.py:437
  9.2 2.9 %collective-permute-start = (bf16[2,8,128,256]{3,2,1,0:T(8,128)(2,1)S(1)}, bf16[2,8,128,256]{3,2,1,0:T(8,128)(2,1)S(1)}, u32[]{:S(2)}, u32[]{:S(2)}) collective-permute-start(bf16[2,8,128,256]{3,2,1,0:T(8,128)(2,1)S(1)} %get-tuple-element.34), channel_id=1, source_target_pairs={{4,8},{8,4},{12,16},{16,12},{20,24},{24,20},{5,9},{9,5},{13,17},{1... | collective-permute-start | bytes 3145736 | tf_op jit(solution)/shard_map/ppermute | solution.py:438
  12.1 0.0 collective-permute-done.1.part_b
  12.1 0.1 collective-permute-start.2
  12.2 0.0 copy-start.1
  12.2 0.0 copy-start.3
  12.2 6.5 %first_near.1 = (bf16[6,8,64,256]{3,2,1,0:T(8,128)(2,1)S(1)}, bf16[192,1152]{1,0:T(8,128)(2,1)S(1)}, bf16[192,768]{1,0:T(8,128)(2,1)S(1)}, bf16[192,768]{1,0:T(8,128)(2,1)S(1)}, f32[64,128]{1,0:T(8,128)S(1)}) custom-call(s32[8]{0:T(128)S(1)} %copy-done.2, bf16[8,8,128,256]{3,2,1,0:T(8,128)(2,1)S(1)} %get-tuple-element.32.own, ...), custom_call_target="tpu_custom_call" | custom-call | flops 8589934592 | bytes 134217728 | tf_op jit(solution)/shard_map/first_near/pallas_call | solution.py:314
  18.7 0.0 collective-permute-done.3.part_a
  18.7 1.1 %collective-permute-start.4 = (bf16[28,32,128]{2,1,0:T(8,128)(2,1)S(1)}, bf16[28,32,128]{2,1,0:T(8,128)(2,1)S(1)}, u32[]{:S(2)}, u32[]{:S(2)}) collective-permute-start(bf16[28,32,128]{2,1,0:T(8,128)(2,1)S(1)} %collective-permute-done.3.part_a), channel_id=1, source_target_pairs={{0,4},{4,0},{8,12},{12,8},{16,20},{20,16},{24,28},{28,24},{1,5},{5... | collective-permute-start | bytes 688136 | tf_op jit(solution)/shard_map/ppermute | solution.py:413
  19.8 0.8 %fill.1 = (bf16[192,1536]{1,0:T(8,128)(2,1)S(1)}, bf16[192,1152]{1,0:T(8,128)(2,1)S(1)}, bf16[192,1152]{1,0:T(8,128)(2,1)S(1)}, f32[64,128]{1,0:T(8,128)S(1)}) custom-call(s32[8]{0:T(128)S(1)} %copy-done.2, bf16[27,32,128]{2,1,0:T(8,128)(2,1)S(1)} %copy-done.1, f32[1,32]{1,0:T(1,128)S(1)} %bitcast.2, bf16[6,8,64,256]{3,2,1,0:T(8,128)(2,1)S(1)} %get-tuple-element.45.after.inner_a), custom_call_target="tpu_custom_call" | custom-call | flops 4096 | bytes 64 | tf_op jit(solution)/shard_map/fill/pallas_call | solution.py:314
  20.6 0.3 collective-permute-done.4.part_b
  20.9 0.0 collective-permute-done.2.mate
  20.9 8.5 %first_far.1 = (bf16[6,8,64,256]{3,2,1,0:T(8,128)(2,1)S(1)}, bf16[8,128,256]{2,1,0:T(8,128)(2,1)S(1)}, bf16[192,1152]{1,0:T(8,128)(2,1)S(1)}, bf16[192,768]{1,0:...) custom-call(s32[8]{0:T(128)S(1)} %copy-done.2, ...), custom_call_target="tpu_custom_call" | custom-call | flops 4096 | bytes 64 | tf_op jit(solution)/shard_map/first_far/pallas_call | solution.py:314
  29.5 0.4 %collective-permute-start.5 = (bf16[8,128,256]{2,1,0:T(8,128)(2,1)S(1)}, bf16[8,128,256]{2,1,0:T(8,128)(2,1)S(1)}, u32[]{:S(2)}, u32[]{:S(2)}) collective-permute-start(bf16[8,128,256]{2,1,0:T(8,128)(2,1)S(1)} %get-tuple-element.52.row_seven), channel_id=1, source_target_pairs={{0,4},{4,0},{8,12},{12,8},{16,20},{20,16},{24,28},{28,24},{1,5},{5... | collective-permute-start | bytes 1572872 | tf_op jit(solution)/shard_map/ppermute | solution.py:413
  29.9 5.4 %second_inner.1 = (bf16[5,8,32,256]{3,2,1,0:T(8,128)(2,1)S(1)}, f32[8,384,256]{2,1,0:T(8,128)S(1)}, f32[8,384,256]{2,1,0:T(8,128)S(1)}) custom-call(s32[8]{0:T(128)S(1)} %copy-done.2, bf16[8,8,128,256]{3,2,1,0:T(8,128)(2,1)S(1)} %get-tuple-element.32.own, bf16[192,1152]{1,0:T(8,128)(2,1)S(1)} %get-tuple-element.37.near, ...), custom_call_target="tpu_custom_call" | custom-call | flops 4096 | bytes 64 | tf_op jit(solution)/shard_map/second_inner/pallas_call | solution.py:314
  35.3 1.0 %collective-permute-done.cross = bf16[2,8,128,256]{3,2,1,0:T(8,128)(2,1)S(1)} collective-permute-done((bf16[2,8,128,256]{3,2,1,0:T(8,128)(2,1)S(1)}, bf16[2,8,128,256]{3,2,1,0:T(8,128)(2,1)S(1)}, u32[]{:S(2)}, u32[]{:S(2)}) %collective-permute-start) | collective-permute-done | bytes 1048608 | tf_op jit(solution)/shard_map/ppermute | solution.py:438
  36.3 0.0 collective-permute-done.5.mate
  36.3 5.5 %last.1 = bf16[1,32,8,8,256]{4,3,2,1,0:T(8,128)(2,1)} custom-call(s32[8]{0:T(128)S(1)} %copy-done.2, bf16[8,8,128,256]{3,2,1,0:T(8,128)(2,1)S(1)} %get-tuple-element.32.own, bf16[2,8,128,256]{3,2,1,0:T(8,128)(2,1)S(1)} %collective-permute-done.cross, bf16[192,1152]{1,0:T(8,128)(2,1)S(1)} %get-tuple-element.37.near, ...), custom_call_target="tpu_custom_call" | custom-call | flops 4096 | bytes 64 | tf_op jit(solution)/shard_map/last/pallas_call | solution.py:314
  (8 shorter events, 0.0 us)
Async XLA Ops:
  0.0 0.7 %copy-start.5 = (f32[32]{0:T(128)S(1)}, f32[32]{0:T(128)}, u32[]{:S(2)}) copy-start(f32[32]{0:T(128)} %param.9) | copy-start | bytes 388
  0.0 0.9 %copy-start.4 = (bf16[27,32,128]{2,1,0:T(8,128)(2,1)S(1)}, bf16[27,32,128]{2,1,0:T(8,128)(2,1)}, u32[]{:S(2)}) copy-start(bf16[27,32,128]{2,1,0:T(8,128)(2,1)} %weights.2) | copy-start | bytes 663556
  1.0 2.3 %copy-start = (bf16[1,128,8,8,256]{4,3,2,1,0:T(8,128)(2,1)S(1)}, bf16[1,128,8,8,256]{4,3,2,1,0:T(8,128)(2,1)}, u32[]{:S(2)}) copy-start(bf16[1,128,8,8,256]{4,3,2,1,0:T(8,128)(2,1)} %features.1) | copy-start | bytes 12582916
  1.0 2.3 %copy-start.2 = (s32[8]{0:T(128)S(1)}, s32[8]{0:T(128)}, u32[]{:S(2)}) copy-start(s32[8]{0:T(128)} %heights.11) | copy-start | bytes 100
  1.1 11.1 %collective-permute-start.1 = (bf16[28,32,128]{2,1,0:T(8,128)(2,1)S(1)}, bf16[28,32,128]{2,1,0:T(8,128)(2,1)S(1)}, u32[]{:S(2)}, u32[]{:S(2)}) collective-permute-start(bf16[28,32,128]{2,1,0:T(8,128)(2,1)S(1)} %pack.1.after.part_a), channel_id=1, source_target_pairs={{0,1},{1,0},{2,3},{3,2},{4,5},{5,4},{6,7},{7,6},{8,9},{9,8},{10,11... | collective-permute-start | bytes 688136 | tf_op jit(solution)/shard_map/ppermute | solution.py:434
  5.1 13.7 %collective-permute-start.3 = (bf16[28,32,128]{2,1,0:T(8,128)(2,1)S(1)}, bf16[28,32,128]{2,1,0:T(8,128)(2,1)S(1)}, u32[]{:S(2)}, u32[]{:S(2)}) collective-permute-start(bf16[28,32,128]{2,1,0:T(8,128)(2,1)S(1)} %pack.1.after.part_a), channel_id=1, source_target_pairs={{0,2},{1,3},{2,0},{3,1},{4,7},{5,6},{6,5},{7,4},{8,10},{9,11},{10,... | collective-permute-start | bytes 688136 | tf_op jit(solution)/shard_map/ppermute | solution.py:437
  9.2 27.1 %collective-permute-start = (bf16[2,8,128,256]{3,2,1,0:T(8,128)(2,1)S(1)}, bf16[2,8,128,256]{3,2,1,0:T(8,128)(2,1)S(1)}, u32[]{:S(2)}, u32[]{:S(2)}) collective-permute-start(bf16[2,8,128,256]{3,2,1,0:T(8,128)(2,1)S(1)} %get-tuple-element.34), channel_id=1, source_target_pairs={{4,8},{8,4},{12,16},{16,12},{20,24},{24,20},{5,9},{9,5},{13,17},{1... | collective-permute-start | bytes 3145736 | tf_op jit(solution)/shard_map/ppermute | solution.py:438
  12.1 8.8 %collective-permute-start.2 = (bf16[8,128,256]{2,1,0:T(8,128)(2,1)S(1)}, bf16[8,128,256]{2,1,0:T(8,128)(2,1)S(1)}, u32[]{:S(2)}, u32[]{:S(2)}) collective-permute-start(bf16[8,128,256]{2,1,0:T(8,128)(2,1)S(1)} %get-tuple-element.41), channel_id=1, source_target_pairs={{0,4},{4,0},{8,12},{12,8},{16,20},{20,16},{24,28},{28,24},{1,5},{5... | collective-permute-start | bytes 1572872 | tf_op jit(solution)/shard_map/ppermute | solution.py:413
  12.2 7.6 %copy-start.1 = (bf16[27,32,128]{2,1,0:T(8,128)(2,1)S(1)}, bf16[27,32,128]{2,1,0:T(8,128)(2,1)}, u32[]{:S(2)}) copy-start(bf16[27,32,128]{2,1,0:T(8,128)(2,1)} %weights.3) | copy-start | bytes 663556
  12.2 7.6 %copy-start.3 = (f32[32]{0:T(128)S(1)}, f32[32]{0:T(128)}, u32[]{:S(2)}) copy-start(f32[32]{0:T(128)} %param.11) | copy-start | bytes 388
  18.7 2.2 %collective-permute-start.4 = (bf16[28,32,128]{2,1,0:T(8,128)(2,1)S(1)}, bf16[28,32,128]{2,1,0:T(8,128)(2,1)S(1)}, u32[]{:S(2)}, u32[]{:S(2)}) collective-permute-start(bf16[28,32,128]{2,1,0:T(8,128)(2,1)S(1)} %collective-permute-done.3.part_a), channel_id=1, source_target_pairs={{0,4},{4,0},{8,12},{12,8},{16,20},{20,16},{24,28},{28,24},{1,5},{5... | collective-permute-start | bytes 688136 | tf_op jit(solution)/shard_map/ppermute | solution.py:413
  29.5 6.8 %collective-permute-start.5 = (bf16[8,128,256]{2,1,0:T(8,128)(2,1)S(1)}, bf16[8,128,256]{2,1,0:T(8,128)(2,1)S(1)}, u32[]{:S(2)}, u32[]{:S(2)}) collective-permute-start(bf16[8,128,256]{2,1,0:T(8,128)(2,1)S(1)} %get-tuple-element.52.row_seven), channel_id=1, source_target_pairs={{0,4},{4,0},{8,12},{12,8},{16,20},{20,16},{24,28},{28,24},{1,5},{5... | collective-permute-start | bytes 1572872 | tf_op jit(solution)/shard_map/ppermute | solution.py:413

commit v10 on v9

--- a/solution.py
+++ b/solution.py
@@ -213,15 +213,20 @@
                         high_matrix[span, pl.ds((j * 3 + at) * channels, channels)] = tile
 
 
-def second_row(get, stored, halo, matrices, both, top):
-    quarter = both.shape[0] // 2
+def second_sums(get, stored, halo, matrices, taps=range(TAPS)):
     for x in range(0, COL_Y, 2):
         low, high = reach(x, 2, stored, halo)
         lhs = matrices[0]
         if high - low == 3:
             lhs = matrices[1] if x == 0 else matrices[2]
-        taken = jnp.concatenate([piece for j in range(TAPS) for piece in get(j, low, high)], axis=0)
-        partial = jnp.dot(lhs[...], taken, preferred_element_type=F32)
+        wide = lhs.shape[1] // TAPS
+        taken = jnp.concatenate([piece for j in taps for piece in get(j, low, high)], axis=0)
+        yield x, jnp.dot(lhs[:, taps[0] * wide : (taps[-1] + 1) * wide], taken, preferred_element_type=F32)
+
+
+def second_row(get, stored, halo, matrices, both, top):
+    quarter = both.shape[0] // 2
+    for x, partial in second_sums(get, stored, halo, matrices):
         done = finish(partial, both, top)
         yield x, done[:quarter], done[quarter:]
 
@@ -245,7 +250,7 @@
 
 def second_inner_kernel(
     halo, heights, own, near, low_near, high_near, bias_near, far, low_far, high_far, bias_far,
-    inner_a, inner_b, row_seven, matrix, low_matrix, high_matrix, both, out, sums_before, sums_zero,
+    inner_a, inner_b, row_seven, matrix, low_matrix, high_matrix, both, out, sums_before, sums_zero, sums_two,
 ):
     top = Place(heights).top()
     two = (matrix, low_matrix, high_matrix)
@@ -257,6 +262,9 @@
         for x, here, beside in second_row(lambda j, a, b: row(u - 1 + j, a, b), inner_a.shape[1], halo, two, both[:, 0:1], top):
             out[u - 2, x] = here
             out[u - 2, x + 1] = beside
+    for u, taps in ((0, (2,)), (1, (1, 2))):
+        for x, sums in second_sums(lambda j, a, b: row(u - 1 + j, a, b), inner_a.shape[1], halo, two, taps):
+            sums_two[u, x // 2] = sums
 
     matrices, _ = join(((near, low_near, high_near), bias_near), ((far, low_far, high_far), bias_far))
     width = own.shape[1]
@@ -267,7 +275,7 @@
 
 
 def last_kernel(
-    halo, heights, own, cross, near, low_near, high_near, bias_near, far, low_far, high_far, bias_far, sums_before, sums_zero,
+    halo, heights, own, cross, near, low_near, high_near, bias_near, far, low_far, high_far, bias_far, sums_before, sums_zero, sums_two,
     inner_a, inner_b, row_seven, mate, done_inner, matrix_two, low_two, high_two, both, out, edge, done_edge, result, sems,
 ):
     place = Place(heights)
@@ -278,19 +286,19 @@
             top = place.top(side_of(x), across=u < 0)
             edge[u + 1, x + halo] = finish(sums + sums_own[x + halo], biases[:, 0:1], top)
 
-    def row(u, a, b):
-        if 0 < u < 7:
-            return halves(inner_a, inner_b, u - 1, a, b)
-        return [edge[u + 1, x] if u < 1 else (row_seven if u == 7 else mate)[x] for x in range(a, b)]
-
-    two = (matrix_two, low_two, high_two)
-    for at, u in enumerate((0, 1, 7)):
-        for x, here, beside in second_row(
-            lambda j, a, b: row(u - 1 + j, a, b), inner_a.shape[1], halo, two, both[:, 0:1], place.top()
-        ):
-            done_edge[at, x] = here
-            done_edge[at, x + 1] = beside
-    quarter = out.shape[1]
+    two, stored, quarter = (matrix_two, low_two, high_two), inner_a.shape[1], out.shape[1]
+    for u, taps in ((0, (0, 1)), (1, (0,))):
+        for x, sums in second_sums(lambda j, a, b: [edge[u + j, x] for x in range(a, b)], stored, halo, two, taps):
+            done = finish(sums + sums_two[u, x // 2], both[:, 0:1], place.top())
+            done_edge[u, x] = done[:quarter]
+            done_edge[u, x + 1] = done[quarter:]
+
+    def row(j, a, b):
+        return halves(inner_a, inner_b, 5, a, b) if j == 0 else [(row_seven if j == 1 else mate)[x] for x in range(a, b)]
+
+    for x, here, beside in second_row(row, stored, halo, two, both[:, 0:1], place.top()):
+        done_edge[2, x] = here
+        done_edge[2, x + 1] = beside
     size = quarter * COL_Y
     at_row = lax.broadcasted_iota(jnp.int32, (size, size), 0)
     at_column = lax.broadcasted_iota(jnp.int32, (size, size), 1)
@@ -382,7 +390,8 @@
     channels, width = own.shape[2], COL_Y + 2 * halo
     quarter = matrices[-1].shape[0] // 2
     sums = (width, TAPS * channels, depth)
-    outputs, kinds = [(rows - 1, COL_Y, quarter, depth), sums, sums], [BF16, F32, F32]
+    outputs = [(rows - 1, COL_Y, quarter, depth), sums, sums, (2, COL_Y // 2, TAPS * 2 * quarter, depth)]
+    kinds = [BF16, F32, F32, F32]
     args = (heights, own, *near, *far, inner_a, inner_b, row_seven, *matrices)
     kernel = functools.partial(second_inner_kernel, halo)
     done, *sums = call(kernel, "second_inner", [SCALARS] + [WHOLE] * (len(args) - 1), outputs, [], SHORT, *args, kinds=kinds)

time: 42.2 us -> 41.6 us (0.986)
  waiting for transfers between devices: 1.3 us -> 0.72 us
    ppermute x1, waiting for transfers between devices: 0.99 us -> 0.42 us  [on_device(): cross = lax.ppermute(cross, 'space', across_pairs(peers))]
  transfers between devices with their start and end apart: 6 -> 6, of which waited for: 2 -> 2; matrix products, arithmetic and copies ran while one was open for 0% -> 0% of each run, Pallas kernels for 55% -> 57%
where the time goes in v10:
time: 41.6 us; the launch traced here: 41.5 us
  Pallas kernels  28.8 us (69%)
  starting transfers between devices  10.8 us (26%)
  local copies, waits for them, and re-layouts  0.9 us (2%)
  waiting for transfers between devices  0.72 us (2%)
    pallas_call x8, Pallas kernels, call(): pl.pallas_call(kernel, out_shape=[jax.ShapeDtypeStruct(*each) for each in...  28.8 us
    ppermute x1, starting transfers between devices, on_device(): lax.ppermute(sent_part, ('space', 'chan'), far_pairs(peers, chans))  4.12 us
    ppermute x1, starting transfers between devices, on_device(): cross = lax.ppermute(cross, 'space', across_pairs(peers))  2.94 us
    ppermute x1, starting transfers between devices, on_device(): lax.ppermute(own_part, 'chan', [(c, c ^ 1) for c in range(chans)])  2.19 us
    ppermute x3, starting transfers between devices, to_mate(): lax.ppermute(value, 'space', [(i, i ^ 1) for i in range(lax.axis_size('sp...  1.57 us
    unnamed x12, local copies, waits for them, and re-layouts  0.9 us
  transfers between devices with their start and end apart: 6, of which 2 were waited for; matrix products, arithmetic and copies ran while one was open for 0% of the time, Pallas kernels for 57%

profile of v10, /device:TPU:1, one launch (start us, length us, event | category | flops | bytes accessed | tf_op | source)
XLA Modules:
  0.0 41.5 jit_solution(12229322755631170549)
XLA Ops:
  0.0 0.1 order.1.after.swap
  0.1 0.6 %copy-done.5 = f32[32]{0:T(128)S(1)} copy-done((f32[32]{0:T(128)S(1)}, f32[32]{0:T(128)}, u32[]{:S(2)}) %copy-start.5) | copy-done | bytes 152
  0.7 0.3 copy-done.4
  1.0 0.1 pack.1.after.part_a
  1.1 2.2 %collective-permute-start.1 = (bf16[28,32,128]{2,1,0:T(8,128)(2,1)S(1)}, bf16[28,32,128]{2,1,0:T(8,128)(2,1)S(1)}, u32[]{:S(2)}, u32[]{:S(2)}) collective-permute-start(bf16[28,32,128]{2,1,0:T(8,128)(2,1)S(1)} %pack.1.after.part_a), channel_id=1, source_target_pairs={{0,1},{1,0},{2,3},{3,2},{4,5},{5,4},{6,7},{7,6},{8,9},{9,8},{10,11... | collective-permute-start | bytes 688136 | tf_op jit(solution)/shard_map/ppermute | solution.py:443
  3.2 1.8 %arrange.1 = (bf16[8,8,128,256]{3,2,1,0:T(8,128)(2,1)S(1)}, bf16[2,8,128,256]{3,2,1,0:T(8,128)(2,1)S(1)}, bf16[8,128,256]{2,1,0:T(8,128)(2,1)S(1)}) custom-call(s32[8]{0:T(128)S(1)} %copy-done.2, bf16[1,128,8,8,256]{4,3,2,1,0:T(8,128)(2,1)S(1)} %copy-done, bf16[256,256]{1,0:T(8,128)(2,1)S(1)} %order.1.after.swap, bf16[28,32,128]{2,1,0:T(8,128)(2,1)S(1)} %pack.1.after.part_a), custom_call_target="tpu_custom_call" | custom-call | flops 4096 | bytes 64 | tf_op jit(solution)/shard_map/arrange/pallas_call | solution.py:322
  5.1 4.1 %collective-permute-start.3 = (bf16[28,32,128]{2,1,0:T(8,128)(2,1)S(1)}, bf16[28,32,128]{2,1,0:T(8,128)(2,1)S(1)}, u32[]{:S(2)}, u32[]{:S(2)}) collective-permute-start(bf16[28,32,128]{2,1,0:T(8,128)(2,1)S(1)} %pack.1.after.part_a), channel_id=1, source_target_pairs={{0,2},{1,3},{2,0},{3,1},{4,7},{5,6},{6,5},{7,4},{8,10},{9,11},{10,... | collective-permute-start | bytes 688136 | tf_op jit(solution)/shard_map/ppermute | solution.py:446
  9.2 2.9 %collective-permute-start = (bf16[2,8,128,256]{3,2,1,0:T(8,128)(2,1)S(1)}, bf16[2,8,128,256]{3,2,1,0:T(8,128)(2,1)S(1)}, u32[]{:S(2)}, u32[]{:S(2)}) collective-permute-start(bf16[2,8,128,256]{3,2,1,0:T(8,128)(2,1)S(1)} %get-tuple-element.35), channel_id=1, source_target_pairs={{4,8},{8,4},{12,16},{16,12},{20,24},{24,20},{5,9},{9,5},{13,17},{1... | collective-permute-start | bytes 3145736 | tf_op jit(solution)/shard_map/ppermute | solution.py:447
  12.1 0.0 collective-permute-done.1.part_b
  12.1 0.1 collective-permute-start.2
  12.2 0.0 copy-start.1
  12.2 0.0 copy-start.3
  12.2 6.5 %first_near.1 = (bf16[6,8,64,256]{3,2,1,0:T(8,128)(2,1)S(1)}, bf16[192,1152]{1,0:T(8,128)(2,1)S(1)}, bf16[192,768]{1,0:T(8,128)(2,1)S(1)}, bf16[192,768]{1,0:T(8,128)(2,1)S(1)}, f32[64,128]{1,0:T(8,128)S(1)}) custom-call(s32[8]{0:T(128)S(1)} %copy-done.2, bf16[8,8,128,256]{3,2,1,0:T(8,128)(2,1)S(1)} %get-tuple-element.33.own, ...), custom_call_target="tpu_custom_call" | custom-call | flops 8589934592 | bytes 134217728 | tf_op jit(solution)/shard_map/first_near/pallas_call | solution.py:322
  18.7 0.0 collective-permute-done.3.part_a
  18.7 1.1 %collective-permute-start.4 = (bf16[28,32,128]{2,1,0:T(8,128)(2,1)S(1)}, bf16[28,32,128]{2,1,0:T(8,128)(2,1)S(1)}, u32[]{:S(2)}, u32[]{:S(2)}) collective-permute-start(bf16[28,32,128]{2,1,0:T(8,128)(2,1)S(1)} %collective-permute-done.3.part_a), channel_id=1, source_target_pairs={{0,4},{4,0},{8,12},{12,8},{16,20},{20,16},{24,28},{28,24},{1,5},{5... | collective-permute-start | bytes 688136 | tf_op jit(solution)/shard_map/ppermute | solution.py:422
  19.8 0.8 %fill.1 = (bf16[192,1536]{1,0:T(8,128)(2,1)S(1)}, bf16[192,1152]{1,0:T(8,128)(2,1)S(1)}, bf16[192,1152]{1,0:T(8,128)(2,1)S(1)}, f32[64,128]{1,0:T(8,128)S(1)}) custom-call(s32[8]{0:T(128)S(1)} %copy-done.2, bf16[27,32,128]{2,1,0:T(8,128)(2,1)S(1)} %copy-done.1, f32[1,32]{1,0:T(1,128)S(1)} %bitcast.2, bf16[6,8,64,256]{3,2,1,0:T(8,128)(2,1)S(1)} %get-tuple-element.46.after.inner_a), custom_call_target="tpu_custom_call" | custom-call | flops 4096 | bytes 64 | tf_op jit(solution)/shard_map/fill/pallas_call | solution.py:322
  20.6 0.3 collective-permute-done.4.part_b
  20.9 0.0 collective-permute-done.2.mate
  20.9 8.5 %first_far.1 = (bf16[6,8,64,256]{3,2,1,0:T(8,128)(2,1)S(1)}, bf16[8,128,256]{2,1,0:T(8,128)(2,1)S(1)}, bf16[192,1152]{1,0:T(8,128)(2,1)S(1)}, bf16[192,768]{1,0:...) custom-call(s32[8]{0:T(128)S(1)} %copy-done.2, ...), custom_call_target="tpu_custom_call" | custom-call | flops 4096 | bytes 64 | tf_op jit(solution)/shard_map/first_far/pallas_call | solution.py:322
  29.5 0.4 %collective-permute-start.5 = (bf16[8,128,256]{2,1,0:T(8,128)(2,1)S(1)}, bf16[8,128,256]{2,1,0:T(8,128)(2,1)S(1)}, u32[]{:S(2)}, u32[]{:S(2)}) collective-permute-start(bf16[8,128,256]{2,1,0:T(8,128)(2,1)S(1)} %get-tuple-element.53.row_seven), channel_id=1, source_target_pairs={{0,4},{4,0},{8,12},{12,8},{16,20},{20,16},{24,28},{28,24},{1,5},{5... | collective-permute-start | bytes 1572872 | tf_op jit(solution)/shard_map/ppermute | solution.py:422
  29.9 6.0 %second_inner.1 = (bf16[5,8,32,256]{3,2,1,0:T(8,128)(2,1)S(1)}, f32[8,384,256]{2,1,0:T(8,128)S(1)}, f32[8,384,256]{2,1,0:T(8,128)S(1)}, f32[2,4,192,256]{3,2,1,0:T(8,128)S(1)}) custom-call(s32[8]{0:T(128)S(1)} %copy-done.2, bf16[8,8,128,256]{3,2,1,0:T(8,128)(2,1)S(1)} %get-tuple-element.33.own, bf16[192,1152]{1,0:T(8,128)(2,1)S(1)} %get-tuple-element.38.near, ...), custom_call_target="tpu_custom_call" | custom-call | flops 4096 | bytes 64 | tf_op jit(solution)/shard_map/second_inner/pallas_call | solution.py:322
  35.9 0.4 %collective-permute-done.cross = bf16[2,8,128,256]{3,2,1,0:T(8,128)(2,1)S(1)} collective-permute-done((bf16[2,8,128,256]{3,2,1,0:T(8,128)(2,1)S(1)}, bf16[2,8,128,256]{3,2,1,0:T(8,128)(2,1)S(1)}, u32[]{:S(2)}, u32[]{:S(2)}) %collective-permute-start) | collective-permute-done | bytes 1048608 | tf_op jit(solution)/shard_map/ppermute | solution.py:447
  36.3 0.0 collective-permute-done.5.mate
  36.3 5.0 %last.1 = bf16[1,32,8,8,256]{4,3,2,1,0:T(8,128)(2,1)} custom-call(s32[8]{0:T(128)S(1)} %copy-done.2, bf16[8,8,128,256]{3,2,1,0:T(8,128)(2,1)S(1)} %get-tuple-element.33.own, bf16[2,8,128,256]{3,2,1,0:T(8,128)(2,1)S(1)} %collective-permute-done.cross, bf16[192,1152]{1,0:T(8,128)(2,1)S(1)} %get-tuple-element.38.near, ...), custom_call_target="tpu_custom_call" | custom-call | flops 4096 | bytes 64 | tf_op jit(solution)/shard_map/last/pallas_call | solution.py:322
  (8 shorter events, 0.0 us)
Async XLA Ops:
  0.0 0.7 %copy-start.5 = (f32[32]{0:T(128)S(1)}, f32[32]{0:T(128)}, u32[]{:S(2)}) copy-start(f32[32]{0:T(128)} %param.9) | copy-start | bytes 388
  0.0 0.9 %copy-start.4 = (bf16[27,32,128]{2,1,0:T(8,128)(2,1)S(1)}, bf16[27,32,128]{2,1,0:T(8,128)(2,1)}, u32[]{:S(2)}) copy-start(bf16[27,32,128]{2,1,0:T(8,128)(2,1)} %weights.2) | copy-start | bytes 663556
  1.0 2.3 %copy-start = (bf16[1,128,8,8,256]{4,3,2,1,0:T(8,128)(2,1)S(1)}, bf16[1,128,8,8,256]{4,3,2,1,0:T(8,128)(2,1)}, u32[]{:S(2)}) copy-start(bf16[1,128,8,8,256]{4,3,2,1,0:T(8,128)(2,1)} %features.1) | copy-start | bytes 12582916
  1.0 2.3 %copy-start.2 = (s32[8]{0:T(128)S(1)}, s32[8]{0:T(128)}, u32[]{:S(2)}) copy-start(s32[8]{0:T(128)} %heights.11) | copy-start | bytes 100
  1.1 11.1 %collective-permute-start.1 = (bf16[28,32,128]{2,1,0:T(8,128)(2,1)S(1)}, bf16[28,32,128]{2,1,0:T(8,128)(2,1)S(1)}, u32[]{:S(2)}, u32[]{:S(2)}) collective-permute-start(bf16[28,32,128]{2,1,0:T(8,128)(2,1)S(1)} %pack.1.after.part_a), channel_id=1, source_target_pairs={{0,1},{1,0},{2,3},{3,2},{4,5},{5,4},{6,7},{7,6},{8,9},{9,8},{10,11... | collective-permute-start | bytes 688136 | tf_op jit(solution)/shard_map/ppermute | solution.py:443
  5.1 13.7 %collective-permute-start.3 = (bf16[28,32,128]{2,1,0:T(8,128)(2,1)S(1)}, bf16[28,32,128]{2,1,0:T(8,128)(2,1)S(1)}, u32[]{:S(2)}, u32[]{:S(2)}) collective-permute-start(bf16[28,32,128]{2,1,0:T(8,128)(2,1)S(1)} %pack.1.after.part_a), channel_id=1, source_target_pairs={{0,2},{1,3},{2,0},{3,1},{4,7},{5,6},{6,5},{7,4},{8,10},{9,11},{10,... | collective-permute-start | bytes 688136 | tf_op jit(solution)/shard_map/ppermute | solution.py:446
  9.2 27.1 %collective-permute-start = (bf16[2,8,128,256]{3,2,1,0:T(8,128)(2,1)S(1)}, bf16[2,8,128,256]{3,2,1,0:T(8,128)(2,1)S(1)}, u32[]{:S(2)}, u32[]{:S(2)}) collective-permute-start(bf16[2,8,128,256]{3,2,1,0:T(8,128)(2,1)S(1)} %get-tuple-element.35), channel_id=1, source_target_pairs={{4,8},{8,4},{12,16},{16,12},{20,24},{24,20},{5,9},{9,5},{13,17},{1... | collective-permute-start | bytes 3145736 | tf_op jit(solution)/shard_map/ppermute | solution.py:447
  12.1 8.8 %collective-permute-start.2 = (bf16[8,128,256]{2,1,0:T(8,128)(2,1)S(1)}, bf16[8,128,256]{2,1,0:T(8,128)(2,1)S(1)}, u32[]{:S(2)}, u32[]{:S(2)}) collective-permute-start(bf16[8,128,256]{2,1,0:T(8,128)(2,1)S(1)} %get-tuple-element.42), channel_id=1, source_target_pairs={{0,4},{4,0},{8,12},{12,8},{16,20},{20,16},{24,28},{28,24},{1,5},{5... | collective-permute-start | bytes 1572872 | tf_op jit(solution)/shard_map/ppermute | solution.py:422
  12.2 7.6 %copy-start.1 = (bf16[27,32,128]{2,1,0:T(8,128)(2,1)S(1)}, bf16[27,32,128]{2,1,0:T(8,128)(2,1)}, u32[]{:S(2)}) copy-start(bf16[27,32,128]{2,1,0:T(8,128)(2,1)} %weights.3) | copy-start | bytes 663556
  12.2 7.6 %copy-start.3 = (f32[32]{0:T(128)S(1)}, f32[32]{0:T(128)}, u32[]{:S(2)}) copy-start(f32[32]{0:T(128)} %param.11) | copy-start | bytes 388
  18.7 2.2 %collective-permute-start.4 = (bf16[28,32,128]{2,1,0:T(8,128)(2,1)S(1)}, bf16[28,32,128]{2,1,0:T(8,128)(2,1)S(1)}, u32[]{:S(2)}, u32[]{:S(2)}) collective-permute-start(bf16[28,32,128]{2,1,0:T(8,128)(2,1)S(1)} %collective-permute-done.3.part_a), channel_id=1, source_target_pairs={{0,4},{4,0},{8,12},{12,8},{16,20},{20,16},{24,28},{28,24},{1,5},{5... | collective-permute-start | bytes 688136 | tf_op jit(solution)/shard_map/ppermute | solution.py:422
  29.5 6.8 %collective-permute-start.5 = (bf16[8,128,256]{2,1,0:T(8,128)(2,1)S(1)}, bf16[8,128,256]{2,1,0:T(8,128)(2,1)S(1)}, u32[]{:S(2)}, u32[]{:S(2)}) collective-permute-start(bf16[8,128,256]{2,1,0:T(8,128)(2,1)S(1)} %get-tuple-element.53.row_seven), channel_id=1, source_target_pairs={{0,4},{4,0},{8,12},{12,8},{16,20},{20,16},{24,28},{28,24},{1,5},{5... | collective-permute-start | bytes 1572872 | tf_op jit(solution)/shard_map/ppermute | solution.py:422

commit v11 on v10

--- a/solution.py
+++ b/solution.py
@@ -160,10 +160,7 @@
     inner_rows(own, out, halo, (matrix, low_matrix, high_matrix), bias, place.top)
 
 
-def first_far_kernel(
-    halo, heights, own, mate, part_a, part_b, near, low_near, high_near, bias_near, after,
-    out, out_last, matrix, low_matrix, high_matrix, bias,
-):
+def first_far_kernel(halo, heights, own, mate, part_a, part_b, near_seven, out, out_last, matrix, low_matrix, high_matrix, bias):
     place = Place(heights)
     fill_first([part_a, part_b], place.slots[2:], place.odd, matrix, low_matrix, high_matrix, bias)
     far = (matrix, low_matrix, high_matrix)
@@ -172,9 +169,10 @@
     def get(j, a, b):
         return span_of(mate, a, b) if j == 2 else span_of(own, COL_Y - 2 + j, a, b)
 
-    matrices, biases = join(((near, low_near, high_near), bias_near), (far, bias))
-    for x, done in first_row(get, own.shape[1], halo, matrices, biases, place.top):
-        out_last[x] = done
+    half = bias.shape[0]
+    out_last[:, :half] = near_seven[...]
+    for x, done in first_row(get, own.shape[1], halo, far, bias, place.top):
+        out_last[x, half:] = done
 
 
 class Joined:
@@ -243,9 +241,19 @@
     both[quarter:] = column
 
 
-def fill_kernel(heights, weights, bias, after, matrix, low_matrix, high_matrix, both):
-    fill_second(weights, Place(heights), matrix, low_matrix, high_matrix)
+def fill_kernel(
+    halo, heights, weights, bias, own, mate, near, low_near, high_near, bias_near, after,
+    matrix, low_matrix, high_matrix, both, near_seven,
+):
+    place = Place(heights)
+    fill_second(weights, place, matrix, low_matrix, high_matrix)
     fill_bias(bias, both)
+
+    def get(j, a, b):
+        return span_of(mate, a, b) if j == 2 else span_of(own, COL_Y - 2 + j, a, b)
+
+    for x, done in first_row(get, own.shape[1], halo, (near, low_near, high_near), bias_near, place.top):
+        near_seven[x] = done
 
 
 def second_inner_kernel(
@@ -276,7 +284,7 @@
 
 def last_kernel(
     halo, heights, own, cross, near, low_near, high_near, bias_near, far, low_far, high_far, bias_far, sums_before, sums_zero, sums_two,
-    inner_a, inner_b, row_seven, mate, done_inner, matrix_two, low_two, high_two, both, out, edge, done_edge, result, sems,
+    inner_a, inner_b, row_seven, mate, done_inner, matrix_two, low_two, high_two, both, out, edge, result, sems,
 ):
     place = Place(heights)
     width, depth = cross.shape[1], cross.shape[3]
@@ -287,30 +295,30 @@
             edge[u + 1, x + halo] = finish(sums + sums_own[x + halo], biases[:, 0:1], top)
 
     two, stored, quarter = (matrix_two, low_two, high_two), inner_a.shape[1], out.shape[1]
-    for u, taps in ((0, (0, 1)), (1, (0,))):
-        for x, sums in second_sums(lambda j, a, b: [edge[u + j, x] for x in range(a, b)], stored, halo, two, taps):
-            done = finish(sums + sums_two[u, x // 2], both[:, 0:1], place.top())
-            done_edge[u, x] = done[:quarter]
-            done_edge[u, x + 1] = done[quarter:]
-
-    def row(j, a, b):
-        return halves(inner_a, inner_b, 5, a, b) if j == 0 else [(row_seven if j == 1 else mate)[x] for x in range(a, b)]
-
-    for x, here, beside in second_row(row, stored, halo, two, both[:, 0:1], place.top()):
-        done_edge[2, x] = here
-        done_edge[2, x + 1] = beside
     size = quarter * COL_Y
     at_row = lax.broadcasted_iota(jnp.int32, (size, size), 0)
     at_column = lax.broadcasted_iota(jnp.int32, (size, size), 1)
     y = lax.rem(at_row, COL_Y)
     u = jnp.where(place.odd == 1, COL_Y - 1 - y, y)
     swap = (at_column == u * quarter + lax.div(at_row, COL_Y)).astype(F32).astype(BF16)
-    for x in range(COL_Y):
-        tiles = [done_edge[0, x], done_edge[1, x]] + [done_inner[v, x] for v in range(COL_Y - 3)] + [done_edge[2, x]]
-        tile = jnp.concatenate(tiles, axis=0)
-        moved = jnp.dot(swap, tile, preferred_element_type=F32).astype(BF16)
-        result[x] = moved.reshape(quarter, COL_Y, depth)
-        pltpu.make_async_copy(result.at[x], out.at[0, :, x], sems.at[x]).start()
+
+    def row(j, a, b):
+        return halves(inner_a, inner_b, 5, a, b) if j == 0 else [(row_seven if j == 1 else mate)[x] for x in range(a, b)]
+
+    rows_two = [
+        second_row(row, stored, halo, two, both[:, 0:1], place.top()),
+        second_sums(lambda j, a, b: [edge[j, x] for x in range(a, b)], stored, halo, two, (0, 1)),
+        second_sums(lambda j, a, b: [edge[1 + j, x] for x in range(a, b)], stored, halo, two, (0,)),
+    ]
+    for (x, *seven), (_, sums_a), (_, sums_b) in zip(*rows_two, strict=True):
+        first = finish(sums_a + sums_two[0, x // 2], both[:, 0:1], place.top())
+        second = finish(sums_b + sums_two[1, x // 2], both[:, 0:1], place.top())
+        for more in range(2):
+            span = slice(more * quarter, (more + 1) * quarter)
+            tiles = [first[span], second[span]] + [done_inner[v, x + more] for v in range(COL_Y - 3)] + [seven[more]]
+            moved = jnp.dot(swap, jnp.concatenate(tiles, axis=0), preferred_element_type=F32).astype(BF16)
+            result[x + more] = moved.reshape(quarter, COL_Y, depth)
+            pltpu.make_async_copy(result.at[x + more], out.at[0, :, x + more], sems.at[x + more]).start()
     for x in range(COL_Y):
         pltpu.make_async_copy(result.at[x], out.at[0, :, x], sems.at[x]).wait()
 
@@ -354,12 +362,16 @@
     return shapes, [BF16, BF16, BF16, F32]
 
 
-def fill(heights, weights, bias, after):
-    quarter, channels = weights.shape[1], weights.shape[2]
-    tall = TAPS * 2 * quarter
+def fill(halo, heights, weights, bias, own, mate, near, after):
+    quarter, channels, depth = weights.shape[1], weights.shape[2], own.shape[3]
+    tall, half = TAPS * 2 * quarter, near[-1].shape[0]
     outputs = [(tall, 12 * channels), (tall, 9 * channels), (tall, 9 * channels), (2 * quarter, 128)]
-    kinds = [BF16, BF16, BF16, F32]
-    return call(fill_kernel, "fill", [SCALARS, WHOLE, WHOLE, ANY], outputs, [], SHORT, heights, weights, bias[None], after, kinds=kinds)
+    outputs.append((COL_Y + 2 * halo, half, depth))
+    args = (heights, weights, bias[None], own, mate, *near, after)
+    inputs = [SCALARS] + [WHOLE] * (len(args) - 2) + [ANY]
+    kernel = functools.partial(fill_kernel, halo)
+    *matrices, seven = call(kernel, "fill", inputs, outputs, [], SHORT, *args, kinds=[BF16, BF16, BF16, F32, BF16])
+    return matrices, seven
 
 
 def first_near(halo, heights, own, part_a, part_b):
@@ -373,14 +385,14 @@
     return inner, matrices
 
 
-def first_far(halo, heights, own, mate, part_a, part_b, near, after):
+def first_far(halo, heights, own, mate, part_a, part_b, near_seven):
     _, _, channels, depth = own.shape
     half, width = 2 * part_a.shape[1], COL_Y + 2 * halo
     shapes, kinds = first_matrices(channels, half)
     inner, row_seven, *matrices = call(
-        functools.partial(first_far_kernel, halo), "first_far", [SCALARS] + [WHOLE] * 8 + [ANY],
+        functools.partial(first_far_kernel, halo), "first_far", [SCALARS] + [WHOLE] * 5,
         [(COL_Y - 2, width, half, depth), (width, channels, depth), *shapes], [], SHORT,
-        heights, own, mate, part_a, part_b, *near, after, kinds=[BF16, BF16, *kinds],
+        heights, own, mate, part_a, part_b, near_seven, kinds=[BF16, BF16, *kinds],
     )
     return inner, row_seven, matrices
 
@@ -401,7 +413,7 @@
 def last(halo, heights, own, cross, near, far, sums, hidden, done_inner, matrices):
     _, _, channels, depth = cross.shape
     quarter, width = matrices[-1].shape[0] // 2, COL_Y + 2 * halo
-    scratch = [pltpu.VMEM((2, width, channels, depth), BF16), pltpu.VMEM((3, COL_Y, quarter, depth), BF16)]
+    scratch = [pltpu.VMEM((2, width, channels, depth), BF16)]
     scratch += [pltpu.VMEM((COL_Y, quarter, COL_Y, depth), BF16), pltpu.SemaphoreType.DMA((COL_Y,))]
     outputs = [(1, quarter, COL_Y, COL_Y, depth)]
     args = (heights, own, cross, *near, *far, *sums, *hidden, done_inner, *matrices)
@@ -454,8 +466,8 @@
     inner_a, near = first_near(halo, column_heights, fields, own_part, near_part)
     far_part, inner_a = lax.optimization_barrier((far_part, inner_a))
     other_part = to_mate(far_part)
-    matrices = fill(column_heights, weight_two, bias_two, inner_a)
-    inner_b, row_seven, far = first_far(halo, column_heights, fields, mate, far_part, other_part, near, matrices[-1])
+    matrices, seven = fill(halo, column_heights, weight_two, bias_two, fields, mate, near, inner_a)
+    inner_b, row_seven, far = first_far(halo, column_heights, fields, mate, far_part, other_part, seven)
     mate = to_mate(row_seven)
     done_inner, sums = second_inner(halo, column_heights, fields, near, far, inner_a, inner_b, row_seven, matrices)
     hidden = (inner_a, inner_b, row_seven, mate)

time: 41.6 us -> 42.7 us (1.026)
  Pallas kernels: 28.8 us -> 30.1 us
  starting transfers between devices: 10.8 us -> 10.3 us
    pallas_call x8, Pallas kernels: 28.8 us -> 30.1 us  [call(): pl.pallas_call(kernel, out_shape=[jax.ShapeDtypeStruct(*each) for each in...]
    ppermute x3, starting transfers between devices: 1.57 us -> 1.06 us  [to_mate(): lax.ppermute(value, 'space', [(i, i ^ 1) for i in range(lax.axis_size('sp...]
    ppermute x1, waiting for transfers between devices: 0.42 us -> 0.87 us  [on_device(): cross = lax.ppermute(cross, 'space', across_pairs(peers))]
  transfers between devices with their start and end apart: 6 -> 6, of which waited for: 2 -> 1; matrix products, arithmetic and copies ran while one was open for 0% -> 0% of each run, Pallas kernels for 57% -> 56%
where the time goes in v11:
time: 42.7 us; the launch traced here: 42.5 us
  Pallas kernels  30.1 us (70%)
  starting transfers between devices  10.3 us (24%)
  local copies, waits for them, and re-layouts  0.9 us (2%)
  waiting for transfers between devices  0.88 us (2%)
    pallas_call x8, Pallas kernels, call(): pl.pallas_call(kernel, out_shape=[jax.ShapeDtypeStruct(*each) for each in...  30.1 us
    ppermute x1, starting transfers between devices, on_device(): lax.ppermute(sent_part, ('space', 'chan'), far_pairs(peers, chans))  4.11 us
    ppermute x1, starting transfers between devices, on_device(): cross = lax.ppermute(cross, 'space', across_pairs(peers))  2.94 us
    ppermute x1, starting transfers between devices, on_device(): lax.ppermute(own_part, 'chan', [(c, c ^ 1) for c in range(chans)])  2.19 us
    ppermute x3, starting transfers between devices, to_mate(): lax.ppermute(value, 'space', [(i, i ^ 1) for i in range(lax.axis_size('sp...  1.06 us
    unnamed x12, local copies, waits for them, and re-layouts  0.9 us
    ppermute x1, waiting for transfers between devices, on_device(): cross = lax.ppermute(cross, 'space', across_pairs(peers))  0.87 us
  transfers between devices with their start and end apart: 6, of which 1 were waited for; matrix products, arithmetic and copies ran while one was open for 0% of the time, Pallas kernels for 56%

profile of v11, /device:TPU:1, one launch (start us, length us, event | category | flops | bytes accessed | tf_op | source)
XLA Modules:
  0.0 42.5 jit_solution(3352177730430057860)
XLA Ops:
  0.0 0.1 order.1.after.swap
  0.1 0.6 %copy-done.5 = f32[32]{0:T(128)S(1)} copy-done((f32[32]{0:T(128)S(1)}, f32[32]{0:T(128)}, u32[]{:S(2)}) %copy-start.5) | copy-done | bytes 152
  0.7 0.3 copy-done.4
  1.0 0.1 pack.1.after.part_a
  1.1 2.2 %collective-permute-start.1 = (bf16[28,32,128]{2,1,0:T(8,128)(2,1)S(1)}, bf16[28,32,128]{2,1,0:T(8,128)(2,1)S(1)}, u32[]{:S(2)}, u32[]{:S(2)}) collective-permute-start(bf16[28,32,128]{2,1,0:T(8,128)(2,1)S(1)} %pack.1.after.part_a), channel_id=1, source_target_pairs={{0,1},{1,0},{2,3},{3,2},{4,5},{5,4},{6,7},{7,6},{8,9},{9,8},{10,11... | collective-permute-start | bytes 688136 | tf_op jit(solution)/shard_map/ppermute | solution.py:455
  3.2 1.9 %arrange.1 = (bf16[8,8,128,256]{3,2,1,0:T(8,128)(2,1)S(1)}, bf16[2,8,128,256]{3,2,1,0:T(8,128)(2,1)S(1)}, bf16[8,128,256]{2,1,0:T(8,128)(2,1)S(1)}) custom-call(s32[8]{0:T(128)S(1)} %copy-done.2, bf16[1,128,8,8,256]{4,3,2,1,0:T(8,128)(2,1)S(1)} %copy-done, bf16[256,256]{1,0:T(8,128)(2,1)S(1)} %order.1.after.swap, bf16[28,32,128]{2,1,0:T(8,128)(2,1)S(1)} %pack.1.after.part_a), custom_call_target="tpu_custom_call" | custom-call | flops 4096 | bytes 64 | tf_op jit(solution)/shard_map/arrange/pallas_call | solution.py:330
  5.1 4.1 %collective-permute-start.3 = (bf16[28,32,128]{2,1,0:T(8,128)(2,1)S(1)}, bf16[28,32,128]{2,1,0:T(8,128)(2,1)S(1)}, u32[]{:S(2)}, u32[]{:S(2)}) collective-permute-start(bf16[28,32,128]{2,1,0:T(8,128)(2,1)S(1)} %pack.1.after.part_a), channel_id=1, source_target_pairs={{0,2},{1,3},{2,0},{3,1},{4,7},{5,6},{6,5},{7,4},{8,10},{9,11},{10,... | collective-permute-start | bytes 688136 | tf_op jit(solution)/shard_map/ppermute | solution.py:458
  9.2 2.9 %collective-permute-start = (bf16[2,8,128,256]{3,2,1,0:T(8,128)(2,1)S(1)}, bf16[2,8,128,256]{3,2,1,0:T(8,128)(2,1)S(1)}, u32[]{:S(2)}, u32[]{:S(2)}) collective-permute-start(bf16[2,8,128,256]{3,2,1,0:T(8,128)(2,1)S(1)} %get-tuple-element.36), channel_id=1, source_target_pairs={{4,8},{8,4},{12,16},{16,12},{20,24},{24,20},{5,9},{9,5},{13,17},{1... | collective-permute-start | bytes 3145736 | tf_op jit(solution)/shard_map/ppermute | solution.py:459
  12.2 0.0 collective-permute-done.1.part_b
  12.2 0.1 collective-permute-start.2
  12.3 0.0 copy-start.1
  12.3 0.0 copy-start.3
  12.3 6.6 %first_near.1 = (bf16[6,8,64,256]{3,2,1,0:T(8,128)(2,1)S(1)}, bf16[192,1152]{1,0:T(8,128)(2,1)S(1)}, bf16[192,768]{1,0:T(8,128)(2,1)S(1)}, bf16[192,768]{1,0:T(8,128)(2,1)S(1)}, f32[64,128]{1,0:T(8,128)S(1)}) custom-call(s32[8]{0:T(128)S(1)} %copy-done.2, bf16[8,8,128,256]{3,2,1,0:T(8,128)(2,1)S(1)} %get-tuple-element.34.own, ...), custom_call_target="tpu_custom_call" | custom-call | flops 8589934592 | bytes 134217728 | tf_op jit(solution)/shard_map/first_near/pallas_call | solution.py:330
  18.9 0.0 collective-permute-done.3.part_a
  18.9 0.9 %collective-permute-start.4 = (bf16[28,32,128]{2,1,0:T(8,128)(2,1)S(1)}, bf16[28,32,128]{2,1,0:T(8,128)(2,1)S(1)}, u32[]{:S(2)}, u32[]{:S(2)}) collective-permute-start(bf16[28,32,128]{2,1,0:T(8,128)(2,1)S(1)} %collective-permute-done.3.part_a), channel_id=1, source_target_pairs={{0,4},{4,0},{8,12},{12,8},{16,20},{20,16},{24,28},{28,24},{1,5},{5... | collective-permute-start | bytes 688136 | tf_op jit(solution)/shard_map/ppermute | solution.py:434
  19.9 0.0 collective-permute-done.2.mate
  19.9 1.8 %fill.1 = (bf16[192,1536]{1,0:T(8,128)(2,1)S(1)}, bf16[192,1152]{1,0:T(8,128)(2,1)S(1)}, bf16[192,1152]{1,0:T(8,128)(2,1)S(1)}, f32[64,128]{1,0:T(8,128)S(1)}, bf16[8,64,256]{2,1,0:T(8,128)(2,1)S(1)}) custom-call(s32[8]{0:T(128)S(1)} %copy-done.2, bf16[27,32,128]{2,1,0:T(8,128)(2,1)S(1)} %copy-done.1, f32[1,32]{1,0:T(1,128)S(1)} %bitcast.2, ...), custom_call_target="tpu_custom_call" | custom-call | flops 4096 | bytes 64 | tf_op jit(solution)/shard_map/fill/pallas_call | solution.py:330
  21.7 0.0 collective-permute-done.4.part_b
  21.7 7.6 %first_far.1 = (bf16[6,8,64,256]{3,2,1,0:T(8,128)(2,1)S(1)}, bf16[8,128,256]{2,1,0:T(8,128)(2,1)S(1)}, bf16[192,1152]{1,0:T(8,128)(2,1)S(1)}, bf16[192,768]{1,0:...) custom-call(s32[8]{0:T(128)S(1)} %copy-done.2, ...), custom_call_target="tpu_custom_call" | custom-call | flops 4096 | bytes 64 | tf_op jit(solution)/shard_map/first_far/pallas_call | solution.py:330
  29.4 0.1 collective-permute-start.5
  29.4 6.0 %second_inner.1 = (bf16[5,8,32,256]{3,2,1,0:T(8,128)(2,1)S(1)}, f32[8,384,256]{2,1,0:T(8,128)S(1)}, f32[8,384,256]{2,1,0:T(8,128)S(1)}, f32[2,4,192,256]{3,2,1,0:T(8,128)S(1)}) custom-call(s32[8]{0:T(128)S(1)} %copy-done.2, bf16[8,8,128,256]{3,2,1,0:T(8,128)(2,1)S(1)} %get-tuple-element.34.own, bf16[192,1152]{1,0:T(8,128)(2,1)S(1)} %get-tuple-element.39.near, ...), custom_call_target="tpu_custom_call" | custom-call | flops 4096 | bytes 64 | tf_op jit(solution)/shard_map/second_inner/pallas_call | solution.py:330
  35.5 0.9 %collective-permute-done.cross = bf16[2,8,128,256]{3,2,1,0:T(8,128)(2,1)S(1)} collective-permute-done((bf16[2,8,128,256]{3,2,1,0:T(8,128)(2,1)S(1)}, bf16[2,8,128,256]{3,2,1,0:T(8,128)(2,1)S(1)}, u32[]{:S(2)}, u32[]{:S(2)}) %collective-permute-start) | collective-permute-done | bytes 1048608 | tf_op jit(solution)/shard_map/ppermute | solution.py:459
  36.4 0.0 collective-permute-done.5.mate
  36.4 6.0 %last.1 = bf16[1,32,8,8,256]{4,3,2,1,0:T(8,128)(2,1)} custom-call(s32[8]{0:T(128)S(1)} %copy-done.2, bf16[8,8,128,256]{3,2,1,0:T(8,128)(2,1)S(1)} %get-tuple-element.34.own, bf16[2,8,128,256]{3,2,1,0:T(8,128)(2,1)S(1)} %collective-permute-done.cross, bf16[192,1152]{1,0:T(8,128)(2,1)S(1)} %get-tuple-element.39.near, ...), custom_call_target="tpu_custom_call" | custom-call | flops 4096 | bytes 64 | tf_op jit(solution)/shard_map/last/pallas_call | solution.py:330
  (8 shorter events, 0.0 us)
Async XLA Ops:
  0.0 0.7 %copy-start.5 = (f32[32]{0:T(128)S(1)}, f32[32]{0:T(128)}, u32[]{:S(2)}) copy-start(f32[32]{0:T(128)} %param.9) | copy-start | bytes 388
  0.0 0.9 %copy-start.4 = (bf16[27,32,128]{2,1,0:T(8,128)(2,1)S(1)}, bf16[27,32,128]{2,1,0:T(8,128)(2,1)}, u32[]{:S(2)}) copy-start(bf16[27,32,128]{2,1,0:T(8,128)(2,1)} %weights.2) | copy-start | bytes 663556
  1.0 2.3 %copy-start = (bf16[1,128,8,8,256]{4,3,2,1,0:T(8,128)(2,1)S(1)}, bf16[1,128,8,8,256]{4,3,2,1,0:T(8,128)(2,1)}, u32[]{:S(2)}) copy-start(bf16[1,128,8,8,256]{4,3,2,1,0:T(8,128)(2,1)} %features.1) | copy-start | bytes 12582916
  1.0 2.3 %copy-start.2 = (s32[8]{0:T(128)S(1)}, s32[8]{0:T(128)}, u32[]{:S(2)}) copy-start(s32[8]{0:T(128)} %heights.11) | copy-start | bytes 100
  1.1 11.1 %collective-permute-start.1 = (bf16[28,32,128]{2,1,0:T(8,128)(2,1)S(1)}, bf16[28,32,128]{2,1,0:T(8,128)(2,1)S(1)}, u32[]{:S(2)}, u32[]{:S(2)}) collective-permute-start(bf16[28,32,128]{2,1,0:T(8,128)(2,1)S(1)} %pack.1.after.part_a), channel_id=1, source_target_pairs={{0,1},{1,0},{2,3},{3,2},{4,5},{5,4},{6,7},{7,6},{8,9},{9,8},{10,11... | collective-permute-start | bytes 688136 | tf_op jit(solution)/shard_map/ppermute | solution.py:455
  5.1 13.8 %collective-permute-start.3 = (bf16[28,32,128]{2,1,0:T(8,128)(2,1)S(1)}, bf16[28,32,128]{2,1,0:T(8,128)(2,1)S(1)}, u32[]{:S(2)}, u32[]{:S(2)}) collective-permute-start(bf16[28,32,128]{2,1,0:T(8,128)(2,1)S(1)} %pack.1.after.part_a), channel_id=1, source_target_pairs={{0,2},{1,3},{2,0},{3,1},{4,7},{5,6},{6,5},{7,4},{8,10},{9,11},{10,... | collective-permute-start | bytes 688136 | tf_op jit(solution)/shard_map/ppermute | solution.py:458
  9.2 27.1 %collective-permute-start = (bf16[2,8,128,256]{3,2,1,0:T(8,128)(2,1)S(1)}, bf16[2,8,128,256]{3,2,1,0:T(8,128)(2,1)S(1)}, u32[]{:S(2)}, u32[]{:S(2)}) collective-permute-start(bf16[2,8,128,256]{3,2,1,0:T(8,128)(2,1)S(1)} %get-tuple-element.36), channel_id=1, source_target_pairs={{4,8},{8,4},{12,16},{16,12},{20,24},{24,20},{5,9},{9,5},{13,17},{1... | collective-permute-start | bytes 3145736 | tf_op jit(solution)/shard_map/ppermute | solution.py:459
  12.2 7.7 %collective-permute-start.2 = (bf16[8,128,256]{2,1,0:T(8,128)(2,1)S(1)}, bf16[8,128,256]{2,1,0:T(8,128)(2,1)S(1)}, u32[]{:S(2)}, u32[]{:S(2)}) collective-permute-start(bf16[8,128,256]{2,1,0:T(8,128)(2,1)S(1)} %get-tuple-element.43), channel_id=1, source_target_pairs={{0,4},{4,0},{8,12},{12,8},{16,20},{20,16},{24,28},{28,24},{1,5},{5... | collective-permute-start | bytes 1572872 | tf_op jit(solution)/shard_map/ppermute | solution.py:434
  12.3 7.6 %copy-start.1 = (bf16[27,32,128]{2,1,0:T(8,128)(2,1)S(1)}, bf16[27,32,128]{2,1,0:T(8,128)(2,1)}, u32[]{:S(2)}) copy-start(bf16[27,32,128]{2,1,0:T(8,128)(2,1)} %weights.3) | copy-start | bytes 663556
  12.3 7.6 %copy-start.3 = (f32[32]{0:T(128)S(1)}, f32[32]{0:T(128)}, u32[]{:S(2)}) copy-start(f32[32]{0:T(128)} %param.11) | copy-start | bytes 388
  18.9 2.8 %collective-permute-start.4 = (bf16[28,32,128]{2,1,0:T(8,128)(2,1)S(1)}, bf16[28,32,128]{2,1,0:T(8,128)(2,1)S(1)}, u32[]{:S(2)}, u32[]{:S(2)}) collective-permute-start(bf16[28,32,128]{2,1,0:T(8,128)(2,1)S(1)} %collective-permute-done.3.part_a), channel_id=1, source_target_pairs={{0,4},{4,0},{8,12},{12,8},{16,20},{20,16},{24,28},{28,24},{1,5},{5... | collective-permute-start | bytes 688136 | tf_op jit(solution)/shard_map/ppermute | solution.py:434
  29.4 7.0 %collective-permute-start.5 = (bf16[8,128,256]{2,1,0:T(8,128)(2,1)S(1)}, bf16[8,128,256]{2,1,0:T(8,128)(2,1)S(1)}, u32[]{:S(2)}, u32[]{:S(2)}) collective-permute-start(bf16[8,128,256]{2,1,0:T(8,128)(2,1)S(1)} %get-tuple-element.54.row_seven), channel_id=1, source_target_pairs={{0,4},{4,0},{8,12},{12,8},{16,20},{20,16},{24,28},{28,24},{1,5},{5... | collective-permute-start | bytes 1572872 | tf_op jit(solution)/shard_map/ppermute | solution.py:434

commit v12 on v11

--- a/solution.py
+++ b/solution.py
@@ -284,7 +284,7 @@
 
 def last_kernel(
     halo, heights, own, cross, near, low_near, high_near, bias_near, far, low_far, high_far, bias_far, sums_before, sums_zero, sums_two,
-    inner_a, inner_b, row_seven, mate, done_inner, matrix_two, low_two, high_two, both, out, edge, result, sems,
+    inner_a, inner_b, row_seven, mate, done_inner, matrix_two, low_two, high_two, both, out, edge, done_edge, result, sems,
 ):
     place = Place(heights)
     width, depth = cross.shape[1], cross.shape[3]
@@ -295,30 +295,30 @@
             edge[u + 1, x + halo] = finish(sums + sums_own[x + halo], biases[:, 0:1], top)
 
     two, stored, quarter = (matrix_two, low_two, high_two), inner_a.shape[1], out.shape[1]
+    for u, taps in ((0, (0, 1)), (1, (0,))):
+        for x, sums in second_sums(lambda j, a, b: [edge[u + j, x] for x in range(a, b)], stored, halo, two, taps):
+            done = finish(sums + sums_two[u, x // 2], both[:, 0:1], place.top())
+            done_edge[u, x] = done[:quarter]
+            done_edge[u, x + 1] = done[quarter:]
+
+    def row(j, a, b):
+        return halves(inner_a, inner_b, 5, a, b) if j == 0 else [(row_seven if j == 1 else mate)[x] for x in range(a, b)]
+
+    for x, here, beside in second_row(row, stored, halo, two, both[:, 0:1], place.top()):
+        done_edge[2, x] = here
+        done_edge[2, x + 1] = beside
     size = quarter * COL_Y
     at_row = lax.broadcasted_iota(jnp.int32, (size, size), 0)
     at_column = lax.broadcasted_iota(jnp.int32, (size, size), 1)
     y = lax.rem(at_row, COL_Y)
     u = jnp.where(place.odd == 1, COL_Y - 1 - y, y)
     swap = (at_column == u * quarter + lax.div(at_row, COL_Y)).astype(F32).astype(BF16)
-
-    def row(j, a, b):
-        return halves(inner_a, inner_b, 5, a, b) if j == 0 else [(row_seven if j == 1 else mate)[x] for x in range(a, b)]
-
-    rows_two = [
-        second_row(row, stored, halo, two, both[:, 0:1], place.top()),
-        second_sums(lambda j, a, b: [edge[j, x] for x in range(a, b)], stored, halo, two, (0, 1)),
-        second_sums(lambda j, a, b: [edge[1 + j, x] for x in range(a, b)], stored, halo, two, (0,)),
-    ]
-    for (x, *seven), (_, sums_a), (_, sums_b) in zip(*rows_two, strict=True):
-        first = finish(sums_a + sums_two[0, x // 2], both[:, 0:1], place.top())
-        second = finish(sums_b + sums_two[1, x // 2], both[:, 0:1], place.top())
-        for more in range(2):
-            span = slice(more * quarter, (more + 1) * quarter)
-            tiles = [first[span], second[span]] + [done_inner[v, x + more] for v in range(COL_Y - 3)] + [seven[more]]
-            moved = jnp.dot(swap, jnp.concatenate(tiles, axis=0), preferred_element_type=F32).astype(BF16)
-            result[x + more] = moved.reshape(quarter, COL_Y, depth)
-            pltpu.make_async_copy(result.at[x + more], out.at[0, :, x + more], sems.at[x + more]).start()
+    for x in range(COL_Y):
+        tiles = [done_edge[0, x], done_edge[1, x]] + [done_inner[v, x] for v in range(COL_Y - 3)] + [done_edge[2, x]]
+        tile = jnp.concatenate(tiles, axis=0)
+        moved = jnp.dot(swap, tile, preferred_element_type=F32).astype(BF16)
+        result[x] = moved.reshape(quarter, COL_Y, depth)
+        pltpu.make_async_copy(result.at[x], out.at[0, :, x], sems.at[x]).start()
     for x in range(COL_Y):
         pltpu.make_async_copy(result.at[x], out.at[0, :, x], sems.at[x]).wait()
 
@@ -413,7 +413,7 @@
 def last(halo, heights, own, cross, near, far, sums, hidden, done_inner, matrices):
     _, _, channels, depth = cross.shape
     quarter, width = matrices[-1].shape[0] // 2, COL_Y + 2 * halo
-    scratch = [pltpu.VMEM((2, width, channels, depth), BF16)]
+    scratch = [pltpu.VMEM((2, width, channels, depth), BF16), pltpu.VMEM((3, COL_Y, quarter, depth), BF16)]
     scratch += [pltpu.VMEM((COL_Y, quarter, COL_Y, depth), BF16), pltpu.SemaphoreType.DMA((COL_Y,))]
     outputs = [(1, quarter, COL_Y, COL_Y, depth)]
     args = (heights, own, cross, *near, *far, *sums, *hidden, done_inner, *matrices)

time: 42.7 us -> 41.8 us (0.979)
  Pallas kernels: 30.1 us -> 29.2 us
    pallas_call x8, Pallas kernels: 30.1 us -> 29.2 us  [call(): pl.pallas_call(kernel, out_shape=[jax.ShapeDtypeStruct(*each) for each in...]
  transfers between devices with their start and end apart: 6 -> 6, of which waited for: 1 -> 1; matrix products, arithmetic and copies ran while one was open for 0% -> 0% of each run, Pallas kernels for 56% -> 58%
where the time goes in v12:
time: 41.8 us; the launch traced here: 41.6 us
  Pallas kernels  29.2 us (70%)
  starting transfers between devices  10.3 us (25%)
  local copies, waits for them, and re-layouts  0.9 us (2%)
  waiting for transfers between devices  0.88 us (2%)
    pallas_call x8, Pallas kernels, call(): pl.pallas_call(kernel, out_shape=[jax.ShapeDtypeStruct(*each) for each in...  29.2 us
    ppermute x1, starting transfers between devices, on_device(): lax.ppermute(sent_part, ('space', 'chan'), far_pairs(peers, chans))  4.11 us
    ppermute x1, starting transfers between devices, on_device(): cross = lax.ppermute(cross, 'space', across_pairs(peers))  2.94 us
    ppermute x1, starting transfers between devices, on_device(): lax.ppermute(own_part, 'chan', [(c, c ^ 1) for c in range(chans)])  2.19 us
    ppermute x3, starting transfers between devices, to_mate(): lax.ppermute(value, 'space', [(i, i ^ 1) for i in range(lax.axis_size('sp...  1.06 us
    unnamed x12, local copies, waits for them, and re-layouts  0.9 us
    ppermute x1, waiting for transfers between devices, on_device(): cross = lax.ppermute(cross, 'space', across_pairs(peers))  0.87 us
  transfers between devices with their start and end apart: 6, of which 1 were waited for; matrix products, arithmetic and copies ran while one was open for 0% of the time, Pallas kernels for 58%

profile of v12, /device:TPU:1, one launch (start us, length us, event | category | flops | bytes accessed | tf_op | source)
XLA Modules:
  0.0 41.6 jit_solution(11021273739293226508)
XLA Ops:
  0.0 0.1 order.1.after.swap
  0.1 0.6 %copy-done.5 = f32[32]{0:T(128)S(1)} copy-done((f32[32]{0:T(128)S(1)}, f32[32]{0:T(128)}, u32[]{:S(2)}) %copy-start.5) | copy-done | bytes 152
  0.7 0.3 copy-done.4
  1.0 0.1 pack.1.after.part_a
  1.1 2.2 %collective-permute-start.1 = (bf16[28,32,128]{2,1,0:T(8,128)(2,1)S(1)}, bf16[28,32,128]{2,1,0:T(8,128)(2,1)S(1)}, u32[]{:S(2)}, u32[]{:S(2)}) collective-permute-start(bf16[28,32,128]{2,1,0:T(8,128)(2,1)S(1)} %pack.1.after.part_a), channel_id=1, source_target_pairs={{0,1},{1,0},{2,3},{3,2},{4,5},{5,4},{6,7},{7,6},{8,9},{9,8},{10,11... | collective-permute-start | bytes 688136 | tf_op jit(solution)/shard_map/ppermute | solution.py:455
  3.2 1.9 %arrange.1 = (bf16[8,8,128,256]{3,2,1,0:T(8,128)(2,1)S(1)}, bf16[2,8,128,256]{3,2,1,0:T(8,128)(2,1)S(1)}, bf16[8,128,256]{2,1,0:T(8,128)(2,1)S(1)}) custom-call(s32[8]{0:T(128)S(1)} %copy-done.2, bf16[1,128,8,8,256]{4,3,2,1,0:T(8,128)(2,1)S(1)} %copy-done, bf16[256,256]{1,0:T(8,128)(2,1)S(1)} %order.1.after.swap, bf16[28,32,128]{2,1,0:T(8,128)(2,1)S(1)} %pack.1.after.part_a), custom_call_target="tpu_custom_call" | custom-call | flops 4096 | bytes 64 | tf_op jit(solution)/shard_map/arrange/pallas_call | solution.py:330
  5.1 4.1 %collective-permute-start.3 = (bf16[28,32,128]{2,1,0:T(8,128)(2,1)S(1)}, bf16[28,32,128]{2,1,0:T(8,128)(2,1)S(1)}, u32[]{:S(2)}, u32[]{:S(2)}) collective-permute-start(bf16[28,32,128]{2,1,0:T(8,128)(2,1)S(1)} %pack.1.after.part_a), channel_id=1, source_target_pairs={{0,2},{1,3},{2,0},{3,1},{4,7},{5,6},{6,5},{7,4},{8,10},{9,11},{10,... | collective-permute-start | bytes 688136 | tf_op jit(solution)/shard_map/ppermute | solution.py:458
  9.2 2.9 %collective-permute-start = (bf16[2,8,128,256]{3,2,1,0:T(8,128)(2,1)S(1)}, bf16[2,8,128,256]{3,2,1,0:T(8,128)(2,1)S(1)}, u32[]{:S(2)}, u32[]{:S(2)}) collective-permute-start(bf16[2,8,128,256]{3,2,1,0:T(8,128)(2,1)S(1)} %get-tuple-element.36), channel_id=1, source_target_pairs={{4,8},{8,4},{12,16},{16,12},{20,24},{24,20},{5,9},{9,5},{13,17},{1... | collective-permute-start | bytes 3145736 | tf_op jit(solution)/shard_map/ppermute | solution.py:459
  12.2 0.0 collective-permute-done.1.part_b
  12.2 0.1 collective-permute-start.2
  12.3 0.0 copy-start.1
  12.3 0.0 copy-start.3
  12.3 6.6 %first_near.1 = (bf16[6,8,64,256]{3,2,1,0:T(8,128)(2,1)S(1)}, bf16[192,1152]{1,0:T(8,128)(2,1)S(1)}, bf16[192,768]{1,0:T(8,128)(2,1)S(1)}, bf16[192,768]{1,0:T(8,128)(2,1)S(1)}, f32[64,128]{1,0:T(8,128)S(1)}) custom-call(s32[8]{0:T(128)S(1)} %copy-done.2, bf16[8,8,128,256]{3,2,1,0:T(8,128)(2,1)S(1)} %get-tuple-element.34.own, ...), custom_call_target="tpu_custom_call" | custom-call | flops 8589934592 | bytes 134217728 | tf_op jit(solution)/shard_map/first_near/pallas_call | solution.py:330
  18.9 0.0 collective-permute-done.3.part_a
  18.9 0.9 %collective-permute-start.4 = (bf16[28,32,128]{2,1,0:T(8,128)(2,1)S(1)}, bf16[28,32,128]{2,1,0:T(8,128)(2,1)S(1)}, u32[]{:S(2)}, u32[]{:S(2)}) collective-permute-start(bf16[28,32,128]{2,1,0:T(8,128)(2,1)S(1)} %collective-permute-done.3.part_a), channel_id=1, source_target_pairs={{0,4},{4,0},{8,12},{12,8},{16,20},{20,16},{24,28},{28,24},{1,5},{5... | collective-permute-start | bytes 688136 | tf_op jit(solution)/shard_map/ppermute | solution.py:434
  19.9 0.0 collective-permute-done.2.mate
  19.9 1.8 %fill.1 = (bf16[192,1536]{1,0:T(8,128)(2,1)S(1)}, bf16[192,1152]{1,0:T(8,128)(2,1)S(1)}, bf16[192,1152]{1,0:T(8,128)(2,1)S(1)}, f32[64,128]{1,0:T(8,128)S(1)}, bf16[8,64,256]{2,1,0:T(8,128)(2,1)S(1)}) custom-call(s32[8]{0:T(128)S(1)} %copy-done.2, bf16[27,32,128]{2,1,0:T(8,128)(2,1)S(1)} %copy-done.1, f32[1,32]{1,0:T(1,128)S(1)} %bitcast.2, ...), custom_call_target="tpu_custom_call" | custom-call | flops 4096 | bytes 64 | tf_op jit(solution)/shard_map/fill/pallas_call | solution.py:330
  21.7 0.0 collective-permute-done.4.part_b
  21.7 7.6 %first_far.1 = (bf16[6,8,64,256]{3,2,1,0:T(8,128)(2,1)S(1)}, bf16[8,128,256]{2,1,0:T(8,128)(2,1)S(1)}, bf16[192,1152]{1,0:T(8,128)(2,1)S(1)}, bf16[192,768]{1,0:...) custom-call(s32[8]{0:T(128)S(1)} %copy-done.2, ...), custom_call_target="tpu_custom_call" | custom-call | flops 4096 | bytes 64 | tf_op jit(solution)/shard_map/first_far/pallas_call | solution.py:330
  29.4 0.1 collective-permute-start.5
  29.4 6.0 %second_inner.1 = (bf16[5,8,32,256]{3,2,1,0:T(8,128)(2,1)S(1)}, f32[8,384,256]{2,1,0:T(8,128)S(1)}, f32[8,384,256]{2,1,0:T(8,128)S(1)}, f32[2,4,192,256]{3,2,1,0:T(8,128)S(1)}) custom-call(s32[8]{0:T(128)S(1)} %copy-done.2, bf16[8,8,128,256]{3,2,1,0:T(8,128)(2,1)S(1)} %get-tuple-element.34.own, bf16[192,1152]{1,0:T(8,128)(2,1)S(1)} %get-tuple-element.39.near, ...), custom_call_target="tpu_custom_call" | custom-call | flops 4096 | bytes 64 | tf_op jit(solution)/shard_map/second_inner/pallas_call | solution.py:330
  35.5 0.9 %collective-permute-done.cross = bf16[2,8,128,256]{3,2,1,0:T(8,128)(2,1)S(1)} collective-permute-done((bf16[2,8,128,256]{3,2,1,0:T(8,128)(2,1)S(1)}, bf16[2,8,128,256]{3,2,1,0:T(8,128)(2,1)S(1)}, u32[]{:S(2)}, u32[]{:S(2)}) %collective-permute-start) | collective-permute-done | bytes 1048608 | tf_op jit(solution)/shard_map/ppermute | solution.py:459
  36.4 0.0 collective-permute-done.5.mate
  36.4 5.1 %last.1 = bf16[1,32,8,8,256]{4,3,2,1,0:T(8,128)(2,1)} custom-call(s32[8]{0:T(128)S(1)} %copy-done.2, bf16[8,8,128,256]{3,2,1,0:T(8,128)(2,1)S(1)} %get-tuple-element.34.own, bf16[2,8,128,256]{3,2,1,0:T(8,128)(2,1)S(1)} %collective-permute-done.cross, bf16[192,1152]{1,0:T(8,128)(2,1)S(1)} %get-tuple-element.39.near, ...), custom_call_target="tpu_custom_call" | custom-call | flops 4096 | bytes 64 | tf_op jit(solution)/shard_map/last/pallas_call | solution.py:330
  (8 shorter events, 0.0 us)
Async XLA Ops:
  0.0 0.7 %copy-start.5 = (f32[32]{0:T(128)S(1)}, f32[32]{0:T(128)}, u32[]{:S(2)}) copy-start(f32[32]{0:T(128)} %param.9) | copy-start | bytes 388
  0.0 0.9 %copy-start.4 = (bf16[27,32,128]{2,1,0:T(8,128)(2,1)S(1)}, bf16[27,32,128]{2,1,0:T(8,128)(2,1)}, u32[]{:S(2)}) copy-start(bf16[27,32,128]{2,1,0:T(8,128)(2,1)} %weights.2) | copy-start | bytes 663556
  1.0 2.3 %copy-start = (bf16[1,128,8,8,256]{4,3,2,1,0:T(8,128)(2,1)S(1)}, bf16[1,128,8,8,256]{4,3,2,1,0:T(8,128)(2,1)}, u32[]{:S(2)}) copy-start(bf16[1,128,8,8,256]{4,3,2,1,0:T(8,128)(2,1)} %features.1) | copy-start | bytes 12582916
  1.0 2.3 %copy-start.2 = (s32[8]{0:T(128)S(1)}, s32[8]{0:T(128)}, u32[]{:S(2)}) copy-start(s32[8]{0:T(128)} %heights.11) | copy-start | bytes 100
  1.1 11.1 %collective-permute-start.1 = (bf16[28,32,128]{2,1,0:T(8,128)(2,1)S(1)}, bf16[28,32,128]{2,1,0:T(8,128)(2,1)S(1)}, u32[]{:S(2)}, u32[]{:S(2)}) collective-permute-start(bf16[28,32,128]{2,1,0:T(8,128)(2,1)S(1)} %pack.1.after.part_a), channel_id=1, source_target_pairs={{0,1},{1,0},{2,3},{3,2},{4,5},{5,4},{6,7},{7,6},{8,9},{9,8},{10,11... | collective-permute-start | bytes 688136 | tf_op jit(solution)/shard_map/ppermute | solution.py:455
  5.1 13.8 %collective-permute-start.3 = (bf16[28,32,128]{2,1,0:T(8,128)(2,1)S(1)}, bf16[28,32,128]{2,1,0:T(8,128)(2,1)S(1)}, u32[]{:S(2)}, u32[]{:S(2)}) collective-permute-start(bf16[28,32,128]{2,1,0:T(8,128)(2,1)S(1)} %pack.1.after.part_a), channel_id=1, source_target_pairs={{0,2},{1,3},{2,0},{3,1},{4,7},{5,6},{6,5},{7,4},{8,10},{9,11},{10,... | collective-permute-start | bytes 688136 | tf_op jit(solution)/shard_map/ppermute | solution.py:458
  9.2 27.1 %collective-permute-start = (bf16[2,8,128,256]{3,2,1,0:T(8,128)(2,1)S(1)}, bf16[2,8,128,256]{3,2,1,0:T(8,128)(2,1)S(1)}, u32[]{:S(2)}, u32[]{:S(2)}) collective-permute-start(bf16[2,8,128,256]{3,2,1,0:T(8,128)(2,1)S(1)} %get-tuple-element.36), channel_id=1, source_target_pairs={{4,8},{8,4},{12,16},{16,12},{20,24},{24,20},{5,9},{9,5},{13,17},{1... | collective-permute-start | bytes 3145736 | tf_op jit(solution)/shard_map/ppermute | solution.py:459
  12.2 7.7 %collective-permute-start.2 = (bf16[8,128,256]{2,1,0:T(8,128)(2,1)S(1)}, bf16[8,128,256]{2,1,0:T(8,128)(2,1)S(1)}, u32[]{:S(2)}, u32[]{:S(2)}) collective-permute-start(bf16[8,128,256]{2,1,0:T(8,128)(2,1)S(1)} %get-tuple-element.43), channel_id=1, source_target_pairs={{0,4},{4,0},{8,12},{12,8},{16,20},{20,16},{24,28},{28,24},{1,5},{5... | collective-permute-start | bytes 1572872 | tf_op jit(solution)/shard_map/ppermute | solution.py:434
  12.3 7.6 %copy-start.1 = (bf16[27,32,128]{2,1,0:T(8,128)(2,1)S(1)}, bf16[27,32,128]{2,1,0:T(8,128)(2,1)}, u32[]{:S(2)}) copy-start(bf16[27,32,128]{2,1,0:T(8,128)(2,1)} %weights.3) | copy-start | bytes 663556
  12.3 7.6 %copy-start.3 = (f32[32]{0:T(128)S(1)}, f32[32]{0:T(128)}, u32[]{:S(2)}) copy-start(f32[32]{0:T(128)} %param.11) | copy-start | bytes 388
  18.9 2.8 %collective-permute-start.4 = (bf16[28,32,128]{2,1,0:T(8,128)(2,1)S(1)}, bf16[28,32,128]{2,1,0:T(8,128)(2,1)S(1)}, u32[]{:S(2)}, u32[]{:S(2)}) collective-permute-start(bf16[28,32,128]{2,1,0:T(8,128)(2,1)S(1)} %collective-permute-done.3.part_a), channel_id=1, source_target_pairs={{0,4},{4,0},{8,12},{12,8},{16,20},{20,16},{24,28},{28,24},{1,5},{5... | collective-permute-start | bytes 688136 | tf_op jit(solution)/shard_map/ppermute | solution.py:434
  29.4 7.0 %collective-permute-start.5 = (bf16[8,128,256]{2,1,0:T(8,128)(2,1)S(1)}, bf16[8,128,256]{2,1,0:T(8,128)(2,1)S(1)}, u32[]{:S(2)}, u32[]{:S(2)}) collective-permute-start(bf16[8,128,256]{2,1,0:T(8,128)(2,1)S(1)} %get-tuple-element.54.row_seven), channel_id=1, source_target_pairs={{0,4},{4,0},{8,12},{12,8},{16,20},{20,16},{24,28},{28,24},{1,5},{5... | collective-permute-start | bytes 1572872 | tf_op jit(solution)/shard_map/ppermute | solution.py:434
